TPU v7x, 32 devices: a whole 2x2x4 slice. The times are simulated.
32 devices in a mesh: bx: 4 (over y, x), by: 8 (over z, core).
Axes of the slice: x: 2, y: 2, z: 4, core: 2. Of those that a mesh axis runs over, the one named last changes fastest.
Arguments:
- views: float32 [3, 2, 64, 256, 128], P(None, None, 'bx', 'by'), may hold values from 0.2 to 3
- estimate: float32 [2, 64, 256, 128], P(None, 'bx', 'by'), may hold values from 0.5 to 2
- profiles: float32 [4, 8, 3, 256, 128], P('bx', 'by'), may hold values from 0.3 to 1
- kernels: float32 [3, 3, 31], replicated, may hold values from 0.004 to 0.06
- owners: int32 [3, 4], replicated, may hold values from 0 to 7
Outputs:
- deconvolved: float32 [2, 64, 256, 128], P(None, 'bx', 'by')
Inputs may be any that keep to these rules, and one draw needn't show every extreme that they name: `owners`: an index along the brick columns.
All inputs are finite; a program needn't handle non-finite values.
Results may differ from a plain program's by a relative error of at most 0.0001.
Values sent between devices are 32-bit elements; how exact they have to be, the bound alone decides.
No kernel may reach another device: no remote copies, remote signals or barrier semaphores. Data moves between devices by JAX's collectives and lax.ppermute only.
A program may use at most 128 MiB of HBM per device.

v0:
```python
import functools

import jax
import jax.numpy as jnp
from jax import lax
from jax.experimental import pallas as pl
from jax.experimental.pallas import tpu as pltpu
from jax.sharding import PartitionSpec as P

F32 = jnp.float32
BF16 = jnp.bfloat16
PAD = 16


def shift(value, axis, step):
    count = lax.axis_size(axis)
    pairs = [(i, i + step) for i in range(count) if 0 <= i + step < count]
    return lax.ppermute(value, axis, pairs)


def halves(value):
    high = value.astype(BF16)
    return high, (value - high.astype(F32)).astype(BF16)


def matrices(taps, y_blur, y_back, z_blur, z_back):
    views, _, count = taps.shape
    half = count // 2
    width = y_blur.shape[0] // views
    slab = y_blur.shape[1] // 3
    depth = z_blur.shape[1] // 2

    def pick(view, axis, offset):
        total = jnp.zeros(offset.shape, F32)
        for step in range(count):
            total = jnp.where(offset == step, taps[view, axis, step], total)
        return halves(total)

    def position(shape, dim):
        place = lax.broadcasted_iota(jnp.int32, shape, dim)
        low = jnp.where(place < width + PAD, place - width - PAD, place - PAD)
        return jnp.where(place < width, place, low)

    def index(shape, dim):
        return lax.broadcasted_iota(jnp.int32, shape, dim)

    highs, lows = [], []
    for view in range(views):
        shape = (width, slab)
        high, low = pick(view, 1, position(shape, 1) - index(shape, 0) + half)
        y_blur[view * width : (view + 1) * width] = jnp.concatenate([high, high, low], axis=1)
        shape = (slab, width)
        high, low = pick(view, 1, position(shape, 0) - index(shape, 1) + half)
        highs.append(high)
        lows.append(low)
        shape = (depth, depth)
        offset = index(shape, 0) - index(shape, 1) + half
        for ref, at in ((z_blur, offset), (z_back, 2 * half - offset)):
            high, low = pick(view, 2, at)
            ref[view, :depth] = jnp.concatenate([high, low], axis=1)
            ref[view, depth:] = jnp.concatenate([high, jnp.zeros_like(low)], axis=1)
    y_back[...] = jnp.concatenate(highs + highs + lows, axis=1)


def bands(kernels, width, depth):
    views = kernels.shape[0]
    slab = width + 2 * PAD
    shapes = [
        (views * width, 3 * slab),
        (slab, 3 * views * width),
        (views, 2 * depth, 2 * depth),
        (views, 2 * depth, 2 * depth),
    ]
    return pl.pallas_call(
        matrices,
        out_shape=[jax.ShapeDtypeStruct(s, BF16) for s in shapes],
        in_specs=[pl.BlockSpec(memory_space=pltpu.SMEM)],
    )(kernels)


def dot(left, right):
    return jnp.dot(left, right, preferred_element_type=F32)


def fused(
    taps, own, xlo, xhi, ylo, yhi, views, lights, y_blur, y_back, z_blur, z_back,
    s_own, s_xlo, s_xhi, s_ylo, s_yhi, wide, mid,
):
    count = views.shape[0]
    planes, width, depth = own.shape[1:]
    reach = xlo.shape[1]
    total = planes + 2 * reach
    tiles = width // 8

    def place(index):
        if index < reach:
            return xlo, s_xlo, index
        if index < reach + planes:
            return own, s_own, index - reach
        return xhi, s_xhi, index - reach - planes

    def slab(index):
        ref, _, at = place(index)
        value = jnp.concatenate([ref[0, at], ylo[0, index], yhi[0, index]], axis=0)
        high, low = halves(value)
        return jnp.concatenate([high, low, high], axis=0)

    for index in range(0, total, 2):
        pair = jnp.concatenate([slab(index), slab(index + 1)], axis=1)
        out = dot(y_blur[...], pair)
        for view in range(count):
            rows = slice(view * width, (view + 1) * width)
            wide[view, index] = out[rows, :depth]
            wide[view, index + 1] = out[rows, depth:]

    def across(step, carry):
        view, rows = step // tiles, pl.ds(pl.multiple_of(step % tiles * 8, 8), 8)
        coef = [taps[view, 0, a] for a in range(2 * reach + 1)]
        sums = [None] * planes
        for index in range(total):
            value = wide[view, index, rows, :]
            for i in range(max(0, index - 2 * reach), min(planes - 1, index) + 1):
                term = coef[index - i] * value
                sums[i] = term if sums[i] is None else sums[i] + term
        for i in range(planes):
            mid[view, i, rows, :] = sums[i]
        return carry

    lax.fori_loop(0, count * tiles, across, 0)

    group = 4
    parts = planes // group

    def through(value, matrix):
        high, low = halves(value)
        out = dot(jnp.concatenate([high, low], axis=1), matrix)
        return out[:, :depth] + out[:, depth:]

    def deep(step, carry):
        view, at = step // parts, pl.ds(step % parts * group, group)
        field = through(mid[view, at].reshape(group * width, depth), z_blur[view])
        field = field.reshape(group, width, depth)
        light = lights[view][None]
        ratio = light * views[view, 0, at] / (light * field + 0.05)
        out = through(ratio.reshape(group * width, depth), z_back[view])
        mid[view, at] = out.reshape(group, width, depth)
        return carry

    lax.fori_loop(0, count * parts, deep, 0)

    def scatter(step, carry):
        view, rows = step // tiles, pl.ds(pl.multiple_of(step % tiles * 8, 8), 8)
        coef = [taps[view, 0, a] for a in range(2 * reach + 1)]
        values = [mid[view, i, rows, :] for i in range(planes)]
        for index in range(total):
            sums = None
            for i in range(max(0, index - 2 * reach), min(planes - 1, index) + 1):
                term = coef[index - i] * values[i]
                sums = term if sums is None else sums + term
            wide[view, index, rows, :] = sums
        return carry

    lax.fori_loop(0, count * tiles, scatter, 0)

    def stack(index):
        value = jnp.concatenate([wide[view, index] for view in range(count)], axis=0)
        high, low = halves(value)
        return jnp.concatenate([high, low, high], axis=0)

    for index in range(0, total, 2):
        pair = jnp.concatenate([stack(index), stack(index + 1)], axis=1)
        out = dot(y_back[...], pair)
        for side in range(2):
            _, ref, at = place(index + side)
            cols = slice(side * depth, (side + 1) * depth)
            ref[0, at] = out[:width, cols]
            s_ylo[0, index + side] = out[width : width + PAD, cols]
            s_yhi[0, index + side] = out[width + PAD :, cols]


def brick(channel, kernels, estimate, xlo, xhi, ylo, yhi, views, lights, mats):
    count = views.shape[0]
    planes, width, depth = estimate.shape[1:]
    reach = xlo.shape[1]
    total = planes + 2 * reach

    def whole(array):
        return pl.BlockSpec(array.shape, lambda i: (0,) * array.ndim)

    shapes = [(1, planes, width, depth)] + [(1, reach, width, depth)] * 2 + [(1, total, PAD, depth)] * 2
    return pl.pallas_call(
        fused,
        grid=(1,),
        out_shape=[jax.ShapeDtypeStruct(s, F32) for s in shapes],
        in_specs=[
            pl.BlockSpec(memory_space=pltpu.SMEM),
            pl.BlockSpec((1, planes, width, depth), lambda i: (channel, 0, 0, 0)),
            whole(xlo), whole(xhi), whole(ylo), whole(yhi),
            pl.BlockSpec((count, 1, planes, width, depth), lambda i: (0, channel, 0, 0, 0)),
            whole(lights),
        ] + [whole(m) for m in mats],
        out_specs=[pl.BlockSpec(s, lambda i: (0,) * 4) for s in shapes],
        scratch_shapes=[
            pltpu.VMEM((count, total, width, depth), F32),
            pltpu.VMEM((count, planes, width, depth), F32),
        ],
        compiler_params=pltpu.CompilerParams(vmem_limit_bytes=40 * 1024 * 1024),
    )(kernels, estimate, xlo, xhi, ylo, yhi, views, lights, *mats)


def illumination(profiles, owners, width):
    row, col = lax.axis_index("bx"), lax.axis_index("by")
    cols = lax.axis_size("by")
    source = lax.dynamic_index_in_dim(owners, row, axis=1, keepdims=False)
    count, _, depth = profiles.shape
    held = jnp.where((source == col)[:, None, None], profiles, F32(0.0))
    held = held.reshape(count, cols, width, depth)
    step = 1
    while step < cols:
        held = held.reshape(count, held.shape[1] // 2, 2, width, depth)
        odd = (col // step) % 2 == 1
        kept = jnp.where(odd, held[:, :, 1], held[:, :, 0])
        sent = jnp.where(odd, held[:, :, 0], held[:, :, 1])
        held = kept + lax.ppermute(sent, "by", [(i, i ^ step) for i in range(cols)])
        step *= 2
    return held.reshape(count, width, depth)


def shards(views, estimate, profiles, kernels, owners):
    channels, planes, width, depth = estimate.shape
    reach = kernels.shape[2] // 2
    mats = bands(kernels, width, depth)
    lights = illumination(profiles[0, 0], owners, width)
    results = []
    for c in range(channels):
        mine = estimate[c : c + 1]
        xlo = shift(mine[:, planes - reach :], "bx", 1)
        xhi = shift(mine[:, :reach], "bx", -1)
        ext = jnp.concatenate([xlo, mine, xhi], axis=1)
        ylo = shift(ext[:, :, width - PAD :], "by", 1)
        yhi = shift(ext[:, :, :PAD], "by", -1)
        s_own, s_xlo, s_xhi, s_ylo, s_yhi = brick(
            c, kernels, estimate, xlo, xhi, ylo, yhi, views, lights, mats
        )
        from_above = shift(s_ylo, "by", -1)
        from_below = shift(s_yhi, "by", 1)
        rim = jnp.concatenate([from_below, from_above], axis=2)
        low = s_xlo + rim[:, :reach]
        high = s_xhi + rim[:, reach + planes :]
        from_next = shift(low, "bx", -1)
        from_last = shift(high, "bx", 1)
        summed = s_own + rim[:, reach : reach + planes]
        nothing = jnp.zeros((1, planes - reach, width, depth), F32)
        summed = summed + jnp.concatenate([from_last, nothing], axis=1)
        summed = summed + jnp.concatenate([nothing, from_next], axis=1)
        results.append(mine * summed / views.shape[0])
    return jnp.concatenate(results, axis=0)


def solution(mesh):
    placed = (
        P(None, None, "bx", "by", None),
        P(None, "bx", "by", None),
        P("bx", "by", None, None, None),
        P(),
        P(),
    )
    return jax.shard_map(
        shards, mesh=mesh, in_specs=placed, out_specs=P(None, "bx", "by", None), check_vma=False
    )
```

profile of v0, /device:TPU:8, one launch (start us, length us, event | category | flops | bytes accessed | tf_op | source)
XLA Modules:
  0.0 98.9 jit_solution(1656176400871882805)
XLA Ops:
  0.0 0.9 fusion.12
  0.9 1.1 %broadcast_select_fusion = f32[3,4,2,32,128]{4,3,2,1,0:T(8,128)S(1)} fusion(f32[3,4,2,32,128]{4,3,2,1,0:T(8,128)} %bitcast.37, pred[3]{0:T(512)(128)(4,1)S(1)} %fusion.12), kind=kLoop, calls=%fused_computation.21 | loop fusion | flops 98304 | bytes 786435 | tf_op jit(solution)/shard_map/jit(_where)/select_n | solution.py:216
  2.1 0.1 collective-permute-start.4
  2.2 0.0 copy-done
  2.2 0.1 fusion.16
  2.3 1.3 %collective-permute-start.1 = (f32[1,15,32,128]{3,2,1,0:T(8,128)S(1)}, f32[1,15,32,128]{3,2,1,0:T(8,128)S(1)}, u32[]{:S(2)}, u32[]{:S(2)}) collective-permute-start(f32[1,15,32,128]{3,2,1,0:T(8,128)S(1)} %get-tuple-element.45), channel_id=1, source_target_pairs={{8,0},{16,8},{24,16},{9,1},{17,9},{25,17},{10,2},{18,10},{26,18},{... | collective-permute-start | bytes 737288 | tf_op jit(solution)/shard_map/ppermute | solution.py:18
  3.6 4.6 %collective-permute-start.11 = (f32[1,15,32,128]{3,2,1,0:T(8,128)S(1)}, f32[1,15,32,128]{3,2,1,0:T(8,128)S(1)}, u32[]{:S(2)}, u32[]{:S(2)}) collective-permute-start(f32[1,15,32,128]{3,2,1,0:T(8,128)S(1)} %get-tuple-element.46), channel_id=1, source_target_pairs={{0,8},{8,16},{16,24},{1,9},{9,17},{17,25},{2,10},{10,18},{18,26},{... | collective-permute-start | bytes 737288 | tf_op jit(solution)/shard_map/ppermute | solution.py:18
  8.2 4.3 %collective-permute-start = (f32[1,15,32,128]{3,2,1,0:T(8,128)S(1)}, f32[1,15,32,128]{3,2,1,0:T(8,128)S(1)}, u32[]{:S(2)}, u32[]{:S(2)}) collective-permute-start(f32[1,15,32,128]{3,2,1,0:T(8,128)S(1)} %get-tuple-element.47), channel_id=1, source_target_pairs={{0,8},{8,16},{16,24},{1,9},{9,17},{17,25},{2,10},{10,18},{18,26},{... | collective-permute-start | bytes 737288 | tf_op jit(solution)/shard_map/ppermute | solution.py:18
  12.5 1.3 %collective-permute-start.12 = (f32[1,15,32,128]{3,2,1,0:T(8,128)S(1)}, f32[1,15,32,128]{3,2,1,0:T(8,128)S(1)}, u32[]{:S(2)}, u32[]{:S(2)}) collective-permute-start(f32[1,15,32,128]{3,2,1,0:T(8,128)S(1)} %get-tuple-element.48), channel_id=1, source_target_pairs={{8,0},{16,8},{24,16},{9,1},{17,9},{25,17},{10,2},{18,10},{26,18},{... | collective-permute-start | bytes 737288 | tf_op jit(solution)/shard_map/ppermute | solution.py:18
  13.8 2.9 %shard_map.55 = (bf16[96,192]{1,0:T(8,128)(2,1)}, bf16[64,288]{1,0:T(8,128)(2,1)}, bf16[3,256,256]{2,1,0:T(8,128)(2,1)}, bf16[3,256,256]{2,1,0:T(8,128)(2,1)}) custom-call(f32[3,3,31]{2,1,0:T(4,128)} %taps.5), custom_call_target="tpu_custom_call" | custom-call | tf_op jit(solution)/shard_map/pallas_call | solution.py:74
  16.7 0.0 collective-permute-done.4
  16.8 0.5 collective-permute-start.5
  17.4 0.0 collective-permute-done.1.xhi
  17.4 0.0 collective-permute-done.11.xlo
  17.4 1.6 %collective-permute-done.xlo = f32[1,15,32,128]{3,2,1,0:T(8,128)S(1)} collective-permute-done((f32[1,15,32,128]{3,2,1,0:T(8,128)S(1)}, f32[1,15,32,128]{3,2,1,0:T(8,128)S(1)}, u32[]{:S(2)}, u32[]{:S(2)}) %collective-permute-start) | collective-permute-done | bytes 245792 | tf_op jit(solution)/shard_map/ppermute | solution.py:18
  19.0 9.4 %collective-permute-done.12.xhi = f32[1,15,32,128]{3,2,1,0:T(8,128)S(1)} collective-permute-done((f32[1,15,32,128]{3,2,1,0:T(8,128)S(1)}, f32[1,15,32,128]{3,2,1,0:T(8,128)S(1)}, u32[]{:S(2)}, u32[]{:S(2)}) %collective-permute-start.12) | collective-permute-done | bytes 245792 | tf_op jit(solution)/shard_map/ppermute | solution.py:18
  28.3 0.1 pad_maximum_fusion
  28.4 0.0 copy-start.1
  28.5 0.0 copy-start.2
  28.5 0.0 copy-start.3
  28.5 0.0 copy-start.4
  28.5 0.0 copy-start.5
  28.5 0.0 copy-start.6
  28.5 0.1 fusion.13
  28.6 2.1 %collective-permute-start.3 = (f32[1,46,16,128]{3,2,1,0:T(8,128)S(1)}, f32[1,46,16,128]{3,2,1,0:T(8,128)S(1)}, u32[]{:S(2)}, u32[]{:S(2)}) collective-permute-start(f32[1,46,16,128]{3,2,1,0:T(8,128)S(1)} %get-tuple-element.35), channel_id=1, source_target_pairs={{1,0},{2,1},{3,2},{4,3},{5,4},{6,5},{7,6},{9,8},{10,9},{11,10},{12... | collective-permute-start | bytes 1130504 | tf_op jit(solution)/shard_map/ppermute | solution.py:18
  30.6 2.4 %collective-permute-start.2 = (f32[1,46,16,128]{3,2,1,0:T(8,128)S(1)}, f32[1,46,16,128]{3,2,1,0:T(8,128)S(1)}, u32[]{:S(2)}, u32[]{:S(2)}) collective-permute-start(f32[1,46,16,128]{3,2,1,0:T(8,128)S(1)} %get-tuple-element.36), channel_id=1, source_target_pairs={{0,1},{1,2},{2,3},{3,4},{4,5},{5,6},{6,7},{8,9},{9,10},{10,11},{11... | collective-permute-start | bytes 1130504 | tf_op jit(solution)/shard_map/ppermute | solution.py:18
  33.0 0.0 collective-permute-done.5
  33.1 2.7 %collective-permute-start.6 = (f32[3,1,32,128]{3,2,0,1:T(8,128)S(1)}, f32[3,1,32,128]{3,2,0,1:T(8,128)S(1)}, u32[]{:S(2)}, u32[]{:S(2)}) collective-permute-start(f32[3,1,32,128]{3,2,0,1:T(8,128)S(1)} %select_bitcast_fusion.2), channel_id=1, source_target_pairs={{0,4},{1,5},{2,6},{3,7},{4,0},{5,1},{6,2},{7,3},{8,12},{9,13},{10,... | collective-permute-start | bytes 147464 | tf_op jit(solution)/shard_map/ppermute | solution.py:224
  35.8 0.1 fusion.14
  35.8 2.9 %collective-permute-start.14 = (f32[1,46,16,128]{3,2,1,0:T(8,128)S(1)}, f32[1,46,16,128]{3,2,1,0:T(8,128)S(1)}, u32[]{:S(2)}, u32[]{:S(2)}) collective-permute-start(f32[1,46,16,128]{3,2,1,0:T(8,128)S(1)} %get-tuple-element.39), channel_id=1, source_target_pairs={{1,0},{2,1},{3,2},{4,3},{5,4},{6,5},{7,6},{9,8},{10,9},{11,10},{12... | collective-permute-start | bytes 1130504 | tf_op jit(solution)/shard_map/ppermute | solution.py:18
  38.7 1.9 %collective-permute-start.13 = (f32[1,46,16,128]{3,2,1,0:T(8,128)S(1)}, f32[1,46,16,128]{3,2,1,0:T(8,128)S(1)}, u32[]{:S(2)}, u32[]{:S(2)}) collective-permute-start(f32[1,46,16,128]{3,2,1,0:T(8,128)S(1)} %get-tuple-element.40), channel_id=1, source_target_pairs={{0,1},{1,2},{2,3},{3,4},{4,5},{5,6},{6,7},{8,9},{9,10},{10,11},{11... | collective-permute-start | bytes 1130504 | tf_op jit(solution)/shard_map/ppermute | solution.py:18
  40.6 0.0 collective-permute-done.6
  40.7 0.0 collective-permute-done.3.yhi
  40.7 0.0 collective-permute-done.2.ylo
  40.7 0.0 copy-done.1
  40.7 0.0 copy-done.2
  40.7 0.0 copy-done.3
  40.7 0.0 copy-done.4
  40.7 0.0 copy-done.5
  40.7 0.0 copy-done.6
  40.7 9.5 %shard_map.56 = (f32[1,16,32,128]{3,2,1,0:T(8,128)S(1)}, f32[1,15,32,128]{3,2,1,0:T(8,128)S(1)}, f32[1,15,32,128]{3,2,1,0:T(8,128)S(1)}, f32[1,46,16,128]{3,2,1,0:T(8,128)S(1)}, f32[1,46,16,128]{3,2,1,0:T(8,128)S(1)}) custom-call(f32[3,3,31]{2,1,0:T(4,128)S(1)} %copy-done.6, f32[2,16,32,128]{3,2,1,0:T(8,128)S(1)} %copy-done, ...), custom_call_target="tpu_custom_call" | custom-call | tf_op jit(solution)/shard_map/pallas_call | solution.py:191
  50.3 2.1 %collective-permute-start.7 = (f32[1,46,16,128]{3,2,1,0:T(8,128)S(1)}, f32[1,46,16,128]{3,2,1,0:T(8,128)S(1)}, u32[]{:S(2)}, u32[]{:S(2)}) collective-permute-start(f32[1,46,16,128]{3,2,1,0:T(8,128)S(1)} %get-tuple-element.24), channel_id=1, source_target_pairs={{0,1},{1,2},{2,3},{3,4},{4,5},{5,6},{6,7},{8,9},{9,10},{10,11},{11... | collective-permute-start | bytes 1130504 | tf_op jit(solution)/shard_map/ppermute | solution.py:18
  52.4 3.4 %collective-permute-start.8 = (f32[1,46,16,128]{3,2,1,0:T(8,128)S(1)}, f32[1,46,16,128]{3,2,1,0:T(8,128)S(1)}, u32[]{:S(2)}, u32[]{:S(2)}) collective-permute-start(f32[1,46,16,128]{3,2,1,0:T(8,128)S(1)} %get-tuple-element.25), channel_id=1, source_target_pairs={{1,0},{2,1},{3,2},{4,3},{5,4},{6,5},{7,6},{9,8},{10,9},{11,10},{12... | collective-permute-start | bytes 1130504 | tf_op jit(solution)/shard_map/ppermute | solution.py:18
  55.8 0.0 collective-permute-done.14.yhi
  55.9 0.0 collective-permute-done.13.ylo
  55.9 9.5 %shard_map.57 = (f32[1,16,32,128]{3,2,1,0:T(8,128)S(1)}, f32[1,15,32,128]{3,2,1,0:T(8,128)S(1)}, f32[1,15,32,128]{3,2,1,0:T(8,128)S(1)}, f32[1,46,16,128]{3,2,1,0:T(8,128)S(1)}, f32[1,46,16,128]{3,2,1,0:T(8,128)S(1)}) custom-call(f32[3,3,31]{2,1,0:T(4,128)S(1)} %copy-done.6, f32[2,16,32,128]{3,2,1,0:T(8,128)S(1)} %copy-done, ...), custom_call_target="tpu_custom_call" | custom-call | tf_op jit(solution)/shard_map/pallas_call | solution.py:191
  65.4 2.3 %collective-permute-start.15 = (f32[1,46,16,128]{3,2,1,0:T(8,128)S(1)}, f32[1,46,16,128]{3,2,1,0:T(8,128)S(1)}, u32[]{:S(2)}, u32[]{:S(2)}) collective-permute-start(f32[1,46,16,128]{3,2,1,0:T(8,128)S(1)} %get-tuple-element.29), channel_id=1, source_target_pairs={{0,1},{1,2},{2,3},{3,4},{4,5},{5,6},{6,7},{8,9},{9,10},{10,11},{11... | collective-permute-start | bytes 1130504 | tf_op jit(solution)/shard_map/ppermute | solution.py:18
  67.7 3.3 %collective-permute-start.16 = (f32[1,46,16,128]{3,2,1,0:T(8,128)S(1)}, f32[1,46,16,128]{3,2,1,0:T(8,128)S(1)}, u32[]{:S(2)}, u32[]{:S(2)}) collective-permute-start(f32[1,46,16,128]{3,2,1,0:T(8,128)S(1)} %get-tuple-element.30), channel_id=1, source_target_pairs={{1,0},{2,1},{3,2},{4,3},{5,4},{6,5},{7,6},{9,8},{10,9},{11,10},{12... | collective-permute-start | bytes 1130504 | tf_op jit(solution)/shard_map/ppermute | solution.py:18
  71.0 0.0 collective-permute-done.7
  71.0 0.0 collective-permute-done.8
  71.1 0.1 slice_add_fusion.5
  71.2 4.3 %collective-permute-start.9 = (f32[1,15,32,128]{3,2,1,0:T(8,128)S(1)}, f32[1,15,32,128]{3,2,1,0:T(8,128)S(1)}, u32[]{:S(2)}, u32[]{:S(2)}) collective-permute-start(f32[1,15,32,128]{3,2,1,0:T(8,128)S(1)} %get-tuple-element.33), channel_id=1, source_target_pairs={{0,8},{8,16},{16,24},{1,9},{9,17},{17,25},{2,10},{10,18},{18,26},{... | collective-permute-start | bytes 737288 | tf_op jit(solution)/shard_map/ppermute | solution.py:18
  75.5 1.3 %collective-permute-start.10 = (f32[1,15,32,128]{3,2,1,0:T(8,128)S(1)}, f32[1,15,32,128]{3,2,1,0:T(8,128)S(1)}, u32[]{:S(2)}, u32[]{:S(2)}) collective-permute-start(f32[1,15,32,128]{3,2,1,0:T(8,128)S(1)} %get-tuple-element.34), channel_id=1, source_target_pairs={{8,0},{16,8},{24,16},{9,1},{17,9},{25,17},{10,2},{18,10},{26,18},{... | collective-permute-start | bytes 737288 | tf_op jit(solution)/shard_map/ppermute | solution.py:18
  76.8 0.0 collective-permute-done.15
  76.9 0.0 collective-permute-done.16
  76.9 0.1 slice_add_fusion.3
  77.0 4.6 %collective-permute-start.17 = (f32[1,15,32,128]{3,2,1,0:T(8,128)S(1)}, f32[1,15,32,128]{3,2,1,0:T(8,128)S(1)}, u32[]{:S(2)}, u32[]{:S(2)}) collective-permute-start(f32[1,15,32,128]{3,2,1,0:T(8,128)S(1)} %get-tuple-element.37), channel_id=1, source_target_pairs={{0,8},{8,16},{16,24},{1,9},{9,17},{17,25},{2,10},{10,18},{18,26},{... | collective-permute-start | bytes 737288 | tf_op jit(solution)/shard_map/ppermute | solution.py:18
  81.6 1.3 %collective-permute-start.18 = (f32[1,15,32,128]{3,2,1,0:T(8,128)S(1)}, f32[1,15,32,128]{3,2,1,0:T(8,128)S(1)}, u32[]{:S(2)}, u32[]{:S(2)}) collective-permute-start(f32[1,15,32,128]{3,2,1,0:T(8,128)S(1)} %get-tuple-element.38), channel_id=1, source_target_pairs={{8,0},{16,8},{24,16},{9,1},{17,9},{25,17},{10,2},{18,10},{26,18},{... | collective-permute-start | bytes 737288 | tf_op jit(solution)/shard_map/ppermute | solution.py:18
  82.9 0.0 collective-permute-done.9
  82.9 4.6 %collective-permute-done.10 = f32[1,15,32,128]{3,2,1,0:T(8,128)S(1)} collective-permute-done((f32[1,15,32,128]{3,2,1,0:T(8,128)S(1)}, f32[1,15,32,128]{3,2,1,0:T(8,128)S(1)}, u32[]{:S(2)}, u32[]{:S(2)}) %collective-permute-start.10) | collective-permute-done | bytes 245792 | tf_op jit(solution)/shard_map/ppermute | solution.py:18
  87.5 0.0 collective-permute-done.17
  87.6 10.2 %collective-permute-done.18 = f32[1,15,32,128]{3,2,1,0:T(8,128)S(1)} collective-permute-done((f32[1,15,32,128]{3,2,1,0:T(8,128)S(1)}, f32[1,15,32,128]{3,2,1,0:T(8,128)S(1)}, u32[]{:S(2)}, u32[]{:S(2)}) %collective-permute-start.18) | collective-permute-done | bytes 245792 | tf_op jit(solution)/shard_map/ppermute | solution.py:18
  97.8 0.3 fusion.7
  98.1 0.8 pad_maximum_fusion.2
  (13 shorter events, 0.3 us)
Async XLA Ops:
  0.0 2.2 %copy-start = (f32[2,16,32,128]{3,2,1,0:T(8,128)S(1)}, f32[2,16,32,128]{3,2,1,0:T(8,128)}, u32[]{:S(2)}) copy-start(f32[2,16,32,128]{3,2,1,0:T(8,128)} %own.3) | copy-start | bytes 1572868
  2.1 14.7 %collective-permute-start.4 = (f32[3,4,32,128]{3,2,1,0:T(8,128)S(1)}, f32[3,4,32,128]{3,2,1,0:T(8,128)S(1)}, u32[]{:S(2)}, u32[]{:S(2)}) collective-permute-start(f32[3,4,32,128]{3,2,1,0:T(8,128)S(1)} %select_bitcast_fusion), channel_id=1, source_target_pairs={{0,1},{1,0},{2,3},{3,2},{4,5},{5,4},{6,7},{7,6},{8,9},{9,8},{10,11... | collective-permute-start | bytes 589832 | tf_op jit(solution)/shard_map/ppermute | solution.py:224
  2.3 15.1 %collective-permute-start.1 = (f32[1,15,32,128]{3,2,1,0:T(8,128)S(1)}, f32[1,15,32,128]{3,2,1,0:T(8,128)S(1)}, u32[]{:S(2)}, u32[]{:S(2)}) collective-permute-start(f32[1,15,32,128]{3,2,1,0:T(8,128)S(1)} %get-tuple-element.45), channel_id=1, source_target_pairs={{8,0},{16,8},{24,16},{9,1},{17,9},{25,17},{10,2},{18,10},{26,18},{... | collective-permute-start | bytes 737288 | tf_op jit(solution)/shard_map/ppermute | solution.py:18
  3.6 13.8 %collective-permute-start.11 = (f32[1,15,32,128]{3,2,1,0:T(8,128)S(1)}, f32[1,15,32,128]{3,2,1,0:T(8,128)S(1)}, u32[]{:S(2)}, u32[]{:S(2)}) collective-permute-start(f32[1,15,32,128]{3,2,1,0:T(8,128)S(1)} %get-tuple-element.46), channel_id=1, source_target_pairs={{0,8},{8,16},{16,24},{1,9},{9,17},{17,25},{2,10},{10,18},{18,26},{... | collective-permute-start | bytes 737288 | tf_op jit(solution)/shard_map/ppermute | solution.py:18
  8.2 10.8 %collective-permute-start = (f32[1,15,32,128]{3,2,1,0:T(8,128)S(1)}, f32[1,15,32,128]{3,2,1,0:T(8,128)S(1)}, u32[]{:S(2)}, u32[]{:S(2)}) collective-permute-start(f32[1,15,32,128]{3,2,1,0:T(8,128)S(1)} %get-tuple-element.47), channel_id=1, source_target_pairs={{0,8},{8,16},{16,24},{1,9},{9,17},{17,25},{2,10},{10,18},{18,26},{... | collective-permute-start | bytes 737288 | tf_op jit(solution)/shard_map/ppermute | solution.py:18
  12.5 15.9 %collective-permute-start.12 = (f32[1,15,32,128]{3,2,1,0:T(8,128)S(1)}, f32[1,15,32,128]{3,2,1,0:T(8,128)S(1)}, u32[]{:S(2)}, u32[]{:S(2)}) collective-permute-start(f32[1,15,32,128]{3,2,1,0:T(8,128)S(1)} %get-tuple-element.48), channel_id=1, source_target_pairs={{8,0},{16,8},{24,16},{9,1},{17,9},{25,17},{10,2},{18,10},{26,18},{... | collective-permute-start | bytes 737288 | tf_op jit(solution)/shard_map/ppermute | solution.py:18
  16.8 16.2 %collective-permute-start.5 = (f32[3,2,32,128]{3,2,0,1:T(8,128)S(1)}, f32[3,2,32,128]{3,2,0,1:T(8,128)S(1)}, u32[]{:S(2)}, u32[]{:S(2)}) collective-permute-start(f32[3,2,32,128]{3,2,0,1:T(8,128)S(1)} %select_bitcast_fusion.1), channel_id=1, source_target_pairs={{0,2},{1,3},{2,0},{3,1},{4,6},{5,7},{6,4},{7,5},{8,10},{9,11},{10,... | collective-permute-start | bytes 294920 | tf_op jit(solution)/shard_map/ppermute | solution.py:224
  28.4 12.2 %copy-start.1 = (f32[3,2,16,32,128]{4,3,2,1,0:T(8,128)S(1)}, f32[3,2,16,32,128]{4,3,2,1,0:T(8,128)}, u32[]{:S(2)}) copy-start(f32[3,2,16,32,128]{4,3,2,1,0:T(8,128)} %views.3) | copy-start | bytes 4718596
  28.5 12.2 %copy-start.2 = (bf16[3,256,256]{2,1,0:T(8,128)(2,1)S(1)}, bf16[3,256,256]{2,1,0:T(8,128)(2,1)}, u32[]{:S(2)}) copy-start(bf16[3,256,256]{2,1,0:T(8,128)(2,1)} %get-tuple-element.21.z_blur) | copy-start | bytes 1179652
  28.5 12.2 %copy-start.3 = (bf16[3,256,256]{2,1,0:T(8,128)(2,1)S(1)}, bf16[3,256,256]{2,1,0:T(8,128)(2,1)}, u32[]{:S(2)}) copy-start(bf16[3,256,256]{2,1,0:T(8,128)(2,1)} %get-tuple-element.22.z_back) | copy-start | bytes 1179652
  28.5 12.2 %copy-start.4 = (bf16[96,192]{1,0:T(8,128)(2,1)S(1)}, bf16[96,192]{1,0:T(8,128)(2,1)}, u32[]{:S(2)}) copy-start(bf16[96,192]{1,0:T(8,128)(2,1)} %get-tuple-element.19.y_blur) | copy-start | bytes 110596
  28.5 12.2 %copy-start.5 = (bf16[64,288]{1,0:T(8,128)(2,1)S(1)}, bf16[64,288]{1,0:T(8,128)(2,1)}, u32[]{:S(2)}) copy-start(bf16[64,288]{1,0:T(8,128)(2,1)} %get-tuple-element.20.y_back) | copy-start | bytes 110596
  28.5 12.2 %copy-start.6 = (f32[3,3,31]{2,1,0:T(4,128)S(1)}, f32[3,3,31]{2,1,0:T(4,128)}, u32[]{:S(2)}) copy-start(f32[3,3,31]{2,1,0:T(4,128)} %taps.5) | copy-start | bytes 3352
  28.6 12.1 %collective-permute-start.3 = (f32[1,46,16,128]{3,2,1,0:T(8,128)S(1)}, f32[1,46,16,128]{3,2,1,0:T(8,128)S(1)}, u32[]{:S(2)}, u32[]{:S(2)}) collective-permute-start(f32[1,46,16,128]{3,2,1,0:T(8,128)S(1)} %get-tuple-element.35), channel_id=1, source_target_pairs={{1,0},{2,1},{3,2},{4,3},{5,4},{6,5},{7,6},{9,8},{10,9},{11,10},{12... | collective-permute-start | bytes 1130504 | tf_op jit(solution)/shard_map/ppermute | solution.py:18
  30.6 10.0 %collective-permute-start.2 = (f32[1,46,16,128]{3,2,1,0:T(8,128)S(1)}, f32[1,46,16,128]{3,2,1,0:T(8,128)S(1)}, u32[]{:S(2)}, u32[]{:S(2)}) collective-permute-start(f32[1,46,16,128]{3,2,1,0:T(8,128)S(1)} %get-tuple-element.36), channel_id=1, source_target_pairs={{0,1},{1,2},{2,3},{3,4},{4,5},{5,6},{6,7},{8,9},{9,10},{10,11},{11... | collective-permute-start | bytes 1130504 | tf_op jit(solution)/shard_map/ppermute | solution.py:18
  33.1 7.5 %collective-permute-start.6 = (f32[3,1,32,128]{3,2,0,1:T(8,128)S(1)}, f32[3,1,32,128]{3,2,0,1:T(8,128)S(1)}, u32[]{:S(2)}, u32[]{:S(2)}) collective-permute-start(f32[3,1,32,128]{3,2,0,1:T(8,128)S(1)} %select_bitcast_fusion.2), channel_id=1, source_target_pairs={{0,4},{1,5},{2,6},{3,7},{4,0},{5,1},{6,2},{7,3},{8,12},{9,13},{10,... | collective-permute-start | bytes 147464 | tf_op jit(solution)/shard_map/ppermute | solution.py:224
  35.8 20.0 %collective-permute-start.14 = (f32[1,46,16,128]{3,2,1,0:T(8,128)S(1)}, f32[1,46,16,128]{3,2,1,0:T(8,128)S(1)}, u32[]{:S(2)}, u32[]{:S(2)}) collective-permute-start(f32[1,46,16,128]{3,2,1,0:T(8,128)S(1)} %get-tuple-element.39), channel_id=1, source_target_pairs={{1,0},{2,1},{3,2},{4,3},{5,4},{6,5},{7,6},{9,8},{10,9},{11,10},{12... | collective-permute-start | bytes 1130504 | tf_op jit(solution)/shard_map/ppermute | solution.py:18
  38.7 17.2 %collective-permute-start.13 = (f32[1,46,16,128]{3,2,1,0:T(8,128)S(1)}, f32[1,46,16,128]{3,2,1,0:T(8,128)S(1)}, u32[]{:S(2)}, u32[]{:S(2)}) collective-permute-start(f32[1,46,16,128]{3,2,1,0:T(8,128)S(1)} %get-tuple-element.40), channel_id=1, source_target_pairs={{0,1},{1,2},{2,3},{3,4},{4,5},{5,6},{6,7},{8,9},{9,10},{10,11},{11... | collective-permute-start | bytes 1130504 | tf_op jit(solution)/shard_map/ppermute | solution.py:18
  50.3 20.7 %collective-permute-start.7 = (f32[1,46,16,128]{3,2,1,0:T(8,128)S(1)}, f32[1,46,16,128]{3,2,1,0:T(8,128)S(1)}, u32[]{:S(2)}, u32[]{:S(2)}) collective-permute-start(f32[1,46,16,128]{3,2,1,0:T(8,128)S(1)} %get-tuple-element.24), channel_id=1, source_target_pairs={{0,1},{1,2},{2,3},{3,4},{4,5},{5,6},{6,7},{8,9},{9,10},{10,11},{11... | collective-permute-start | bytes 1130504 | tf_op jit(solution)/shard_map/ppermute | solution.py:18
  52.4 18.6 %collective-permute-start.8 = (f32[1,46,16,128]{3,2,1,0:T(8,128)S(1)}, f32[1,46,16,128]{3,2,1,0:T(8,128)S(1)}, u32[]{:S(2)}, u32[]{:S(2)}) collective-permute-start(f32[1,46,16,128]{3,2,1,0:T(8,128)S(1)} %get-tuple-element.25), channel_id=1, source_target_pairs={{1,0},{2,1},{3,2},{4,3},{5,4},{6,5},{7,6},{9,8},{10,9},{11,10},{12... | collective-permute-start | bytes 1130504 | tf_op jit(solution)/shard_map/ppermute | solution.py:18
  65.4 11.4 %collective-permute-start.15 = (f32[1,46,16,128]{3,2,1,0:T(8,128)S(1)}, f32[1,46,16,128]{3,2,1,0:T(8,128)S(1)}, u32[]{:S(2)}, u32[]{:S(2)}) collective-permute-start(f32[1,46,16,128]{3,2,1,0:T(8,128)S(1)} %get-tuple-element.29), channel_id=1, source_target_pairs={{0,1},{1,2},{2,3},{3,4},{4,5},{5,6},{6,7},{8,9},{9,10},{10,11},{11... | collective-permute-start | bytes 1130504 | tf_op jit(solution)/shard_map/ppermute | solution.py:18
  67.7 9.2 %collective-permute-start.16 = (f32[1,46,16,128]{3,2,1,0:T(8,128)S(1)}, f32[1,46,16,128]{3,2,1,0:T(8,128)S(1)}, u32[]{:S(2)}, u32[]{:S(2)}) collective-permute-start(f32[1,46,16,128]{3,2,1,0:T(8,128)S(1)} %get-tuple-element.30), channel_id=1, source_target_pairs={{1,0},{2,1},{3,2},{4,3},{5,4},{6,5},{7,6},{9,8},{10,9},{11,10},{12... | collective-permute-start | bytes 1130504 | tf_op jit(solution)/shard_map/ppermute | solution.py:18
  71.2 11.7 %collective-permute-start.9 = (f32[1,15,32,128]{3,2,1,0:T(8,128)S(1)}, f32[1,15,32,128]{3,2,1,0:T(8,128)S(1)}, u32[]{:S(2)}, u32[]{:S(2)}) collective-permute-start(f32[1,15,32,128]{3,2,1,0:T(8,128)S(1)} %get-tuple-element.33), channel_id=1, source_target_pairs={{0,8},{8,16},{16,24},{1,9},{9,17},{17,25},{2,10},{10,18},{18,26},{... | collective-permute-start | bytes 737288 | tf_op jit(solution)/shard_map/ppermute | solution.py:18
  75.5 12.0 %collective-permute-start.10 = (f32[1,15,32,128]{3,2,1,0:T(8,128)S(1)}, f32[1,15,32,128]{3,2,1,0:T(8,128)S(1)}, u32[]{:S(2)}, u32[]{:S(2)}) collective-permute-start(f32[1,15,32,128]{3,2,1,0:T(8,128)S(1)} %get-tuple-element.34), channel_id=1, source_target_pairs={{8,0},{16,8},{24,16},{9,1},{17,9},{25,17},{10,2},{18,10},{26,18},{... | collective-permute-start | bytes 737288 | tf_op jit(solution)/shard_map/ppermute | solution.py:18
  77.0 10.5 %collective-permute-start.17 = (f32[1,15,32,128]{3,2,1,0:T(8,128)S(1)}, f32[1,15,32,128]{3,2,1,0:T(8,128)S(1)}, u32[]{:S(2)}, u32[]{:S(2)}) collective-permute-start(f32[1,15,32,128]{3,2,1,0:T(8,128)S(1)} %get-tuple-element.37), channel_id=1, source_target_pairs={{0,8},{8,16},{16,24},{1,9},{9,17},{17,25},{2,10},{10,18},{18,26},{... | collective-permute-start | bytes 737288 | tf_op jit(solution)/shard_map/ppermute | solution.py:18
  81.6 16.2 %collective-permute-start.18 = (f32[1,15,32,128]{3,2,1,0:T(8,128)S(1)}, f32[1,15,32,128]{3,2,1,0:T(8,128)S(1)}, u32[]{:S(2)}, u32[]{:S(2)}) collective-permute-start(f32[1,15,32,128]{3,2,1,0:T(8,128)S(1)} %get-tuple-element.38), channel_id=1, source_target_pairs={{8,0},{16,8},{24,16},{9,1},{17,9},{25,17},{10,2},{18,10},{26,18},{... | collective-permute-start | bytes 737288 | tf_op jit(solution)/shard_map/ppermute | solution.py:18
where the time goes:
time: 99.5 us; the launch traced here: 98.9 us
  starting transfers between devices  46.5 us (47%)
  waiting for transfers between devices  25.9 us (26%)
  Pallas kernels  21.9 us (22%)
  other arithmetic  3.54 us (4%)
    ppermute x16, starting transfers between devices, shift(): return lax.ppermute(value, axis, pairs)  43.3 us
    ppermute x16, waiting for transfers between devices, shift(): return lax.ppermute(value, axis, pairs)  25.9 us
    pallas_call x2, Pallas kernels, brick(): pl.pallas_call(fused, grid=(1,), out_shape=[jax.ShapeDtypeStruct(s, F32)...  19.1 us
    ppermute x3, starting transfers between devices, illumination(): held = kept + lax.ppermute(sent, 'by', [(i, i ^ step) for i in range(cols)])  3.26 us
    pallas_call x1, Pallas kernels, bands(): pl.pallas_call(matrices, out_shape=[jax.ShapeDtypeStruct(s, BF16) for s i...  2.89 us
  transfers between devices with their start and end apart: 19, of which 4 were waited for; matrix products, arithmetic and copies ran while one was open for 1% of the time, Pallas kernels for 22%

commit v1 on v0

v1 whole, which is shorter than its diff:
```python
import functools

import jax
import jax.numpy as jnp
from jax import lax
from jax.experimental import pallas as pl
from jax.experimental.pallas import tpu as pltpu
from jax.sharding import PartitionSpec as P

F32 = jnp.float32
BF16 = jnp.bfloat16
SMALL = pltpu.CompilerParams(vmem_limit_bytes=8 * 1024 * 1024)
SKEW = 8
PAD = 16


def halves(value):
    high = value.astype(BF16)
    return high, (value - high.astype(F32)).astype(BF16)


def position(shape, dim, own, rim, reach, odd):
    at = lax.broadcasted_iota(jnp.int32, shape, dim)
    outside = 4 * own + 4 * rim
    step = jnp.where(at < own + rim, at - own, at - own - rim)
    above = own + step
    below = step - reach
    first = jnp.where(odd, below, above)
    second = jnp.where(odd, above, below)
    place = jnp.where(at < own + rim, first, second)
    place = jnp.where(step < reach, place, outside)
    return jnp.where(at < own, at, place)


def matrices(taps, parity, x_blur, x_back, y_blur, y_back, z_blur, z_back):
    views, _, count = taps.shape
    half = count // 2
    planes = x_blur.shape[0] // views
    wide = x_back.shape[0]
    width, slab = y_blur.shape[1], y_back.shape[1]
    depth = z_blur.shape[1] // 2
    odd_x, odd_y = parity[0] == 1, parity[1] == 1

    def pick(view, axis, offset):
        total = jnp.zeros(offset.shape, F32)
        for step in range(count):
            total = jnp.where(offset == step, taps[view, axis, step], total)
        return halves(total)

    def index(shape, dim):
        return lax.broadcasted_iota(jnp.int32, shape, dim)

    def tripled(high, low):
        return jnp.concatenate([high, high, low], axis=1)

    highs, lows = [], []
    for view in range(views):
        shape = (planes, wide)
        at = position(shape, 1, planes, PAD, half, odd_x)
        high, low = pick(view, 0, at - index(shape, 0) + half)
        x_blur[view * planes : (view + 1) * planes] = tripled(high, low)
        shape = (wide, planes)
        at = position(shape, 0, planes, PAD, half, odd_x)
        high, low = pick(view, 0, at - index(shape, 1) + half)
        highs.append(high)
        lows.append(low)
        shape = (width, slab)
        at = position(shape, 1, width, PAD, PAD, odd_y)
        y_blur[view] = tripled(*pick(view, 1, at - index(shape, 0) + half))
        shape = (slab, width)
        at = position(shape, 0, width, PAD, PAD, odd_y)
        y_back[view] = tripled(*pick(view, 1, at - index(shape, 1) + half))
        shape = (depth, depth)
        offset = index(shape, 0) - index(shape, 1) + half
        for ref, at in ((z_blur, offset), (z_back, 2 * half - offset)):
            high, low = pick(view, 2, at)
            ref[view, :depth] = jnp.concatenate([high, low], axis=1)
            ref[view, depth:] = jnp.concatenate([high, jnp.zeros_like(low)], axis=1)
    x_back[...] = jnp.concatenate(highs + highs + lows, axis=1)


def bands(kernels, parity, planes, width, depth):
    views = kernels.shape[0]
    wide, slab = planes + 2 * PAD, width + 2 * PAD
    shapes = [
        (views * planes, 3 * wide),
        (wide, 3 * views * planes),
        (views, width, 3 * slab),
        (views, slab, 3 * width),
        (views, 2 * depth, 2 * depth),
        (views, 2 * depth, 2 * depth),
    ]
    return pl.pallas_call(
        matrices,
        out_shape=[jax.ShapeDtypeStruct(s, BF16) for s in shapes],
        in_specs=[pl.BlockSpec(memory_space=pltpu.SMEM)] * 2,
        compiler_params=SMALL,
    )(kernels, parity)


def dot(left, right):
    return jnp.dot(left, right, preferred_element_type=F32)


def fused(
    own, xa, xb, yc, yd, views, lights, x_blur, x_back, y_blur, y_back, z_blur, z_back,
    s_own, s_xa, s_xb, s_yc, s_yd, ext, mid,
):
    count = views.shape[0]
    planes, width, depth = own.shape[1:]
    reach = xa.shape[1]
    wide, slab = planes + 2 * PAD, width + 2 * PAD
    pitch = slab + SKEW
    blocks = ((0, planes, own, s_own, 0), (planes, reach, xa, s_xa, planes), (planes + PAD, reach, xb, s_xb, planes + reach))

    def stacked(value):
        high, low = halves(value)
        return jnp.concatenate([high, low, high], axis=0)

    for start, size, ref, _, at in blocks:
        for i in range(size):
            base = (start + i) * pitch
            ext[base : base + width] = ref[0, i]
            ext[base + width : base + width + PAD] = yc[0, at + i]
            ext[base + width + PAD : base + slab] = yd[0, at + i]
    for plane in (planes + reach, planes + PAD + reach):
        ext[plane * pitch : plane * pitch + slab] = jnp.zeros((slab, depth), F32)

    rows = count * planes
    for y in range(0, slab, 2):
        pair = [stacked(ext[pl.ds(y + side, wide, stride=pitch), :]) for side in range(2)]
        out = dot(x_blur[...], jnp.concatenate(pair, axis=1))
        for side in range(2):
            mid[pl.ds(y + side, rows, stride=pitch), :] = out[:, side * depth : (side + 1) * depth]

    def through(value, matrix):
        high, low = halves(value)
        out = dot(jnp.concatenate([high, low], axis=1), matrix)
        return out[:, :depth] + out[:, depth:]

    def alone(view, matrix, values):
        outs = []
        for i in range(0, planes, 2):
            pair = jnp.concatenate([stacked(values[i]), stacked(values[i + 1])], axis=1)
            out = dot(matrix, pair)
            outs += [out[:, :depth], out[:, depth:]]
        return outs

    fields = []
    for view in range(count):
        bases = [(view * planes + i) * pitch for i in range(planes)]
        values = [mid[base : base + slab] for base in bases]
        fields.append(jnp.concatenate(alone(view, y_blur[view], values), axis=0))
    fields = [through(fields[view], z_blur[view]) for view in range(count)]
    ratios = []
    for view in range(count):
        light = lights[view][None]
        field = fields[view].reshape(planes, width, depth)
        ratio = light * views[view, 0] / (light * field + 0.05)
        ratios.append(ratio.reshape(planes * width, depth))
    backs = [through(ratios[view], z_back[view]) for view in range(count)]
    for view in range(count):
        values = [backs[view][i * width : (i + 1) * width] for i in range(planes)]
        for i, out in enumerate(alone(view, y_back[view], values)):
            base = (view * planes + i) * pitch
            mid[base : base + slab] = out

    for y in range(0, slab, 2):
        pair = [stacked(mid[pl.ds(y + side, rows, stride=pitch), :]) for side in range(2)]
        out = dot(x_back[...], jnp.concatenate(pair, axis=1))
        for side in range(2):
            ext[pl.ds(y + side, wide, stride=pitch), :] = out[:, side * depth : (side + 1) * depth]

    for start, size, _, ref, at in blocks:
        for i in range(size):
            base = (start + i) * pitch
            ref[0, i] = ext[base : base + width]
            s_yc[0, at + i] = ext[base + width : base + width + PAD]
            s_yd[0, at + i] = ext[base + width + PAD : base + slab]


def brick(channel, estimate, xa, xb, yc, yd, views, lights, mats):
    count = views.shape[0]
    planes, width, depth = estimate.shape[1:]
    reach = xa.shape[1]
    total = planes + 2 * reach
    wide, slab = planes + 2 * PAD, width + 2 * PAD

    shapes = [(1, planes, width, depth)] + [(1, reach, width, depth)] * 2 + [(1, total, PAD, depth)] * 2
    return pl.pallas_call(
        fused,
        grid=(1,),
        out_shape=[jax.ShapeDtypeStruct(s, F32) for s in shapes],
        in_specs=[
            pl.BlockSpec((1, planes, width, depth), lambda i: (channel, 0, 0, 0)),
            whole(xa), whole(xb), whole(yc), whole(yd),
            pl.BlockSpec((count, 1, planes, width, depth), lambda i: (0, channel, 0, 0, 0)),
            whole(lights),
        ] + [whole(m) for m in mats],
        out_specs=[pl.BlockSpec(s, lambda i: (0,) * 4) for s in shapes],
        scratch_shapes=[
            pltpu.VMEM((wide * (slab + SKEW), depth), F32),
            pltpu.VMEM((count * planes * (slab + SKEW), depth), F32),
        ],
        compiler_params=pltpu.CompilerParams(vmem_limit_bytes=24 * 1024 * 1024),
    )(estimate, xa, xb, yc, yd, views, lights, *mats)


def trade(value, axis, first):
    count = lax.axis_size(axis)
    pairs = []
    for low in range(0 if first else 1, count - 1, 2):
        pairs += [(low, low + 1), (low + 1, low)]
    return lax.ppermute(value, axis, pairs)


def illumination(profiles, owners, width):
    row, col = lax.axis_index("bx"), lax.axis_index("by")
    cols = lax.axis_size("by")
    source = lax.dynamic_index_in_dim(owners, row, axis=1, keepdims=False)
    count, _, depth = profiles.shape
    held = jnp.where((source == col)[:, None, None], profiles, F32(0.0))
    held = held.reshape(count, cols, width, depth)
    step = 1
    while step < cols:
        held = held.reshape(count, held.shape[1] // 2, 2, width, depth)
        odd = (col // step) % 2 == 1
        kept = jnp.where(odd, held[:, :, 1], held[:, :, 0])
        sent = jnp.where(odd, held[:, :, 0], held[:, :, 1])
        held = kept + lax.ppermute(sent, "by", [(i, i ^ step) for i in range(cols)])
        step *= 2
    return held.reshape(count, width, depth)


def whole(array):
    return pl.BlockSpec(array.shape, lambda i: (0,) * array.ndim)


SCALARS = pl.BlockSpec(memory_space=pltpu.SMEM)


def one_channel(array, channel):
    return pl.BlockSpec((1,) + array.shape[1:], lambda i: (channel, 0, 0, 0))


def row_starts(parity, width):
    first = jnp.where(parity[1] == 1, 0, width - PAD)
    second = jnp.where(parity[1] == 1, width - PAD, 0)
    return tuple(pl.ds(pl.multiple_of(start, PAD), PAD) for start in (first, second))


def rim_rows(parity, own, xa, xb, yc, yd):
    planes, width, reach = own.shape[1], own.shape[2], xa.shape[1]
    for out, rows in zip((yc, yd), row_starts(parity, width)):
        out[0, :planes] = own[0, :, rows, :]
        out[0, planes : planes + reach] = xa[0, :, rows, :]
        out[0, planes + reach :] = xb[0, :, rows, :]


def pack_rows(channel, parity, estimate, xa, xb):
    _, planes, _, depth = estimate.shape
    shape = (1, planes + 2 * xa.shape[1], PAD, depth)
    return pl.pallas_call(
        rim_rows,
        grid=(1,),
        out_shape=[jax.ShapeDtypeStruct(shape, F32)] * 2,
        in_specs=[SCALARS, one_channel(estimate, channel), whole(xa), whole(xb)],
        out_specs=[pl.BlockSpec(shape, lambda i: (0,) * 4)] * 2,
        compiler_params=SMALL,
    )(parity, estimate, xa, xb)


def rim_planes(parity, s_xa, s_xb, rc, rd, out_a, out_b):
    reach, width = s_xa.shape[1:3]
    base = rc.shape[1] - 2 * reach
    out_a[...] = s_xa[...]
    out_b[...] = s_xb[...]
    for got, rows in zip((rc, rd), row_starts(parity, width)):
        out_a[0, :, rows, :] += got[0, base : base + reach]
        out_b[0, :, rows, :] += got[0, base + reach :]


def pack_planes(parity, s_xa, s_xb, rc, rd):
    return pl.pallas_call(
        rim_planes,
        grid=(1,),
        out_shape=[jax.ShapeDtypeStruct(s_xa.shape, F32)] * 2,
        in_specs=[SCALARS, whole(s_xa), whole(s_xb), whole(rc), whole(rd)],
        out_specs=[whole(s_xa)] * 2,
        compiler_params=SMALL,
    )(parity, s_xa, s_xb, rc, rd)


def closing(parity, estimate, s_own, rc, rd, qa, qb, out, *, views):
    planes, width = s_own.shape[1:3]
    reach = qa.shape[1]
    out[...] = s_own[...]
    for got, rows in zip((rc, rd), row_starts(parity, width)):
        out[0, :, rows, :] += got[0, :planes]
    first = jnp.where(parity[0] == 1, 0, planes - reach)
    second = jnp.where(parity[0] == 1, planes - reach, 0)
    out[0, pl.ds(first, reach)] += qa[0]
    out[0, pl.ds(second, reach)] += qb[0]
    out[...] = estimate[...] * out[...] / views


def finish(channel, views, parity, estimate, s_own, rc, rd, qa, qb, done):
    planes = s_own.shape[1]

    def own_planes(array):
        return pl.BlockSpec((1, planes) + array.shape[2:], lambda i: (0,) * 4)

    def body(*refs):
        closing(*refs[:7], refs[-1], views=views)

    more = [] if done is None else [done]
    return pl.pallas_call(
        body,
        grid=(1,),
        out_shape=jax.ShapeDtypeStruct(estimate.shape, F32),
        in_specs=[
            SCALARS, one_channel(estimate, channel), whole(s_own), own_planes(rc), own_planes(rd),
            whole(qa), whole(qb),
        ] + [pl.BlockSpec(memory_space=pl.ANY)] * len(more),
        out_specs=one_channel(estimate, channel),
        compiler_params=SMALL,
        input_output_aliases={7: 0} if more else {},
    )(parity, estimate, s_own, rc, rd, qa, qb, *more)


def shards(views, estimate, profiles, kernels, owners):
    channels, planes, width, depth = estimate.shape
    reach = kernels.shape[2] // 2
    odd_x, odd_y = lax.axis_index("bx") % 2, lax.axis_index("by") % 2
    parity = jnp.stack([odd_x, odd_y]).astype(jnp.int32)
    x_first, x_second = (planes - reach) * (1 - odd_x), (planes - reach) * odd_x
    halo = []
    for c in range(channels):
        mine = estimate[c : c + 1]
        xa = trade(lax.dynamic_slice_in_dim(mine, x_first, reach, axis=1), "bx", True)
        xb = trade(lax.dynamic_slice_in_dim(mine, x_second, reach, axis=1), "bx", False)
        halo.append((xa, xb))
    mats = bands(kernels, parity, planes, width, depth)
    lights = illumination(profiles[0, 0], owners, width)
    parts = []
    for c in range(channels):
        xa, xb = halo[c]
        yc, yd = pack_rows(c, parity, estimate, xa, xb)
        yc, yd = trade(yc, "by", True), trade(yd, "by", False)
        parts.append(brick(c, estimate, xa, xb, yc, yd, views, lights, mats))
    ends = []
    for c in range(channels):
        s_own, s_xa, s_xb, s_yc, s_yd = parts[c]
        rc, rd = trade(s_yc, "by", True), trade(s_yd, "by", False)
        qa, qb = pack_planes(parity, s_xa, s_xb, rc, rd)
        ends.append((s_own, rc, rd, trade(qa, "bx", True), trade(qb, "bx", False)))
    done = None
    for c in range(channels):
        done = finish(c, views.shape[0], parity, estimate, *ends[c], done)
    return done


def solution(mesh):
    placed = (
        P(None, None, "bx", "by", None),
        P(None, "bx", "by", None),
        P("bx", "by", None, None, None),
        P(),
        P(),
    )
    return jax.shard_map(
        shards, mesh=mesh, in_specs=placed, out_specs=P(None, "bx", "by", None), check_vma=False
    )
```

time: 99.5 us -> 77.8 us (0.78)
  the two profiles are of different devices: /device:TPU:8 before, /device:TPU:9 now
where the time goes in v1:
time: 77.8 us; the launch traced here: 77.5 us
  starting transfers between devices  38.7 us (50%)
  waiting for transfers between devices  23.3 us (30%)
  Pallas kernels  12.7 us (16%)
  other arithmetic  2.23 us (3%)
    ppermute x16, starting transfers between devices, trade(): return lax.ppermute(value, axis, pairs)  37.7 us
    ppermute x16, waiting for transfers between devices, trade(): return lax.ppermute(value, axis, pairs)  19.1 us
    pallas_call x2, Pallas kernels, brick(): pl.pallas_call(fused, grid=(1,), out_shape=[jax.ShapeDtypeStruct(s, F32)...  5.13 us
    ppermute x3, waiting for transfers between devices, illumination(): held = kept + lax.ppermute(sent, 'by', [(i, i ^ step) for i in range(cols)])  4.17 us
    pallas_call x2, Pallas kernels, finish(): pl.pallas_call(body, grid=(1,), out_shape=jax.ShapeDtypeStruct(estimate.s...  2.75 us
    pallas_call x1, Pallas kernels, bands(): pl.pallas_call(matrices, out_shape=[jax.ShapeDtypeStruct(s, BF16) for s i...  2.31 us
  transfers between devices with their start and end apart: 19, of which 5 were waited for; matrix products, arithmetic and copies ran while one was open for 0% of the time, Pallas kernels for 15%

profile of v1, /device:TPU:9, one launch (start us, length us, event | category | flops | bytes accessed | tf_op | source)
XLA Modules:
  0.0 77.5 jit_solution(15155976980508248025)
XLA Ops:
  0.0 0.0 copy-start
  0.0 0.9 %fusion.4 = pred[3]{0:T(512)(128)(4,1)S(1)} fusion(s32[3,4]{1,0:T(4,128)} %param.9, s32[]{:T(128)S(6)} %select_n.127, s32[]{:T(128)S(6)} %axis_index.33), kind=kLoop, calls=%fused_computation.12 | loop fusion | flops 3 | bytes 23 | tf_op jit(solution)/shard_map/eq | solution.py:222
  0.9 1.1 %broadcast_select_fusion = f32[3,4,2,32,128]{4,3,2,1,0:T(8,128)S(1)} fusion(f32[3,4,2,32,128]{4,3,2,1,0:T(8,128)} %bitcast.39, pred[3]{0:T(512)(128)(4,1)S(1)} %fusion.4), kind=kLoop, calls=%fused_computation.4 | loop fusion | flops 98304 | bytes 786435 | tf_op jit(solution)/shard_map/jit(_where)/select_n | solution.py:222
  2.1 0.7 collective-permute-start.4
  2.8 0.0 copy-done
  2.9 1.3 %collective-permute-start.11 = (f32[1,15,32,128]{3,2,1,0:T(8,128)S(1)}, f32[1,15,32,128]{3,2,1,0:T(8,128)S(1)}, u32[]{:S(2)}, u32[]{:S(2)}) collective-permute-start(f32[1,15,32,128]{3,2,1,0:T(8,128)S(1)} %get-tuple-element.56), channel_id=1, source_target_pairs={{0,8},{8,0},{16,24},{24,16},{1,9},{9,1},{17,25},{25,17},{2,10},{10... | collective-permute-start | bytes 737288 | tf_op jit(solution)/shard_map/ppermute | solution.py:214
  4.2 0.7 collective-permute-start.12
  4.9 3.7 %collective-permute-start = (f32[1,15,32,128]{3,2,1,0:T(8,128)S(1)}, f32[1,15,32,128]{3,2,1,0:T(8,128)S(1)}, u32[]{:S(2)}, u32[]{:S(2)}) collective-permute-start(f32[1,15,32,128]{3,2,1,0:T(8,128)S(1)} %get-tuple-element.58), channel_id=1, source_target_pairs={{0,8},{8,0},{16,24},{24,16},{1,9},{9,1},{17,25},{25,17},{2,10},{10... | collective-permute-start | bytes 737288 | tf_op jit(solution)/shard_map/ppermute | solution.py:214
  8.6 0.7 collective-permute-start.1
  9.4 0.0 collective-permute-done.4
  9.4 0.0 copy-start.2
  9.5 0.0 copy-start.1
  9.5 0.2 collective-permute-start.5
  9.7 0.1 pad_add_fusion.parity.refs_0_
  9.8 0.7 collective-permute-done.11.xa
  10.5 0.0 collective-permute-done.12.xb
  10.5 0.6 shard_map.59
  11.1 1.3 %collective-permute-start.13 = (f32[1,46,16,128]{3,2,1,0:T(8,128)S(1)}, f32[1,46,16,128]{3,2,1,0:T(8,128)S(1)}, u32[]{:S(2)}, u32[]{:S(2)}) collective-permute-start(f32[1,46,16,128]{3,2,1,0:T(8,128)S(1)} %get-tuple-element.44), channel_id=1, source_target_pairs={{0,1},{1,0},{2,3},{3,2},{4,5},{5,4},{6,7},{7,6},{8,9},{9,8},{10,11... | collective-permute-start | bytes 1130504 | tf_op jit(solution)/shard_map/ppermute | solution.py:214
  12.5 3.4 %collective-permute-start.14 = (f32[1,46,16,128]{3,2,1,0:T(8,128)S(1)}, f32[1,46,16,128]{3,2,1,0:T(8,128)S(1)}, u32[]{:S(2)}, u32[]{:S(2)}) collective-permute-start(f32[1,46,16,128]{3,2,1,0:T(8,128)S(1)} %get-tuple-element.45), channel_id=1, source_target_pairs={{1,2},{2,1},{3,4},{4,3},{5,6},{6,5},{9,10},{10,9},{11,12},{12,11},... | collective-permute-start | bytes 1130504 | tf_op jit(solution)/shard_map/ppermute | solution.py:214
  15.9 5.2 %collective-permute-done.xa = f32[1,15,32,128]{3,2,1,0:T(8,128)S(1)} collective-permute-done((f32[1,15,32,128]{3,2,1,0:T(8,128)S(1)}, f32[1,15,32,128]{3,2,1,0:T(8,128)S(1)}, u32[]{:S(2)}, u32[]{:S(2)}) %collective-permute-start) | collective-permute-done | bytes 245792 | tf_op jit(solution)/shard_map/ppermute | solution.py:214
  21.1 0.0 collective-permute-done.1.xb
  21.1 0.6 shard_map.55
  21.7 1.3 %collective-permute-start.2 = (f32[1,46,16,128]{3,2,1,0:T(8,128)S(1)}, f32[1,46,16,128]{3,2,1,0:T(8,128)S(1)}, u32[]{:S(2)}, u32[]{:S(2)}) collective-permute-start(f32[1,46,16,128]{3,2,1,0:T(8,128)S(1)} %get-tuple-element.29), channel_id=1, source_target_pairs={{0,1},{1,0},{2,3},{3,2},{4,5},{5,4},{6,7},{7,6},{8,9},{9,8},{10,11... | collective-permute-start | bytes 1130504 | tf_op jit(solution)/shard_map/ppermute | solution.py:214
  23.0 3.1 %collective-permute-start.3 = (f32[1,46,16,128]{3,2,1,0:T(8,128)S(1)}, f32[1,46,16,128]{3,2,1,0:T(8,128)S(1)}, u32[]{:S(2)}, u32[]{:S(2)}) collective-permute-start(f32[1,46,16,128]{3,2,1,0:T(8,128)S(1)} %get-tuple-element.30), channel_id=1, source_target_pairs={{1,2},{2,1},{3,4},{4,3},{5,6},{6,5},{9,10},{10,9},{11,12},{12,11},... | collective-permute-start | bytes 1130504 | tf_op jit(solution)/shard_map/ppermute | solution.py:214
  26.1 0.0 collective-permute-done.5
  26.2 0.1 collective-permute-start.6
  26.2 0.0 copy-done.2
  26.2 2.3 %shard_map.56 = (bf16[48,144]{1,0:T(8,128)(2,1)S(1)}, bf16[48,144]{1,0:T(8,128)(2,1)S(1)}, bf16[3,32,192]{2,1,0:T(8,128)(2,1)S(1)}, bf16[3,64,96]{2,1,0:T(8,128)...) custom-call(f32[3,3,31]{2,1,0:T(4,128)S(1)} %copy-done.2, s32[2]{0:T(128)S(1)} %pad_add_fusion.parity.refs_0_), custom_call_target="tpu_custom_call" | custom-call | tf_op jit(solution)/shard_map/pallas_call | solution.py:93
  28.6 4.2 %collective-permute-done.6 = f32[3,1,32,128]{3,2,0,1:T(8,128)S(1)} collective-permute-done((f32[3,1,32,128]{3,2,0,1:T(8,128)S(1)}, f32[3,1,32,128]{3,2,0,1:T(8,128)S(1)}, u32[]{:S(2)}, u32[]{:S(2)}) %collective-permute-start.6) | collective-permute-done | bytes 49184 | tf_op jit(solution)/shard_map/ppermute | solution.py:230
  32.7 0.0 collective-permute-done.13.yc
  32.8 0.0 collective-permute-done.14.yd
  32.8 0.0 copy-done.1
  32.8 2.6 %shard_map.60 = (f32[1,16,32,128]{3,2,1,0:T(8,128)S(1)}, f32[1,15,32,128]{3,2,1,0:T(8,128)S(1)}, f32[1,15,32,128]{3,2,1,0:T(8,128)S(1)}, f32[1,46,16,128]{3,2,1,0:T(8,128)S(1)}, f32[1,46,16,128]{3,2,1,0:T(8,128)S(1)}) custom-call(f32[2,16,32,128]{3,2,1,0:T(8,128)S(1)} %copy-done, f32[1,15,32,128]{3,2,1,0:T(8,128)S(1)} %collective-permute-done.11.xa, ...), custom_call_target="tpu_custom_call" | custom-call | tf_op jit(solution)/shard_map/pallas_call | solution.py:190
  35.3 2.0 %collective-permute-start.15 = (f32[1,46,16,128]{3,2,1,0:T(8,128)S(1)}, f32[1,46,16,128]{3,2,1,0:T(8,128)S(1)}, u32[]{:S(2)}, u32[]{:S(2)}) collective-permute-start(f32[1,46,16,128]{3,2,1,0:T(8,128)S(1)} %get-tuple-element.47), channel_id=1, source_target_pairs={{0,1},{1,0},{2,3},{3,2},{4,5},{5,4},{6,7},{7,6},{8,9},{9,8},{10,11... | collective-permute-start | bytes 1130504 | tf_op jit(solution)/shard_map/ppermute | solution.py:214
  37.4 1.9 %collective-permute-start.16 = (f32[1,46,16,128]{3,2,1,0:T(8,128)S(1)}, f32[1,46,16,128]{3,2,1,0:T(8,128)S(1)}, u32[]{:S(2)}, u32[]{:S(2)}) collective-permute-start(f32[1,46,16,128]{3,2,1,0:T(8,128)S(1)} %get-tuple-element.48), channel_id=1, source_target_pairs={{1,2},{2,1},{3,4},{4,3},{5,6},{6,5},{9,10},{10,9},{11,12},{12,11},... | collective-permute-start | bytes 1130504 | tf_op jit(solution)/shard_map/ppermute | solution.py:214
  39.3 0.0 collective-permute-done.2.yc
  39.3 0.0 collective-permute-done.3.yd
  39.3 2.6 %shard_map.57 = (f32[1,16,32,128]{3,2,1,0:T(8,128)S(1)}, f32[1,15,32,128]{3,2,1,0:T(8,128)S(1)}, f32[1,15,32,128]{3,2,1,0:T(8,128)S(1)}, f32[1,46,16,128]{3,2,1,0:T(8,128)S(1)}, f32[1,46,16,128]{3,2,1,0:T(8,128)S(1)}) custom-call(f32[2,16,32,128]{3,2,1,0:T(8,128)S(1)} %copy-done, f32[1,15,32,128]{3,2,1,0:T(8,128)S(1)} %collective-permute-done.xa, ...), custom_call_target="tpu_custom_call" | custom-call | tf_op jit(solution)/shard_map/pallas_call | solution.py:190
  41.9 1.1 %collective-permute-start.7 = (f32[1,46,16,128]{3,2,1,0:T(8,128)S(1)}, f32[1,46,16,128]{3,2,1,0:T(8,128)S(1)}, u32[]{:S(2)}, u32[]{:S(2)}) collective-permute-start(f32[1,46,16,128]{3,2,1,0:T(8,128)S(1)} %get-tuple-element.38), channel_id=1, source_target_pairs={{0,1},{1,0},{2,3},{3,2},{4,5},{5,4},{6,7},{7,6},{8,9},{9,8},{10,11... | collective-permute-start | bytes 1130504 | tf_op jit(solution)/shard_map/ppermute | solution.py:214
  43.0 2.7 %collective-permute-start.8 = (f32[1,46,16,128]{3,2,1,0:T(8,128)S(1)}, f32[1,46,16,128]{3,2,1,0:T(8,128)S(1)}, u32[]{:S(2)}, u32[]{:S(2)}) collective-permute-start(f32[1,46,16,128]{3,2,1,0:T(8,128)S(1)} %get-tuple-element.39), channel_id=1, source_target_pairs={{1,2},{2,1},{3,4},{4,3},{5,6},{6,5},{9,10},{10,9},{11,12},{12,11},... | collective-permute-start | bytes 1130504 | tf_op jit(solution)/shard_map/ppermute | solution.py:214
  45.7 0.0 collective-permute-done.15.rc.refs_3_
  45.7 0.5 collective-permute-done.16.rd.refs_4_
  46.3 0.6 shard_map.61
  46.9 7.1 %collective-permute-start.17 = (f32[1,15,32,128]{3,2,1,0:T(8,128)S(1)}, f32[1,15,32,128]{3,2,1,0:T(8,128)S(1)}, u32[]{:S(2)}, u32[]{:S(2)}) collective-permute-start(f32[1,15,32,128]{3,2,1,0:T(8,128)S(1)} %get-tuple-element.51), channel_id=1, source_target_pairs={{0,8},{8,0},{16,24},{24,16},{1,9},{9,1},{17,25},{25,17},{2,10},{10... | collective-permute-start | bytes 737288 | tf_op jit(solution)/shard_map/ppermute | solution.py:214
  54.0 0.7 collective-permute-start.18
  54.7 0.0 collective-permute-done.7.rc.refs_3_
  54.7 0.0 collective-permute-done.8.rd.refs_4_
  54.7 0.6 shard_map.58
  55.3 0.7 collective-permute-start.10
  56.0 6.0 %collective-permute-start.9 = (f32[1,15,32,128]{3,2,1,0:T(8,128)S(1)}, f32[1,15,32,128]{3,2,1,0:T(8,128)S(1)}, u32[]{:S(2)}, u32[]{:S(2)}) collective-permute-start(f32[1,15,32,128]{3,2,1,0:T(8,128)S(1)} %get-tuple-element.42), channel_id=1, source_target_pairs={{0,8},{8,0},{16,24},{24,16},{1,9},{9,1},{17,25},{25,17},{2,10},{10... | collective-permute-start | bytes 737288 | tf_op jit(solution)/shard_map/ppermute | solution.py:214
  62.0 0.0 collective-permute-done.17.refs_5_
  62.0 0.0 collective-permute-done.18.refs_6_
  62.0 1.4 %shard_map.62.refs_7_ = f32[2,16,32,128]{3,2,1,0:T(8,128)} custom-call(s32[2]{0:T(128)S(1)} %pad_add_fusion.parity.refs_0_, f32[2,16,32,128]{3,2,1,0:T(8,128)S(1)} %copy-done, f32[1,16,32,128]{3,2,1,0:T(8,128)S(1)} %get-tuple-element.46.refs_2_, f32[1,46,16,128]{3,2,1,0:T(8,128)S(1)} %collective-permute-done.15.rc.refs_3_, ...), custom_call_target="tpu_custom_call" | custom-call | tf_op jit(solution)/shard_map/pallas_call | solution.py:317
  63.4 0.0 collective-permute-done.10.refs_6_
  63.4 12.7 %collective-permute-done.9.refs_5_ = f32[1,15,32,128]{3,2,1,0:T(8,128)S(1)} collective-permute-done((f32[1,15,32,128]{3,2,1,0:T(8,128)S(1)}, f32[1,15,32,128]{3,2,1,0:T(8,128)S(1)}, u32[]{:S(2)}, u32[]{:S(2)}) %collective-permute-start.9) | collective-permute-done | bytes 245792 | tf_op jit(solution)/shard_map/ppermute | solution.py:214
  76.1 1.4 %shard_map.63 = f32[2,16,32,128]{3,2,1,0:T(8,128)} custom-call(s32[2]{0:T(128)S(1)} %pad_add_fusion.parity.refs_0_, f32[2,16,32,128]{3,2,1,0:T(8,128)S(1)} %copy-done, f32[1,16,32,128]{3,2,1,0:T(8,128)S(1)} %get-tuple-element.37.refs_2_, f32[1,46,16,128]{3,2,1,0:T(8,128)S(1)} %collective-permute-done.7.rc.refs_3_, ...), custom_call_target="tpu_custom_call", output_to_operand_aliasing={{}: (7, {})} | custom-call | tf_op jit(solution)/shard_map/pallas_call | solution.py:317
  (10 shorter events, 0.3 us)
Async XLA Ops:
  0.0 2.8 %copy-start = (f32[2,16,32,128]{3,2,1,0:T(8,128)S(1)}, f32[2,16,32,128]{3,2,1,0:T(8,128)}, u32[]{:S(2)}) copy-start(f32[2,16,32,128]{3,2,1,0:T(8,128)} %refs_1_.3) | copy-start | bytes 1572868
  2.1 7.3 %collective-permute-start.4 = (f32[3,4,32,128]{3,2,1,0:T(8,128)S(1)}, f32[3,4,32,128]{3,2,1,0:T(8,128)S(1)}, u32[]{:S(2)}, u32[]{:S(2)}) collective-permute-start(f32[3,4,32,128]{3,2,1,0:T(8,128)S(1)} %select_bitcast_fusion), channel_id=1, source_target_pairs={{0,1},{1,0},{2,3},{3,2},{4,5},{5,4},{6,7},{7,6},{8,9},{9,8},{10,11... | collective-permute-start | bytes 589832 | tf_op jit(solution)/shard_map/ppermute | solution.py:230
  2.9 7.6 %collective-permute-start.11 = (f32[1,15,32,128]{3,2,1,0:T(8,128)S(1)}, f32[1,15,32,128]{3,2,1,0:T(8,128)S(1)}, u32[]{:S(2)}, u32[]{:S(2)}) collective-permute-start(f32[1,15,32,128]{3,2,1,0:T(8,128)S(1)} %get-tuple-element.56), channel_id=1, source_target_pairs={{0,8},{8,0},{16,24},{24,16},{1,9},{9,1},{17,25},{25,17},{2,10},{10... | collective-permute-start | bytes 737288 | tf_op jit(solution)/shard_map/ppermute | solution.py:214
  4.2 6.3 %collective-permute-start.12 = (f32[1,15,32,128]{3,2,1,0:T(8,128)S(1)}, f32[1,15,32,128]{3,2,1,0:T(8,128)S(1)}, u32[]{:S(2)}, u32[]{:S(2)}) collective-permute-start(f32[1,15,32,128]{3,2,1,0:T(8,128)S(1)} %get-tuple-element.55), channel_id=1, source_target_pairs={{8,16},{16,8},{9,17},{17,9},{10,18},{18,10},{11,19},{19,11},{12,20... | collective-permute-start | bytes 737288 | tf_op jit(solution)/shard_map/ppermute | solution.py:214
  4.9 16.1 %collective-permute-start = (f32[1,15,32,128]{3,2,1,0:T(8,128)S(1)}, f32[1,15,32,128]{3,2,1,0:T(8,128)S(1)}, u32[]{:S(2)}, u32[]{:S(2)}) collective-permute-start(f32[1,15,32,128]{3,2,1,0:T(8,128)S(1)} %get-tuple-element.58), channel_id=1, source_target_pairs={{0,8},{8,0},{16,24},{24,16},{1,9},{9,1},{17,25},{25,17},{2,10},{10... | collective-permute-start | bytes 737288 | tf_op jit(solution)/shard_map/ppermute | solution.py:214
  8.6 12.4 %collective-permute-start.1 = (f32[1,15,32,128]{3,2,1,0:T(8,128)S(1)}, f32[1,15,32,128]{3,2,1,0:T(8,128)S(1)}, u32[]{:S(2)}, u32[]{:S(2)}) collective-permute-start(f32[1,15,32,128]{3,2,1,0:T(8,128)S(1)} %get-tuple-element.57), channel_id=1, source_target_pairs={{8,16},{16,8},{9,17},{17,9},{10,18},{18,10},{11,19},{19,11},{12,20... | collective-permute-start | bytes 737288 | tf_op jit(solution)/shard_map/ppermute | solution.py:214
  9.4 16.8 %copy-start.2 = (f32[3,3,31]{2,1,0:T(4,128)S(1)}, f32[3,3,31]{2,1,0:T(4,128)}, u32[]{:S(2)}) copy-start(f32[3,3,31]{2,1,0:T(4,128)} %taps.1) | copy-start | bytes 3352
  9.5 23.3 %copy-start.1 = (f32[3,2,16,32,128]{4,3,2,1,0:T(8,128)S(1)}, f32[3,2,16,32,128]{4,3,2,1,0:T(8,128)}, u32[]{:S(2)}) copy-start(f32[3,2,16,32,128]{4,3,2,1,0:T(8,128)} %views.3) | copy-start | bytes 4718596
  9.5 16.6 %collective-permute-start.5 = (f32[3,2,32,128]{3,2,0,1:T(8,128)S(1)}, f32[3,2,32,128]{3,2,0,1:T(8,128)S(1)}, u32[]{:S(2)}, u32[]{:S(2)}) collective-permute-start(f32[3,2,32,128]{3,2,0,1:T(8,128)S(1)} %select_bitcast_fusion.1), channel_id=1, source_target_pairs={{0,2},{1,3},{2,0},{3,1},{4,6},{5,7},{6,4},{7,5},{8,10},{9,11},{10,... | collective-permute-start | bytes 294920 | tf_op jit(solution)/shard_map/ppermute | solution.py:230
  11.1 21.6 %collective-permute-start.13 = (f32[1,46,16,128]{3,2,1,0:T(8,128)S(1)}, f32[1,46,16,128]{3,2,1,0:T(8,128)S(1)}, u32[]{:S(2)}, u32[]{:S(2)}) collective-permute-start(f32[1,46,16,128]{3,2,1,0:T(8,128)S(1)} %get-tuple-element.44), channel_id=1, source_target_pairs={{0,1},{1,0},{2,3},{3,2},{4,5},{5,4},{6,7},{7,6},{8,9},{9,8},{10,11... | collective-permute-start | bytes 1130504 | tf_op jit(solution)/shard_map/ppermute | solution.py:214
  12.5 20.3 %collective-permute-start.14 = (f32[1,46,16,128]{3,2,1,0:T(8,128)S(1)}, f32[1,46,16,128]{3,2,1,0:T(8,128)S(1)}, u32[]{:S(2)}, u32[]{:S(2)}) collective-permute-start(f32[1,46,16,128]{3,2,1,0:T(8,128)S(1)} %get-tuple-element.45), channel_id=1, source_target_pairs={{1,2},{2,1},{3,4},{4,3},{5,6},{6,5},{9,10},{10,9},{11,12},{12,11},... | collective-permute-start | bytes 1130504 | tf_op jit(solution)/shard_map/ppermute | solution.py:214
  21.7 17.6 %collective-permute-start.2 = (f32[1,46,16,128]{3,2,1,0:T(8,128)S(1)}, f32[1,46,16,128]{3,2,1,0:T(8,128)S(1)}, u32[]{:S(2)}, u32[]{:S(2)}) collective-permute-start(f32[1,46,16,128]{3,2,1,0:T(8,128)S(1)} %get-tuple-element.29), channel_id=1, source_target_pairs={{0,1},{1,0},{2,3},{3,2},{4,5},{5,4},{6,7},{7,6},{8,9},{9,8},{10,11... | collective-permute-start | bytes 1130504 | tf_op jit(solution)/shard_map/ppermute | solution.py:214
  23.0 16.3 %collective-permute-start.3 = (f32[1,46,16,128]{3,2,1,0:T(8,128)S(1)}, f32[1,46,16,128]{3,2,1,0:T(8,128)S(1)}, u32[]{:S(2)}, u32[]{:S(2)}) collective-permute-start(f32[1,46,16,128]{3,2,1,0:T(8,128)S(1)} %get-tuple-element.30), channel_id=1, source_target_pairs={{1,2},{2,1},{3,4},{4,3},{5,6},{6,5},{9,10},{10,9},{11,12},{12,11},... | collective-permute-start | bytes 1130504 | tf_op jit(solution)/shard_map/ppermute | solution.py:214
  26.2 6.6 %collective-permute-start.6 = (f32[3,1,32,128]{3,2,0,1:T(8,128)S(1)}, f32[3,1,32,128]{3,2,0,1:T(8,128)S(1)}, u32[]{:S(2)}, u32[]{:S(2)}) collective-permute-start(f32[3,1,32,128]{3,2,0,1:T(8,128)S(1)} %select_bitcast_fusion.2), channel_id=1, source_target_pairs={{0,4},{1,5},{2,6},{3,7},{4,0},{5,1},{6,2},{7,3},{8,12},{9,13},{10,... | collective-permute-start | bytes 147464 | tf_op jit(solution)/shard_map/ppermute | solution.py:230
  35.3 10.4 %collective-permute-start.15 = (f32[1,46,16,128]{3,2,1,0:T(8,128)S(1)}, f32[1,46,16,128]{3,2,1,0:T(8,128)S(1)}, u32[]{:S(2)}, u32[]{:S(2)}) collective-permute-start(f32[1,46,16,128]{3,2,1,0:T(8,128)S(1)} %get-tuple-element.47), channel_id=1, source_target_pairs={{0,1},{1,0},{2,3},{3,2},{4,5},{5,4},{6,7},{7,6},{8,9},{9,8},{10,11... | collective-permute-start | bytes 1130504 | tf_op jit(solution)/shard_map/ppermute | solution.py:214
  37.4 8.9 %collective-permute-start.16 = (f32[1,46,16,128]{3,2,1,0:T(8,128)S(1)}, f32[1,46,16,128]{3,2,1,0:T(8,128)S(1)}, u32[]{:S(2)}, u32[]{:S(2)}) collective-permute-start(f32[1,46,16,128]{3,2,1,0:T(8,128)S(1)} %get-tuple-element.48), channel_id=1, source_target_pairs={{1,2},{2,1},{3,4},{4,3},{5,6},{6,5},{9,10},{10,9},{11,12},{12,11},... | collective-permute-start | bytes 1130504 | tf_op jit(solution)/shard_map/ppermute | solution.py:214
  41.9 12.8 %collective-permute-start.7 = (f32[1,46,16,128]{3,2,1,0:T(8,128)S(1)}, f32[1,46,16,128]{3,2,1,0:T(8,128)S(1)}, u32[]{:S(2)}, u32[]{:S(2)}) collective-permute-start(f32[1,46,16,128]{3,2,1,0:T(8,128)S(1)} %get-tuple-element.38), channel_id=1, source_target_pairs={{0,1},{1,0},{2,3},{3,2},{4,5},{5,4},{6,7},{7,6},{8,9},{9,8},{10,11... | collective-permute-start | bytes 1130504 | tf_op jit(solution)/shard_map/ppermute | solution.py:214
  43.0 11.7 %collective-permute-start.8 = (f32[1,46,16,128]{3,2,1,0:T(8,128)S(1)}, f32[1,46,16,128]{3,2,1,0:T(8,128)S(1)}, u32[]{:S(2)}, u32[]{:S(2)}) collective-permute-start(f32[1,46,16,128]{3,2,1,0:T(8,128)S(1)} %get-tuple-element.39), channel_id=1, source_target_pairs={{1,2},{2,1},{3,4},{4,3},{5,6},{6,5},{9,10},{10,9},{11,12},{12,11},... | collective-permute-start | bytes 1130504 | tf_op jit(solution)/shard_map/ppermute | solution.py:214
  46.9 15.1 %collective-permute-start.17 = (f32[1,15,32,128]{3,2,1,0:T(8,128)S(1)}, f32[1,15,32,128]{3,2,1,0:T(8,128)S(1)}, u32[]{:S(2)}, u32[]{:S(2)}) collective-permute-start(f32[1,15,32,128]{3,2,1,0:T(8,128)S(1)} %get-tuple-element.51), channel_id=1, source_target_pairs={{0,8},{8,0},{16,24},{24,16},{1,9},{9,1},{17,25},{25,17},{2,10},{10... | collective-permute-start | bytes 737288 | tf_op jit(solution)/shard_map/ppermute | solution.py:214
  54.0 8.0 %collective-permute-start.18 = (f32[1,15,32,128]{3,2,1,0:T(8,128)S(1)}, f32[1,15,32,128]{3,2,1,0:T(8,128)S(1)}, u32[]{:S(2)}, u32[]{:S(2)}) collective-permute-start(f32[1,15,32,128]{3,2,1,0:T(8,128)S(1)} %get-tuple-element.52), channel_id=1, source_target_pairs={{8,16},{16,8},{9,17},{17,9},{10,18},{18,10},{11,19},{19,11},{12,20... | collective-permute-start | bytes 737288 | tf_op jit(solution)/shard_map/ppermute | solution.py:214
  55.3 8.1 %collective-permute-start.10 = (f32[1,15,32,128]{3,2,1,0:T(8,128)S(1)}, f32[1,15,32,128]{3,2,1,0:T(8,128)S(1)}, u32[]{:S(2)}, u32[]{:S(2)}) collective-permute-start(f32[1,15,32,128]{3,2,1,0:T(8,128)S(1)} %get-tuple-element.43), channel_id=1, source_target_pairs={{8,16},{16,8},{9,17},{17,9},{10,18},{18,10},{11,19},{19,11},{12,20... | collective-permute-start | bytes 737288 | tf_op jit(solution)/shard_map/ppermute | solution.py:214
  56.0 20.1 %collective-permute-start.9 = (f32[1,15,32,128]{3,2,1,0:T(8,128)S(1)}, f32[1,15,32,128]{3,2,1,0:T(8,128)S(1)}, u32[]{:S(2)}, u32[]{:S(2)}) collective-permute-start(f32[1,15,32,128]{3,2,1,0:T(8,128)S(1)} %get-tuple-element.42), channel_id=1, source_target_pairs={{0,8},{8,0},{16,24},{24,16},{1,9},{9,1},{17,25},{25,17},{2,10},{10... | collective-permute-start | bytes 737288 | tf_op jit(solution)/shard_map/ppermute | solution.py:214

commit v2 on v1

--- a/solution.py
+++ b/solution.py
@@ -10,6 +10,7 @@
 F32 = jnp.float32
 BF16 = jnp.bfloat16
 SMALL = pltpu.CompilerParams(vmem_limit_bytes=8 * 1024 * 1024)
+FREE = pl.CostEstimate(flops=0, bytes_accessed=0, transcendentals=0)
 SKEW = 8
 PAD = 16
 
@@ -32,14 +33,14 @@
     return jnp.where(at < own, at, place)
 
 
-def matrices(taps, parity, x_blur, x_back, y_blur, y_back, z_blur, z_back):
+def matrices(taps, parity, _, x_blur, x_back, y_blur, y_back, z_blur, z_back):
     views, _, count = taps.shape
     half = count // 2
     planes = x_blur.shape[0] // views
     wide = x_back.shape[0]
     width, slab = y_blur.shape[1], y_back.shape[1]
     depth = z_blur.shape[1] // 2
-    odd_x, odd_y = parity[0] == 1, parity[1] == 1
+    odd_x, odd_y = parity[0] % 2 == 1, parity[1] % 2 == 1
 
     def pick(view, axis, offset):
         total = jnp.zeros(offset.shape, F32)
@@ -79,7 +80,7 @@
     x_back[...] = jnp.concatenate(highs + highs + lows, axis=1)
 
 
-def bands(kernels, parity, planes, width, depth):
+def bands(kernels, parity, planes, width, depth, after):
     views = kernels.shape[0]
     wide, slab = planes + 2 * PAD, width + 2 * PAD
     shapes = [
@@ -93,9 +94,10 @@
     return pl.pallas_call(
         matrices,
         out_shape=[jax.ShapeDtypeStruct(s, BF16) for s in shapes],
-        in_specs=[pl.BlockSpec(memory_space=pltpu.SMEM)] * 2,
+        in_specs=[pl.BlockSpec(memory_space=pltpu.SMEM)] * 2 + [LATER],
         compiler_params=SMALL,
-    )(kernels, parity)
+        name="matrices",
+    )(kernels, parity, after)
 
 
 def dot(left, right):
@@ -103,7 +105,7 @@
 
 
 def fused(
-    own, xa, xb, yc, yd, views, lights, x_blur, x_back, y_blur, y_back, z_blur, z_back,
+    own, xa, xb, yc, yd, views, light_kept, light_got, x_blur, x_back, y_blur, y_back, z_blur, z_back, _,
     s_own, s_xa, s_xb, s_yc, s_yd, ext, mid,
 ):
     count = views.shape[0]
@@ -154,7 +156,7 @@
     fields = [through(fields[view], z_blur[view]) for view in range(count)]
     ratios = []
     for view in range(count):
-        light = lights[view][None]
+        light = (light_kept[view] + light_got[view])[None]
         field = fields[view].reshape(planes, width, depth)
         ratio = light * views[view, 0] / (light * field + 0.05)
         ratios.append(ratio.reshape(planes * width, depth))
@@ -179,7 +181,7 @@
             s_yd[0, at + i] = ext[base + width + PAD : base + slab]
 
 
-def brick(channel, estimate, xa, xb, yc, yd, views, lights, mats):
+def brick(channel, estimate, xa, xb, yc, yd, views, lights, mats, after):
     count = views.shape[0]
     planes, width, depth = estimate.shape[1:]
     reach = xa.shape[1]
@@ -195,15 +197,15 @@
             pl.BlockSpec((1, planes, width, depth), lambda i: (channel, 0, 0, 0)),
             whole(xa), whole(xb), whole(yc), whole(yd),
             pl.BlockSpec((count, 1, planes, width, depth), lambda i: (0, channel, 0, 0, 0)),
-            whole(lights),
-        ] + [whole(m) for m in mats],
+        ] + [whole(m) for m in (*lights, *mats)] + [LATER],
         out_specs=[pl.BlockSpec(s, lambda i: (0,) * 4) for s in shapes],
         scratch_shapes=[
             pltpu.VMEM((wide * (slab + SKEW), depth), F32),
             pltpu.VMEM((count * planes * (slab + SKEW), depth), F32),
         ],
         compiler_params=pltpu.CompilerParams(vmem_limit_bytes=24 * 1024 * 1024),
-    )(estimate, xa, xb, yc, yd, views, lights, *mats)
+        name="brick%d" % channel,
+    )(estimate, xa, xb, yc, yd, views, *lights, *mats, after)
 
 
 def trade(value, axis, first):
@@ -214,106 +216,150 @@
     return lax.ppermute(value, axis, pairs)
 
 
-def illumination(profiles, owners, width):
-    row, col = lax.axis_index("bx"), lax.axis_index("by")
-    cols = lax.axis_size("by")
-    source = lax.dynamic_index_in_dim(owners, row, axis=1, keepdims=False)
-    count, _, depth = profiles.shape
-    held = jnp.where((source == col)[:, None, None], profiles, F32(0.0))
-    held = held.reshape(count, cols, width, depth)
-    step = 1
-    while step < cols:
-        held = held.reshape(count, held.shape[1] // 2, 2, width, depth)
-        odd = (col // step) % 2 == 1
-        kept = jnp.where(odd, held[:, :, 1], held[:, :, 0])
-        sent = jnp.where(odd, held[:, :, 0], held[:, :, 1])
-        held = kept + lax.ppermute(sent, "by", [(i, i ^ step) for i in range(cols)])
-        step *= 2
-    return held.reshape(count, width, depth)
-
-
 def whole(array):
-    return pl.BlockSpec(array.shape, lambda i: (0,) * array.ndim)
+    return pl.BlockSpec(array.shape, lambda i: (0,) * len(array.shape))
 
 
 SCALARS = pl.BlockSpec(memory_space=pltpu.SMEM)
+LATER = pl.BlockSpec(memory_space=pl.ANY)
 
 
 def one_channel(array, channel):
     return pl.BlockSpec((1,) + array.shape[1:], lambda i: (channel, 0, 0, 0))
 
 
-def row_starts(parity, width):
-    first = jnp.where(parity[1] == 1, 0, width - PAD)
-    second = jnp.where(parity[1] == 1, width - PAD, 0)
-    return tuple(pl.ds(pl.multiple_of(start, PAD), PAD) for start in (first, second))
-
-
-def rim_rows(parity, own, xa, xb, yc, yd):
-    planes, width, reach = own.shape[1], own.shape[2], xa.shape[1]
-    for out, rows in zip((yc, yd), row_starts(parity, width)):
-        out[0, :planes] = own[0, :, rows, :]
-        out[0, planes : planes + reach] = xa[0, :, rows, :]
-        out[0, planes + reach :] = xb[0, :, rows, :]
-
-
-def pack_rows(channel, parity, estimate, xa, xb):
-    _, planes, _, depth = estimate.shape
-    shape = (1, planes + 2 * xa.shape[1], PAD, depth)
-    return pl.pallas_call(
-        rim_rows,
+def call(body, name, ins, outs, deps=(), **more):
+    count = len(ins)
+
+    def kernel(*refs):
+        body(*refs[:count], *refs[count + len(deps) :])
+
+    out = pl.pallas_call(
+        kernel,
         grid=(1,),
-        out_shape=[jax.ShapeDtypeStruct(shape, F32)] * 2,
-        in_specs=[SCALARS, one_channel(estimate, channel), whole(xa), whole(xb)],
-        out_specs=[pl.BlockSpec(shape, lambda i: (0,) * 4)] * 2,
+        out_shape=[jax.ShapeDtypeStruct(s, F32) for s in outs],
+        in_specs=[spec for spec, _ in ins] + [LATER] * len(deps),
+        out_specs=[pl.BlockSpec(s, lambda i, n=len(s): (0,) * n) for s in outs],
         compiler_params=SMALL,
-    )(parity, estimate, xa, xb)
-
-
-def rim_planes(parity, s_xa, s_xb, rc, rd, out_a, out_b):
+        name=name,
+        **more,
+    )
+    return out(*[array for _, array in ins], *deps)
+
+
+def mask_profiles(cols, place, owners, profile, estimate, deps):
+    _, _, count, _, depth = profile.shape
+    width = estimate.shape[2]
+    shape = (count, cols // 2, width, depth)
+
+    def body(place, owners, profile, kept, sent):
+        bit = place[1] % 2
+        for view in range(count):
+            valid = owners[view, place[0]] == place[1]
+            for block in range(cols // 2):
+                for ref, side in ((kept, bit), (sent, 1 - bit)):
+                    start = pl.multiple_of((2 * block + side) * width, width)
+                    value = profile[0, 0, view, pl.ds(start, width), :]
+                    ref[view, block] = jnp.where(valid, value, 0.0)
+
+    return call(
+        body, "mask_profiles",
+        [(SCALARS, place), (SCALARS, owners), (whole(profile), profile)], [shape] * 2, deps,
+    )
+
+
+def halve_profiles(step, place, kept, got, deps):
+    count, blocks, width, depth = kept.shape
+    shape = (count, blocks // 2, width, depth)
+
+    def body(place, kept, got, out_kept, out_sent):
+        bit = place[1] // step % 2
+        for view in range(count):
+            for block in range(blocks // 2):
+                for ref, side in ((out_kept, bit), (out_sent, 1 - bit)):
+                    at = 2 * block + side
+                    ref[view, block] = kept[view, at] + got[view, at]
+
+    return call(
+        body, "halve_profiles%d" % step,
+        [(SCALARS, place), (whole(kept), kept), (whole(got), got)], [shape] * 2, deps,
+    )
+
+
+def pack_planes(place, estimate, reach):
+    channels, planes, width, depth = estimate.shape
+
+    def body(place, own, *outs):
+        odd = place[0] % 2
+        for channel in range(channels):
+            for out, side in zip(outs[2 * channel :], (1 - odd, odd)):
+                out[0] = own[channel, pl.ds((planes - reach) * side, reach)]
+
+    return call(
+        body, "pack_planes", [(SCALARS, place), (whole(estimate), estimate)],
+        [(1, reach, width, depth)] * (2 * channels),
+    )
+
+
+def row_starts(place, width):
+    odd = place[1] % 2
+    starts = ((width - PAD) * (1 - odd), (width - PAD) * odd)
+    return tuple(pl.ds(pl.multiple_of(start, PAD), PAD) for start in starts)
+
+
+def pack_rows(channel, place, estimate, xa, xb, deps):
+    _, planes, width, depth = estimate.shape
+    reach = xa.shape[1]
+
+    def body(place, own, xa, xb, first, second):
+        for out, rows in zip((first, second), row_starts(place, width)):
+            out[0, :planes] = own[0, :, rows, :]
+            out[0, planes : planes + reach] = xa[0, :, rows, :]
+            out[0, planes + reach :] = xb[0, :, rows, :]
+
+    return call(
+        body, "pack_rows%d" % channel,
+        [(SCALARS, place), (one_channel(estimate, channel), estimate), (whole(xa), xa), (whole(xb), xb)],
+        [(1, planes + 2 * reach, PAD, depth)] * 2, deps,
+    )
+
+
+def add_rows(channel, place, s_xa, s_xb, rc, rd, deps):
     reach, width = s_xa.shape[1:3]
     base = rc.shape[1] - 2 * reach
-    out_a[...] = s_xa[...]
-    out_b[...] = s_xb[...]
-    for got, rows in zip((rc, rd), row_starts(parity, width)):
-        out_a[0, :, rows, :] += got[0, base : base + reach]
-        out_b[0, :, rows, :] += got[0, base + reach :]
-
-
-def pack_planes(parity, s_xa, s_xb, rc, rd):
-    return pl.pallas_call(
-        rim_planes,
-        grid=(1,),
-        out_shape=[jax.ShapeDtypeStruct(s_xa.shape, F32)] * 2,
-        in_specs=[SCALARS, whole(s_xa), whole(s_xb), whole(rc), whole(rd)],
-        out_specs=[whole(s_xa)] * 2,
-        compiler_params=SMALL,
-    )(parity, s_xa, s_xb, rc, rd)
-
-
-def closing(parity, estimate, s_own, rc, rd, qa, qb, out, *, views):
+
+    def body(place, s_xa, s_xb, rc, rd, first, second):
+        first[...] = s_xa[...]
+        second[...] = s_xb[...]
+        for got, rows in zip((rc, rd), row_starts(place, width)):
+            first[0, :, rows, :] += got[0, base : base + reach]
+            second[0, :, rows, :] += got[0, base + reach :]
+
+    return call(
+        body, "add_rows%d" % channel,
+        [(SCALARS, place)] + [(whole(a), a) for a in (s_xa, s_xb, rc, rd)], [s_xa.shape] * 2, deps,
+    )
+
+
+def finish(channel, views, place, estimate, s_own, rc, rd, qa, qb, done, deps):
     planes, width = s_own.shape[1:3]
     reach = qa.shape[1]
-    out[...] = s_own[...]
-    for got, rows in zip((rc, rd), row_starts(parity, width)):
-        out[0, :, rows, :] += got[0, :planes]
-    first = jnp.where(parity[0] == 1, 0, planes - reach)
-    second = jnp.where(parity[0] == 1, planes - reach, 0)
-    out[0, pl.ds(first, reach)] += qa[0]
-    out[0, pl.ds(second, reach)] += qb[0]
-    out[...] = estimate[...] * out[...] / views
-
-
-def finish(channel, views, parity, estimate, s_own, rc, rd, qa, qb, done):
-    planes = s_own.shape[1]
 
     def own_planes(array):
         return pl.BlockSpec((1, planes) + array.shape[2:], lambda i: (0,) * 4)
 
-    def body(*refs):
-        closing(*refs[:7], refs[-1], views=views)
+    def body(place, estimate, s_own, rc, rd, qa, qb, *rest):
+        out = rest[-1]
+        out[...] = s_own[...]
+        for got, rows in zip((rc, rd), row_starts(place, width)):
+            out[0, :, rows, :] += got[0]
+        odd = place[0] % 2
+        out[0, pl.ds((planes - reach) * (1 - odd), reach)] += qa[0]
+        out[0, pl.ds((planes - reach) * odd, reach)] += qb[0]
+        out[...] = estimate[...] * out[...] / views
 
     more = [] if done is None else [done]
+    ins = [place, estimate, s_own, rc, rd, qa, qb] + more + list(deps)
     return pl.pallas_call(
         body,
         grid=(1,),
@@ -321,42 +367,64 @@
         in_specs=[
             SCALARS, one_channel(estimate, channel), whole(s_own), own_planes(rc), own_planes(rd),
             whole(qa), whole(qb),
-        ] + [pl.BlockSpec(memory_space=pl.ANY)] * len(more),
+        ] + [LATER] * (len(more) + len(deps)),
         out_specs=one_channel(estimate, channel),
+        input_output_aliases={7: 0} if more else {},
         compiler_params=SMALL,
-        input_output_aliases={7: 0} if more else {},
-    )(parity, estimate, s_own, rc, rd, qa, qb, *more)
+        name="finish%d" % channel,
+    )(*ins)
+
+
+def flip(value, axis, step):
+    return lax.ppermute(value, axis, [(i, i ^ step) for i in range(lax.axis_size(axis))])
 
 
 def shards(views, estimate, profiles, kernels, owners):
     channels, planes, width, depth = estimate.shape
     reach = kernels.shape[2] // 2
-    odd_x, odd_y = lax.axis_index("bx") % 2, lax.axis_index("by") % 2
-    parity = jnp.stack([odd_x, odd_y]).astype(jnp.int32)
-    x_first, x_second = (planes - reach) * (1 - odd_x), (planes - reach) * odd_x
+    cols = lax.axis_size("by")
+    place = jnp.stack([lax.axis_index("bx"), lax.axis_index("by")]).astype(jnp.int32)
+    odd = place[0] % 2
+    packed = []
+    for c in range(channels):
+        for side in (1 - odd, odd):
+            packed.append(lax.dynamic_slice_in_dim(estimate[c : c + 1], (planes - reach) * side, reach, axis=1))
     halo = []
     for c in range(channels):
-        mine = estimate[c : c + 1]
-        xa = trade(lax.dynamic_slice_in_dim(mine, x_first, reach, axis=1), "bx", True)
-        xb = trade(lax.dynamic_slice_in_dim(mine, x_second, reach, axis=1), "bx", False)
-        halo.append((xa, xb))
-    mats = bands(kernels, parity, planes, width, depth)
-    lights = illumination(profiles[0, 0], owners, width)
-    parts = []
+        xb = trade(packed[2 * c + 1], "bx", False)
+        halo.append((trade(packed[2 * c], "bx", True), xb))
+    kept, sent = mask_profiles(cols, place, owners, profiles, estimate, (packed[0],))
+    step, mats = 1, None
+    while True:
+        got = flip(sent, "by", step)
+        if mats is None:
+            mats = bands(kernels, place, planes, width, depth, sent)
+        step *= 2
+        if step == cols:
+            break
+        kept, sent = halve_profiles(step, place, kept, got, (mats[0],))
+    lights = (kept.reshape(-1, width, depth), got.reshape(-1, width, depth))
+    rims = []
     for c in range(channels):
         xa, xb = halo[c]
-        yc, yd = pack_rows(c, parity, estimate, xa, xb)
-        yc, yd = trade(yc, "by", True), trade(yd, "by", False)
-        parts.append(brick(c, estimate, xa, xb, yc, yd, views, lights, mats))
-    ends = []
+        yc, yd = pack_rows(c, place, estimate, xa, xb, (got,))
+        yd = trade(yd, "by", False)
+        rims.append((yc, trade(yc, "by", True), yd))
+    ends, sums, done, prev = [], kernels, None, ()
     for c in range(channels):
-        s_own, s_xa, s_xb, s_yc, s_yd = parts[c]
-        rc, rd = trade(s_yc, "by", True), trade(s_yd, "by", False)
-        qa, qb = pack_planes(parity, s_xa, s_xb, rc, rd)
-        ends.append((s_own, rc, rd, trade(qa, "bx", True), trade(qb, "bx", False)))
+        _, yc, yd = rims[c]
+        s_own, s_xa, s_xb, s_yc, s_yd = brick(c, estimate, *halo[c], yc, yd, views, lights, mats, sums)
+        rd = trade(s_yd, "by", False)
+        rc = trade(s_yc, "by", True)
+        first, second = add_rows(c, place, s_xa, s_xb, rc, rd, prev)
+        sums = kernels
+        qb = trade(second, "bx", False)
+        qa = trade(first, "bx", True)
+        prev = ()
+        ends.append((s_own, rc, rd, qa, qb))
     done = None
     for c in range(channels):
-        done = finish(c, views.shape[0], parity, estimate, *ends[c], done)
+        done = finish(c, views.shape[0], place, estimate, *ends[c], done, (sums,))
     return done
 
 

time: 77.8 us -> 72.6 us (0.933)
  the two profiles are of different devices: /device:TPU:9 before, /device:TPU:13 now
where the time goes in v2:
time: 72.6 us; the launch traced here: 72.2 us
  starting transfers between devices  35.5 us (49%)
  waiting for transfers between devices  20.6 us (28%)
  Pallas kernels  14.5 us (20%)
  local copies, waits for them, and re-layouts  1.21 us (2%)
    ppermute x16, starting transfers between devices, trade(): return lax.ppermute(value, axis, pairs)  31.9 us
    ppermute x16, waiting for transfers between devices, trade(): return lax.ppermute(value, axis, pairs)  14.9 us
    ppermute x3, waiting for transfers between devices, flip(): lax.ppermute(value, axis, [(i, i ^ step) for i in range(lax.axis_size(axi...  5.73 us
    pallas_call x2, Pallas kernels, brick(): pl.pallas_call(fused, grid=(1,), out_shape=[jax.ShapeDtypeStruct(s, F32)...  5.2 us
    pallas_call x7, Pallas kernels, call(): return out(*[array for _, array in ins], *deps)  4.24 us
    ppermute x3, starting transfers between devices, flip(): lax.ppermute(value, axis, [(i, i ^ step) for i in range(lax.axis_size(axi...  3.63 us
    pallas_call x2, Pallas kernels, finish(): pl.pallas_call(body, grid=(1,), out_shape=jax.ShapeDtypeStruct(estimate.s...  2.78 us
    pallas_call x1, Pallas kernels, bands(): pl.pallas_call(matrices, out_shape=[jax.ShapeDtypeStruct(s, BF16) for s i...  2.3 us
  transfers between devices with their start and end apart: 19, of which 7 were waited for; matrix products, arithmetic and copies ran while one was open for 0% of the time, Pallas kernels for 18%

profile of v2, /device:TPU:13, one launch (start us, length us, event | category | flops | bytes accessed | tf_op | source)
XLA Modules:
  0.0 72.2 jit_solution(10745119059625047005)
XLA Ops:
  0.0 0.0 copy-start.4
  0.0 0.0 copy-start.2
  0.0 1.1 %fusion = (f32[1,16,32,128]{3,2,1,0:T(8,128)S(1)}, f32[1,16,32,128]{3,2,1,0:T(8,128)S(1)}) fusion(f32[2,16,32,128]{3,2,1,0:T(8,128)} %estimate.3), kind=kLoop, calls=%fused_computation.5 | loop fusion | bytes 1048576 | tf_op jit(solution)/shard_map/slice | solution.py:391
  1.1 0.0 copy-start.3
  1.1 0.0 copy-start
  1.2 3.2 %collective-permute-start.12 = (f32[1,15,32,128]{3,2,1,0:T(8,128)S(1)}, f32[1,15,32,128]{3,2,1,0:T(8,128)S(1)}, u32[]{:S(2)}, u32[]{:S(2)}) collective-permute-start(f32[1,15,32,128]{3,2,1,0:T(8,128)S(1)} %get-tuple-element.67), channel_id=1, source_target_pairs={{8,16},{16,8},{9,17},{17,9},{10,18},{18,10},{11,19},{19,11},{12,20... | collective-permute-start | bytes 737288 | tf_op jit(solution)/shard_map/ppermute | solution.py:216
  4.4 0.1 collective-permute-start.11
  4.5 0.1 pad_add_fusion.refs_0_.parity.place
  4.6 0.0 copy-done.4
  4.6 0.0 copy-done.2
  4.6 0.6 mask_profiles.1
  5.2 1.0 %collective-permute-start.2 = (f32[3,4,32,128]{3,2,1,0:T(8,128)S(1)}, f32[3,4,32,128]{3,2,1,0:T(8,128)S(1)}, u32[]{:S(2)}, u32[]{:S(2)}) collective-permute-start(f32[3,4,32,128]{3,2,1,0:T(8,128)S(1)} %get-tuple-element.36._), channel_id=1, source_target_pairs={{0,1},{1,0},{2,3},{3,2},{4,5},{5,4},{6,7},{7,6},{8,9},{9,8},{10,11... | collective-permute-start | bytes 589832 | tf_op jit(solution)/shard_map/ppermute | solution.py:379
  6.3 0.0 copy-start.1
  6.3 3.3 %collective-permute-start.1 = (f32[1,15,32,128]{3,2,1,0:T(8,128)S(1)}, f32[1,15,32,128]{3,2,1,0:T(8,128)S(1)}, u32[]{:S(2)}, u32[]{:S(2)}) collective-permute-start(f32[1,15,32,128]{3,2,1,0:T(8,128)S(1)} %get-tuple-element.69), channel_id=1, source_target_pairs={{8,16},{16,8},{9,17},{17,9},{10,18},{18,10},{11,19},{19,11},{12,20... | collective-permute-start | bytes 737288 | tf_op jit(solution)/shard_map/ppermute | solution.py:216
  9.5 0.1 collective-permute-start
  9.6 0.0 copy-done.3
  9.6 2.3 %matrices.1 = (bf16[48,144]{1,0:T(8,128)(2,1)S(1)}, bf16[48,144]{1,0:T(8,128)(2,1)S(1)}, bf16[3,32,192]{2,1,0:T(8,128)(2,1)S(1)}, bf16[3,64,96]{2,1,0:T(8,128)(2...) custom-call(f32[3,3,31]{2,1,0:T(4,128)S(1)} %copy-done.3, ...), custom_call_target="tpu_custom_call" | custom-call | tf_op jit(solution)/shard_map/matrices/pallas_call | solution.py:94
  11.9 0.0 collective-permute-done.2.refs_2_
  12.0 0.6 halve_profiles2.1
  12.5 0.2 collective-permute-start.3
  12.8 3.9 %collective-permute-done.3.refs_2_ = f32[3,2,32,128]{3,2,1,0:T(8,128)S(1)} collective-permute-done((f32[3,2,32,128]{3,2,1,0:T(8,128)S(1)}, f32[3,2,32,128]{3,2,1,0:T(8,128)S(1)}, u32[]{:S(2)}, u32[]{:S(2)}) %collective-permute-start.3) | collective-permute-done | bytes 98336 | tf_op jit(solution)/shard_map/ppermute | solution.py:379
  16.7 0.6 halve_profiles4.1
  17.3 2.4 %collective-permute-start.4 = (f32[3,1,32,128]{3,2,0,1:T(8,128)S(1)}, f32[3,1,32,128]{3,2,0,1:T(8,128)S(1)}, u32[]{:S(2)}, u32[]{:S(2)}) collective-permute-start(f32[3,1,32,128]{3,2,0,1:T(8,128)S(1)} %bitcast.12), channel_id=1, source_target_pairs={{0,4},{1,5},{2,6},{3,7},{4,0},{5,1},{6,2},{7,3},{8,12},{9,13},{10,... | collective-permute-start | bytes 147464 | tf_op jit(solution)/shard_map/ppermute | solution.py:379
  19.6 0.0 collective-permute-done.12.refs_3_.xb
  19.6 0.0 collective-permute-done.11.refs_2_.xa
  19.6 1.8 %collective-permute-done.4 = f32[3,1,32,128]{3,2,0,1:T(8,128)S(1)} collective-permute-done((f32[3,1,32,128]{3,2,0,1:T(8,128)S(1)}, f32[3,1,32,128]{3,2,0,1:T(8,128)S(1)}, u32[]{:S(2)}, u32[]{:S(2)}) %collective-permute-start.4) | collective-permute-done | bytes 49184 | tf_op jit(solution)/shard_map/ppermute | solution.py:379
  21.5 0.0 copy-done
  21.5 0.6 pack_rows0.1
  22.1 2.0 %collective-permute-start.13 = (f32[1,46,16,128]{3,2,1,0:T(8,128)S(1)}, f32[1,46,16,128]{3,2,1,0:T(8,128)S(1)}, u32[]{:S(2)}, u32[]{:S(2)}) collective-permute-start(f32[1,46,16,128]{3,2,1,0:T(8,128)S(1)} %get-tuple-element.56), channel_id=1, source_target_pairs={{0,1},{1,0},{2,3},{3,2},{4,5},{5,4},{6,7},{7,6},{8,9},{9,8},{10,11... | collective-permute-start | bytes 1130504 | tf_op jit(solution)/shard_map/ppermute | solution.py:216
  24.1 3.1 %collective-permute-start.14 = (f32[1,46,16,128]{3,2,1,0:T(8,128)S(1)}, f32[1,46,16,128]{3,2,1,0:T(8,128)S(1)}, u32[]{:S(2)}, u32[]{:S(2)}) collective-permute-start(f32[1,46,16,128]{3,2,1,0:T(8,128)S(1)} %get-tuple-element.57), channel_id=1, source_target_pairs={{1,2},{2,1},{3,4},{4,3},{5,6},{6,5},{9,10},{10,9},{11,12},{12,11},... | collective-permute-start | bytes 1130504 | tf_op jit(solution)/shard_map/ppermute | solution.py:216
  27.3 0.0 collective-permute-done.1.refs_3_.xb
  27.3 0.0 collective-permute-done.refs_2_.xa
  27.3 0.6 pack_rows1.1
  27.9 0.1 collective-permute-start.5
  28.0 3.9 %collective-permute-start.6 = (f32[1,46,16,128]{3,2,1,0:T(8,128)S(1)}, f32[1,46,16,128]{3,2,1,0:T(8,128)S(1)}, u32[]{:S(2)}, u32[]{:S(2)}) collective-permute-start(f32[1,46,16,128]{3,2,1,0:T(8,128)S(1)} %get-tuple-element.42), channel_id=1, source_target_pairs={{1,2},{2,1},{3,4},{4,3},{5,6},{6,5},{9,10},{10,9},{11,12},{12,11},... | collective-permute-start | bytes 1130504 | tf_op jit(solution)/shard_map/ppermute | solution.py:216
  31.9 0.0 collective-permute-done.13.yc
  31.9 1.4 %collective-permute-done.14.yd = f32[1,46,16,128]{3,2,1,0:T(8,128)S(1)} collective-permute-done((f32[1,46,16,128]{3,2,1,0:T(8,128)S(1)}, f32[1,46,16,128]{3,2,1,0:T(8,128)S(1)}, u32[]{:S(2)}, u32[]{:S(2)}) %collective-permute-start.14) | collective-permute-done | bytes 376864 | tf_op jit(solution)/shard_map/ppermute | solution.py:216
  33.3 0.0 copy-done.1
  33.3 2.6 %brick0.1 = (f32[1,16,32,128]{3,2,1,0:T(8,128)S(1)}, f32[1,15,32,128]{3,2,1,0:T(8,128)S(1)}, f32[1,15,32,128]{3,2,1,0:T(8,128)S(1)}, f32[1,46,16,128]{3,2,1,0:T(8,128)S(1)}, f32[1,46,16,128]{3,2,1,0:T(8,128)S(1)}) custom-call(f32[2,16,32,128]{3,2,1,0:T(8,128)S(1)} %copy-done, f32[1,15,32,128]{3,2,1,0:T(8,128)S(1)} %collective-permute-done.11.refs_2_.xa, ...), custom_call_target="tpu_custom_call" | custom-call | tf_op jit(solution)/shard_map/brick0/pallas_call | solution.py:192
  35.9 0.1 collective-permute-start.15
  36.0 3.6 %collective-permute-start.16 = (f32[1,46,16,128]{3,2,1,0:T(8,128)S(1)}, f32[1,46,16,128]{3,2,1,0:T(8,128)S(1)}, u32[]{:S(2)}, u32[]{:S(2)}) collective-permute-start(f32[1,46,16,128]{3,2,1,0:T(8,128)S(1)} %get-tuple-element.60), channel_id=1, source_target_pairs={{1,2},{2,1},{3,4},{4,3},{5,6},{6,5},{9,10},{10,9},{11,12},{12,11},... | collective-permute-start | bytes 1130504 | tf_op jit(solution)/shard_map/ppermute | solution.py:216
  39.6 0.0 collective-permute-done.5.yc
  39.6 0.0 collective-permute-done.6.yd
  39.6 2.6 %brick1.1 = (f32[1,16,32,128]{3,2,1,0:T(8,128)S(1)}, f32[1,15,32,128]{3,2,1,0:T(8,128)S(1)}, f32[1,15,32,128]{3,2,1,0:T(8,128)S(1)}, f32[1,46,16,128]{3,2,1,0:T(8,128)S(1)}, f32[1,46,16,128]{3,2,1,0:T(8,128)S(1)}) custom-call(f32[2,16,32,128]{3,2,1,0:T(8,128)S(1)} %copy-done, f32[1,15,32,128]{3,2,1,0:T(8,128)S(1)} %collective-permute-done.refs_2_.xa, ...), custom_call_target="tpu_custom_call" | custom-call | tf_op jit(solution)/shard_map/brick1/pallas_call | solution.py:192
  42.3 0.1 collective-permute-start.7
  42.3 3.2 %collective-permute-start.8 = (f32[1,46,16,128]{3,2,1,0:T(8,128)S(1)}, f32[1,46,16,128]{3,2,1,0:T(8,128)S(1)}, u32[]{:S(2)}, u32[]{:S(2)}) collective-permute-start(f32[1,46,16,128]{3,2,1,0:T(8,128)S(1)} %get-tuple-element.51), channel_id=1, source_target_pairs={{1,2},{2,1},{3,4},{4,3},{5,6},{6,5},{9,10},{10,9},{11,12},{12,11},... | collective-permute-start | bytes 1130504 | tf_op jit(solution)/shard_map/ppermute | solution.py:216
  45.5 0.0 collective-permute-done.15.refs_3_.rc
  45.5 0.0 collective-permute-done.16.refs_4_.rd
  45.5 0.6 add_rows0.1
  46.2 1.5 %collective-permute-start.17 = (f32[1,15,32,128]{3,2,1,0:T(8,128)S(1)}, f32[1,15,32,128]{3,2,1,0:T(8,128)S(1)}, u32[]{:S(2)}, u32[]{:S(2)}) collective-permute-start(f32[1,15,32,128]{3,2,1,0:T(8,128)S(1)} %get-tuple-element.63), channel_id=1, source_target_pairs={{0,8},{8,0},{16,24},{24,16},{1,9},{9,1},{17,25},{25,17},{2,10},{10... | collective-permute-start | bytes 737288 | tf_op jit(solution)/shard_map/ppermute | solution.py:216
  47.7 3.0 %collective-permute-start.18 = (f32[1,15,32,128]{3,2,1,0:T(8,128)S(1)}, f32[1,15,32,128]{3,2,1,0:T(8,128)S(1)}, u32[]{:S(2)}, u32[]{:S(2)}) collective-permute-start(f32[1,15,32,128]{3,2,1,0:T(8,128)S(1)} %get-tuple-element.64), channel_id=1, source_target_pairs={{8,16},{16,8},{9,17},{17,9},{10,18},{18,10},{11,19},{19,11},{12,20... | collective-permute-start | bytes 737288 | tf_op jit(solution)/shard_map/ppermute | solution.py:216
  50.7 0.0 collective-permute-done.7.refs_3_.rc
  50.8 0.8 %collective-permute-done.8.refs_4_.rd = f32[1,46,16,128]{3,2,1,0:T(8,128)S(1)} collective-permute-done((f32[1,46,16,128]{3,2,1,0:T(8,128)S(1)}, f32[1,46,16,128]{3,2,1,0:T(8,128)S(1)}, u32[]{:S(2)}, u32[]{:S(2)}) %collective-permute-start.8) | collective-permute-done | bytes 376864 | tf_op jit(solution)/shard_map/ppermute | solution.py:216
  51.6 0.6 add_rows1.1
  52.2 1.5 %collective-permute-start.9 = (f32[1,15,32,128]{3,2,1,0:T(8,128)S(1)}, f32[1,15,32,128]{3,2,1,0:T(8,128)S(1)}, u32[]{:S(2)}, u32[]{:S(2)}) collective-permute-start(f32[1,15,32,128]{3,2,1,0:T(8,128)S(1)} %get-tuple-element.54), channel_id=1, source_target_pairs={{0,8},{8,0},{16,24},{24,16},{1,9},{9,1},{17,25},{25,17},{2,10},{10... | collective-permute-start | bytes 737288 | tf_op jit(solution)/shard_map/ppermute | solution.py:216
  53.7 3.0 %collective-permute-start.10 = (f32[1,15,32,128]{3,2,1,0:T(8,128)S(1)}, f32[1,15,32,128]{3,2,1,0:T(8,128)S(1)}, u32[]{:S(2)}, u32[]{:S(2)}) collective-permute-start(f32[1,15,32,128]{3,2,1,0:T(8,128)S(1)} %get-tuple-element.55), channel_id=1, source_target_pairs={{8,16},{16,8},{9,17},{17,9},{10,18},{18,10},{11,19},{19,11},{12,20... | collective-permute-start | bytes 737288 | tf_op jit(solution)/shard_map/ppermute | solution.py:216
  56.7 0.0 collective-permute-done.17.qa
  56.8 3.5 %collective-permute-done.18.qb = f32[1,15,32,128]{3,2,1,0:T(8,128)S(1)} collective-permute-done((f32[1,15,32,128]{3,2,1,0:T(8,128)S(1)}, f32[1,15,32,128]{3,2,1,0:T(8,128)S(1)}, u32[]{:S(2)}, u32[]{:S(2)}) %collective-permute-start.18) | collective-permute-done | bytes 245792 | tf_op jit(solution)/shard_map/ppermute | solution.py:216
  60.3 1.4 %finish0.1.rest_0_ = f32[2,16,32,128]{3,2,1,0:T(8,128)} custom-call(s32[2]{0:T(128)S(1)} %pad_add_fusion.refs_0_.parity.place, f32[2,16,32,128]{3,2,1,0:T(8,128)S(1)} %copy-done, f32[1,16,32,128]{3,2,1,0:T(8,128)S(1)} %get-tuple-element.58.s_own, f32[1,46,16,128]{3,2,1,0:T(8,128)S(1)} %collective-permute-done.15.refs_3_.rc, ...), custom_call_target="tpu_custom_call" | custom-call | tf_op jit(solution)/shard_map/finish0/pallas_call | solution.py:363
  61.7 2.0 %collective-permute-done.9.qa = f32[1,15,32,128]{3,2,1,0:T(8,128)S(1)} collective-permute-done((f32[1,15,32,128]{3,2,1,0:T(8,128)S(1)}, f32[1,15,32,128]{3,2,1,0:T(8,128)S(1)}, u32[]{:S(2)}, u32[]{:S(2)}) %collective-permute-start.9) | collective-permute-done | bytes 245792 | tf_op jit(solution)/shard_map/ppermute | solution.py:216
  63.7 7.2 %collective-permute-done.10.qb = f32[1,15,32,128]{3,2,1,0:T(8,128)S(1)} collective-permute-done((f32[1,15,32,128]{3,2,1,0:T(8,128)S(1)}, f32[1,15,32,128]{3,2,1,0:T(8,128)S(1)}, u32[]{:S(2)}, u32[]{:S(2)}) %collective-permute-start.10) | collective-permute-done | bytes 245792 | tf_op jit(solution)/shard_map/ppermute | solution.py:216
  70.8 1.4 %finish1.1 = f32[2,16,32,128]{3,2,1,0:T(8,128)} custom-call(s32[2]{0:T(128)S(1)} %pad_add_fusion.refs_0_.parity.place, f32[2,16,32,128]{3,2,1,0:T(8,128)S(1)} %copy-done, f32[1,16,32,128]{3,2,1,0:T(8,128)S(1)} %get-tuple-element.49.s_own, f32[1,46,16,128]{3,2,1,0:T(8,128)S(1)} %collective-permute-done.7.refs_3_.rc, ...), custom_call_target="tpu_custom_call", output_to_operand_aliasing={{}: (7, {})} | custom-call | tf_op jit(solution)/shard_map/finish1/pallas_call | solution.py:363
  (2 shorter events, 0.1 us)
Async XLA Ops:
  0.0 4.6 %copy-start.4 = (s32[3,4]{1,0:T(4,128)S(1)}, s32[3,4]{1,0:T(4,128)}, u32[]{:S(2)}) copy-start(s32[3,4]{1,0:T(4,128)} %refs_1_.3) | copy-start | bytes 148
  0.0 4.6 %copy-start.2 = (f32[1,1,3,256,128]{4,3,2,1,0:T(8,128)S(1)}, f32[1,1,3,256,128]{4,3,2,1,0:T(8,128)}, u32[]{:S(2)}) copy-start(f32[1,1,3,256,128]{4,3,2,1,0:T(8,128)} %refs_2_.1) | copy-start | bytes 1179652
  1.1 8.5 %copy-start.3 = (f32[3,3,31]{2,1,0:T(4,128)S(1)}, f32[3,3,31]{2,1,0:T(4,128)}, u32[]{:S(2)}) copy-start(f32[3,3,31]{2,1,0:T(4,128)} %rest_1_.1) | copy-start | bytes 3352
  1.1 20.3 %copy-start = (f32[2,16,32,128]{3,2,1,0:T(8,128)S(1)}, f32[2,16,32,128]{3,2,1,0:T(8,128)}, u32[]{:S(2)}) copy-start(f32[2,16,32,128]{3,2,1,0:T(8,128)} %estimate.3) | copy-start | bytes 1572868
  1.2 18.4 %collective-permute-start.12 = (f32[1,15,32,128]{3,2,1,0:T(8,128)S(1)}, f32[1,15,32,128]{3,2,1,0:T(8,128)S(1)}, u32[]{:S(2)}, u32[]{:S(2)}) collective-permute-start(f32[1,15,32,128]{3,2,1,0:T(8,128)S(1)} %get-tuple-element.67), channel_id=1, source_target_pairs={{8,16},{16,8},{9,17},{17,9},{10,18},{18,10},{11,19},{19,11},{12,20... | collective-permute-start | bytes 737288 | tf_op jit(solution)/shard_map/ppermute | solution.py:216
  4.4 15.2 %collective-permute-start.11 = (f32[1,15,32,128]{3,2,1,0:T(8,128)S(1)}, f32[1,15,32,128]{3,2,1,0:T(8,128)S(1)}, u32[]{:S(2)}, u32[]{:S(2)}) collective-permute-start(f32[1,15,32,128]{3,2,1,0:T(8,128)S(1)} %get-tuple-element.68.refs_3_), channel_id=1, source_target_pairs={{0,8},{8,0},{16,24},{24,16},{1,9},{9,1},{17,25},{25,17},{2,10},{10... | collective-permute-start | bytes 737288 | tf_op jit(solution)/shard_map/ppermute | solution.py:216
  5.2 6.7 %collective-permute-start.2 = (f32[3,4,32,128]{3,2,1,0:T(8,128)S(1)}, f32[3,4,32,128]{3,2,1,0:T(8,128)S(1)}, u32[]{:S(2)}, u32[]{:S(2)}) collective-permute-start(f32[3,4,32,128]{3,2,1,0:T(8,128)S(1)} %get-tuple-element.36._), channel_id=1, source_target_pairs={{0,1},{1,0},{2,3},{3,2},{4,5},{5,4},{6,7},{7,6},{8,9},{9,8},{10,11... | collective-permute-start | bytes 589832 | tf_op jit(solution)/shard_map/ppermute | solution.py:379
  6.3 27.1 %copy-start.1 = (f32[3,2,16,32,128]{4,3,2,1,0:T(8,128)S(1)}, f32[3,2,16,32,128]{4,3,2,1,0:T(8,128)}, u32[]{:S(2)}) copy-start(f32[3,2,16,32,128]{4,3,2,1,0:T(8,128)} %views.3) | copy-start | bytes 4718596
  6.3 21.0 %collective-permute-start.1 = (f32[1,15,32,128]{3,2,1,0:T(8,128)S(1)}, f32[1,15,32,128]{3,2,1,0:T(8,128)S(1)}, u32[]{:S(2)}, u32[]{:S(2)}) collective-permute-start(f32[1,15,32,128]{3,2,1,0:T(8,128)S(1)} %get-tuple-element.69), channel_id=1, source_target_pairs={{8,16},{16,8},{9,17},{17,9},{10,18},{18,10},{11,19},{19,11},{12,20... | collective-permute-start | bytes 737288 | tf_op jit(solution)/shard_map/ppermute | solution.py:216
  9.5 17.7 %collective-permute-start = (f32[1,15,32,128]{3,2,1,0:T(8,128)S(1)}, f32[1,15,32,128]{3,2,1,0:T(8,128)S(1)}, u32[]{:S(2)}, u32[]{:S(2)}) collective-permute-start(f32[1,15,32,128]{3,2,1,0:T(8,128)S(1)} %get-tuple-element.70), channel_id=1, source_target_pairs={{0,8},{8,0},{16,24},{24,16},{1,9},{9,1},{17,25},{25,17},{2,10},{10... | collective-permute-start | bytes 737288 | tf_op jit(solution)/shard_map/ppermute | solution.py:216
  12.5 4.1 %collective-permute-start.3 = (f32[3,2,32,128]{3,2,1,0:T(8,128)S(1)}, f32[3,2,32,128]{3,2,1,0:T(8,128)S(1)}, u32[]{:S(2)}, u32[]{:S(2)}) collective-permute-start(f32[3,2,32,128]{3,2,1,0:T(8,128)S(1)} %get-tuple-element.39), channel_id=1, source_target_pairs={{0,2},{1,3},{2,0},{3,1},{4,6},{5,7},{6,4},{7,5},{8,10},{9,11},{10,... | collective-permute-start | bytes 294920 | tf_op jit(solution)/shard_map/ppermute | solution.py:379
  17.3 4.2 %collective-permute-start.4 = (f32[3,1,32,128]{3,2,0,1:T(8,128)S(1)}, f32[3,1,32,128]{3,2,0,1:T(8,128)S(1)}, u32[]{:S(2)}, u32[]{:S(2)}) collective-permute-start(f32[3,1,32,128]{3,2,0,1:T(8,128)S(1)} %bitcast.12), channel_id=1, source_target_pairs={{0,4},{1,5},{2,6},{3,7},{4,0},{5,1},{6,2},{7,3},{8,12},{9,13},{10,... | collective-permute-start | bytes 147464 | tf_op jit(solution)/shard_map/ppermute | solution.py:379
  22.1 9.9 %collective-permute-start.13 = (f32[1,46,16,128]{3,2,1,0:T(8,128)S(1)}, f32[1,46,16,128]{3,2,1,0:T(8,128)S(1)}, u32[]{:S(2)}, u32[]{:S(2)}) collective-permute-start(f32[1,46,16,128]{3,2,1,0:T(8,128)S(1)} %get-tuple-element.56), channel_id=1, source_target_pairs={{0,1},{1,0},{2,3},{3,2},{4,5},{5,4},{6,7},{7,6},{8,9},{9,8},{10,11... | collective-permute-start | bytes 1130504 | tf_op jit(solution)/shard_map/ppermute | solution.py:216
  24.1 9.2 %collective-permute-start.14 = (f32[1,46,16,128]{3,2,1,0:T(8,128)S(1)}, f32[1,46,16,128]{3,2,1,0:T(8,128)S(1)}, u32[]{:S(2)}, u32[]{:S(2)}) collective-permute-start(f32[1,46,16,128]{3,2,1,0:T(8,128)S(1)} %get-tuple-element.57), channel_id=1, source_target_pairs={{1,2},{2,1},{3,4},{4,3},{5,6},{6,5},{9,10},{10,9},{11,12},{12,11},... | collective-permute-start | bytes 1130504 | tf_op jit(solution)/shard_map/ppermute | solution.py:216
  27.9 11.7 %collective-permute-start.5 = (f32[1,46,16,128]{3,2,1,0:T(8,128)S(1)}, f32[1,46,16,128]{3,2,1,0:T(8,128)S(1)}, u32[]{:S(2)}, u32[]{:S(2)}) collective-permute-start(f32[1,46,16,128]{3,2,1,0:T(8,128)S(1)} %get-tuple-element.41), channel_id=1, source_target_pairs={{0,1},{1,0},{2,3},{3,2},{4,5},{5,4},{6,7},{7,6},{8,9},{9,8},{10,11... | collective-permute-start | bytes 1130504 | tf_op jit(solution)/shard_map/ppermute | solution.py:216
  28.0 11.7 %collective-permute-start.6 = (f32[1,46,16,128]{3,2,1,0:T(8,128)S(1)}, f32[1,46,16,128]{3,2,1,0:T(8,128)S(1)}, u32[]{:S(2)}, u32[]{:S(2)}) collective-permute-start(f32[1,46,16,128]{3,2,1,0:T(8,128)S(1)} %get-tuple-element.42), channel_id=1, source_target_pairs={{1,2},{2,1},{3,4},{4,3},{5,6},{6,5},{9,10},{10,9},{11,12},{12,11},... | collective-permute-start | bytes 1130504 | tf_op jit(solution)/shard_map/ppermute | solution.py:216
  35.9 9.6 %collective-permute-start.15 = (f32[1,46,16,128]{3,2,1,0:T(8,128)S(1)}, f32[1,46,16,128]{3,2,1,0:T(8,128)S(1)}, u32[]{:S(2)}, u32[]{:S(2)}) collective-permute-start(f32[1,46,16,128]{3,2,1,0:T(8,128)S(1)} %get-tuple-element.59), channel_id=1, source_target_pairs={{0,1},{1,0},{2,3},{3,2},{4,5},{5,4},{6,7},{7,6},{8,9},{9,8},{10,11... | collective-permute-start | bytes 1130504 | tf_op jit(solution)/shard_map/ppermute | solution.py:216
  36.0 9.5 %collective-permute-start.16 = (f32[1,46,16,128]{3,2,1,0:T(8,128)S(1)}, f32[1,46,16,128]{3,2,1,0:T(8,128)S(1)}, u32[]{:S(2)}, u32[]{:S(2)}) collective-permute-start(f32[1,46,16,128]{3,2,1,0:T(8,128)S(1)} %get-tuple-element.60), channel_id=1, source_target_pairs={{1,2},{2,1},{3,4},{4,3},{5,6},{6,5},{9,10},{10,9},{11,12},{12,11},... | collective-permute-start | bytes 1130504 | tf_op jit(solution)/shard_map/ppermute | solution.py:216
  42.3 8.5 %collective-permute-start.7 = (f32[1,46,16,128]{3,2,1,0:T(8,128)S(1)}, f32[1,46,16,128]{3,2,1,0:T(8,128)S(1)}, u32[]{:S(2)}, u32[]{:S(2)}) collective-permute-start(f32[1,46,16,128]{3,2,1,0:T(8,128)S(1)} %get-tuple-element.50), channel_id=1, source_target_pairs={{0,1},{1,0},{2,3},{3,2},{4,5},{5,4},{6,7},{7,6},{8,9},{9,8},{10,11... | collective-permute-start | bytes 1130504 | tf_op jit(solution)/shard_map/ppermute | solution.py:216
  42.3 9.2 %collective-permute-start.8 = (f32[1,46,16,128]{3,2,1,0:T(8,128)S(1)}, f32[1,46,16,128]{3,2,1,0:T(8,128)S(1)}, u32[]{:S(2)}, u32[]{:S(2)}) collective-permute-start(f32[1,46,16,128]{3,2,1,0:T(8,128)S(1)} %get-tuple-element.51), channel_id=1, source_target_pairs={{1,2},{2,1},{3,4},{4,3},{5,6},{6,5},{9,10},{10,9},{11,12},{12,11},... | collective-permute-start | bytes 1130504 | tf_op jit(solution)/shard_map/ppermute | solution.py:216
  46.2 10.6 %collective-permute-start.17 = (f32[1,15,32,128]{3,2,1,0:T(8,128)S(1)}, f32[1,15,32,128]{3,2,1,0:T(8,128)S(1)}, u32[]{:S(2)}, u32[]{:S(2)}) collective-permute-start(f32[1,15,32,128]{3,2,1,0:T(8,128)S(1)} %get-tuple-element.63), channel_id=1, source_target_pairs={{0,8},{8,0},{16,24},{24,16},{1,9},{9,1},{17,25},{25,17},{2,10},{10... | collective-permute-start | bytes 737288 | tf_op jit(solution)/shard_map/ppermute | solution.py:216
  47.7 12.6 %collective-permute-start.18 = (f32[1,15,32,128]{3,2,1,0:T(8,128)S(1)}, f32[1,15,32,128]{3,2,1,0:T(8,128)S(1)}, u32[]{:S(2)}, u32[]{:S(2)}) collective-permute-start(f32[1,15,32,128]{3,2,1,0:T(8,128)S(1)} %get-tuple-element.64), channel_id=1, source_target_pairs={{8,16},{16,8},{9,17},{17,9},{10,18},{18,10},{11,19},{19,11},{12,20... | collective-permute-start | bytes 737288 | tf_op jit(solution)/shard_map/ppermute | solution.py:216
  52.2 11.5 %collective-permute-start.9 = (f32[1,15,32,128]{3,2,1,0:T(8,128)S(1)}, f32[1,15,32,128]{3,2,1,0:T(8,128)S(1)}, u32[]{:S(2)}, u32[]{:S(2)}) collective-permute-start(f32[1,15,32,128]{3,2,1,0:T(8,128)S(1)} %get-tuple-element.54), channel_id=1, source_target_pairs={{0,8},{8,0},{16,24},{24,16},{1,9},{9,1},{17,25},{25,17},{2,10},{10... | collective-permute-start | bytes 737288 | tf_op jit(solution)/shard_map/ppermute | solution.py:216
  53.7 17.1 %collective-permute-start.10 = (f32[1,15,32,128]{3,2,1,0:T(8,128)S(1)}, f32[1,15,32,128]{3,2,1,0:T(8,128)S(1)}, u32[]{:S(2)}, u32[]{:S(2)}) collective-permute-start(f32[1,15,32,128]{3,2,1,0:T(8,128)S(1)} %get-tuple-element.55), channel_id=1, source_target_pairs={{8,16},{16,8},{9,17},{17,9},{10,18},{18,10},{11,19},{19,11},{12,20... | collective-permute-start | bytes 737288 | tf_op jit(solution)/shard_map/ppermute | solution.py:216

commit v3 on v2

--- a/solution.py
+++ b/solution.py
@@ -397,17 +397,19 @@
     step, mats = 1, None
     while True:
         got = flip(sent, "by", step)
-        if mats is None:
-            mats = bands(kernels, place, planes, width, depth, sent)
         step *= 2
         if step == cols:
             break
-        kept, sent = halve_profiles(step, place, kept, got, (mats[0],))
+        kept, sent = halve_profiles(step, place, kept, got, () if mats is None else (mats[0],))
+        if mats is None:
+            mats = bands(kernels, place, planes, width, depth, sent)
+    if mats is None:
+        mats = bands(kernels, place, planes, width, depth, sent)
     lights = (kept.reshape(-1, width, depth), got.reshape(-1, width, depth))
     rims = []
     for c in range(channels):
         xa, xb = halo[c]
-        yc, yd = pack_rows(c, place, estimate, xa, xb, (got,))
+        yc, yd = pack_rows(c, place, estimate, xa, xb, (sent if c == 0 else got,))
         yd = trade(yd, "by", False)
         rims.append((yc, trade(yc, "by", True), yd))
     ends, sums, done, prev = [], kernels, None, ()

time: 72.6 us -> 68 us (0.937)
  the two profiles are of different devices: /device:TPU:13 before, /device:TPU:9 now
where the time goes in v3:
time: 68 us; the launch traced here: 67.6 us
  starting transfers between devices  34.8 us (51%)
  waiting for transfers between devices  16.7 us (25%)
  Pallas kernels  14.5 us (21%)
  local copies, waits for them, and re-layouts  1.22 us (2%)
    ppermute x16, starting transfers between devices, trade(): return lax.ppermute(value, axis, pairs)  31.2 us
    ppermute x16, waiting for transfers between devices, trade(): return lax.ppermute(value, axis, pairs)  15.7 us
    pallas_call x2, Pallas kernels, brick(): pl.pallas_call(fused, grid=(1,), out_shape=[jax.ShapeDtypeStruct(s, F32)...  5.19 us
    pallas_call x7, Pallas kernels, call(): return out(*[array for _, array in ins], *deps)  4.23 us
    ppermute x3, starting transfers between devices, flip(): lax.ppermute(value, axis, [(i, i ^ step) for i in range(lax.axis_size(axi...  3.63 us
    pallas_call x2, Pallas kernels, finish(): pl.pallas_call(body, grid=(1,), out_shape=jax.ShapeDtypeStruct(estimate.s...  2.78 us
    pallas_call x1, Pallas kernels, bands(): pl.pallas_call(matrices, out_shape=[jax.ShapeDtypeStruct(s, BF16) for s i...  2.3 us
  transfers between devices with their start and end apart: 19, of which 5 were waited for; matrix products, arithmetic and copies ran while one was open for 0% of the time, Pallas kernels for 19%

profile of v3, /device:TPU:9, one launch (start us, length us, event | category | flops | bytes accessed | tf_op | source)
XLA Modules:
  0.0 67.6 jit_solution(13643307127026684191)
XLA Ops:
  0.0 0.0 copy-start.2
  0.0 0.0 copy-start.4
  0.0 1.1 %fusion = (f32[1,16,32,128]{3,2,1,0:T(8,128)S(1)}, f32[1,16,32,128]{3,2,1,0:T(8,128)S(1)}) fusion(f32[2,16,32,128]{3,2,1,0:T(8,128)} %estimate.3), kind=kLoop, calls=%fused_computation.5 | loop fusion | bytes 1048576 | tf_op jit(solution)/shard_map/slice | solution.py:391
  1.1 0.0 copy-start.3
  1.1 0.0 copy-start
  1.2 1.3 %collective-permute-start.11 = (f32[1,15,32,128]{3,2,1,0:T(8,128)S(1)}, f32[1,15,32,128]{3,2,1,0:T(8,128)S(1)}, u32[]{:S(2)}, u32[]{:S(2)}) collective-permute-start(f32[1,15,32,128]{3,2,1,0:T(8,128)S(1)} %get-tuple-element.68.refs_3_), channel_id=1, source_target_pairs={{0,8},{8,0},{16,24},{24,16},{1,9},{9,1},{17,25},{25,17},{2,10},{10... | collective-permute-start | bytes 737288 | tf_op jit(solution)/shard_map/ppermute | solution.py:216
  2.5 0.1 pad_add_fusion.refs_0_.parity.place
  2.6 0.0 copy-done.2
  2.6 0.0 copy-done.4
  2.6 0.6 mask_profiles.1
  3.2 1.0 %collective-permute-start.2 = (f32[3,4,32,128]{3,2,1,0:T(8,128)S(1)}, f32[3,4,32,128]{3,2,1,0:T(8,128)S(1)}, u32[]{:S(2)}, u32[]{:S(2)}) collective-permute-start(f32[3,4,32,128]{3,2,1,0:T(8,128)S(1)} %get-tuple-element.36), channel_id=1, source_target_pairs={{0,1},{1,0},{2,3},{3,2},{4,5},{5,4},{6,7},{7,6},{8,9},{9,8},{10,11... | collective-permute-start | bytes 589832 | tf_op jit(solution)/shard_map/ppermute | solution.py:379
  4.2 0.7 collective-permute-start.12
  4.9 0.0 copy-start.1
  5.0 3.7 %collective-permute-start = (f32[1,15,32,128]{3,2,1,0:T(8,128)S(1)}, f32[1,15,32,128]{3,2,1,0:T(8,128)S(1)}, u32[]{:S(2)}, u32[]{:S(2)}) collective-permute-start(f32[1,15,32,128]{3,2,1,0:T(8,128)S(1)} %get-tuple-element.70), channel_id=1, source_target_pairs={{0,8},{8,0},{16,24},{24,16},{1,9},{9,1},{17,25},{25,17},{2,10},{10... | collective-permute-start | bytes 737288 | tf_op jit(solution)/shard_map/ppermute | solution.py:216
  8.7 0.7 collective-permute-start.1
  9.3 0.0 collective-permute-done.2.refs_2_
  9.4 0.6 halve_profiles2.1
  9.9 0.2 collective-permute-start.3
  10.2 0.0 copy-done.3
  10.2 2.3 %matrices.1 = (bf16[48,144]{1,0:T(8,128)(2,1)S(1)}, bf16[48,144]{1,0:T(8,128)(2,1)S(1)}, bf16[3,32,192]{2,1,0:T(8,128)(2,1)S(1)}, bf16[3,64,96]{2,1,0:T(8,128)(2...) custom-call(f32[3,3,31]{2,1,0:T(4,128)S(1)} %copy-done.3, ...), custom_call_target="tpu_custom_call" | custom-call | tf_op jit(solution)/shard_map/matrices/pallas_call | solution.py:94
  12.5 1.0 %collective-permute-done.3.refs_2_ = f32[3,2,32,128]{3,2,1,0:T(8,128)S(1)} collective-permute-done((f32[3,2,32,128]{3,2,1,0:T(8,128)S(1)}, f32[3,2,32,128]{3,2,1,0:T(8,128)S(1)}, u32[]{:S(2)}, u32[]{:S(2)}) %collective-permute-start.3) | collective-permute-done | bytes 98336 | tf_op jit(solution)/shard_map/ppermute | solution.py:379
  13.5 0.6 halve_profiles4.1
  14.0 2.4 %collective-permute-start.4 = (f32[3,1,32,128]{3,2,0,1:T(8,128)S(1)}, f32[3,1,32,128]{3,2,0,1:T(8,128)S(1)}, u32[]{:S(2)}, u32[]{:S(2)}) collective-permute-start(f32[3,1,32,128]{3,2,0,1:T(8,128)S(1)} %bitcast.11), channel_id=1, source_target_pairs={{0,4},{1,5},{2,6},{3,7},{4,0},{5,1},{6,2},{7,3},{8,12},{9,13},{10,... | collective-permute-start | bytes 147464 | tf_op jit(solution)/shard_map/ppermute | solution.py:379
  16.4 0.0 collective-permute-done.11.refs_2_.xa
  16.4 0.0 collective-permute-done.12.refs_3_.xb
  16.4 0.0 copy-done
  16.4 0.6 pack_rows0.1
  17.0 2.1 %collective-permute-start.13 = (f32[1,46,16,128]{3,2,1,0:T(8,128)S(1)}, f32[1,46,16,128]{3,2,1,0:T(8,128)S(1)}, u32[]{:S(2)}, u32[]{:S(2)}) collective-permute-start(f32[1,46,16,128]{3,2,1,0:T(8,128)S(1)} %get-tuple-element.56), channel_id=1, source_target_pairs={{0,1},{1,0},{2,3},{3,2},{4,5},{5,4},{6,7},{7,6},{8,9},{9,8},{10,11... | collective-permute-start | bytes 1130504 | tf_op jit(solution)/shard_map/ppermute | solution.py:216
  19.1 1.9 %collective-permute-start.14 = (f32[1,46,16,128]{3,2,1,0:T(8,128)S(1)}, f32[1,46,16,128]{3,2,1,0:T(8,128)S(1)}, u32[]{:S(2)}, u32[]{:S(2)}) collective-permute-start(f32[1,46,16,128]{3,2,1,0:T(8,128)S(1)} %get-tuple-element.57), channel_id=1, source_target_pairs={{1,2},{2,1},{3,4},{4,3},{5,6},{6,5},{9,10},{10,9},{11,12},{12,11},... | collective-permute-start | bytes 1130504 | tf_op jit(solution)/shard_map/ppermute | solution.py:216
  21.0 0.0 collective-permute-done.refs_2_.xa
  21.1 0.0 collective-permute-done.1.refs_3_.xb
  21.1 0.0 collective-permute-done.4
  21.1 0.6 pack_rows1.1
  21.7 0.6 collective-permute-start.5
  22.3 3.1 %collective-permute-start.6 = (f32[1,46,16,128]{3,2,1,0:T(8,128)S(1)}, f32[1,46,16,128]{3,2,1,0:T(8,128)S(1)}, u32[]{:S(2)}, u32[]{:S(2)}) collective-permute-start(f32[1,46,16,128]{3,2,1,0:T(8,128)S(1)} %get-tuple-element.42), channel_id=1, source_target_pairs={{1,2},{2,1},{3,4},{4,3},{5,6},{6,5},{9,10},{10,9},{11,12},{12,11},... | collective-permute-start | bytes 1130504 | tf_op jit(solution)/shard_map/ppermute | solution.py:216
  25.4 0.0 collective-permute-done.13.yc
  25.4 2.9 %collective-permute-done.14.yd = f32[1,46,16,128]{3,2,1,0:T(8,128)S(1)} collective-permute-done((f32[1,46,16,128]{3,2,1,0:T(8,128)S(1)}, f32[1,46,16,128]{3,2,1,0:T(8,128)S(1)}, u32[]{:S(2)}, u32[]{:S(2)}) %collective-permute-start.14) | collective-permute-done | bytes 376864 | tf_op jit(solution)/shard_map/ppermute | solution.py:216
  28.3 0.0 copy-done.1
  28.3 2.6 %brick0.1 = (f32[1,16,32,128]{3,2,1,0:T(8,128)S(1)}, f32[1,15,32,128]{3,2,1,0:T(8,128)S(1)}, f32[1,15,32,128]{3,2,1,0:T(8,128)S(1)}, f32[1,46,16,128]{3,2,1,0:T(8,128)S(1)}, f32[1,46,16,128]{3,2,1,0:T(8,128)S(1)}) custom-call(f32[2,16,32,128]{3,2,1,0:T(8,128)S(1)} %copy-done, f32[1,15,32,128]{3,2,1,0:T(8,128)S(1)} %collective-permute-done.11.refs_2_.xa, ...), custom_call_target="tpu_custom_call" | custom-call | tf_op jit(solution)/shard_map/brick0/pallas_call | solution.py:192
  30.9 0.1 collective-permute-start.15
  31.0 1.9 %collective-permute-start.16 = (f32[1,46,16,128]{3,2,1,0:T(8,128)S(1)}, f32[1,46,16,128]{3,2,1,0:T(8,128)S(1)}, u32[]{:S(2)}, u32[]{:S(2)}) collective-permute-start(f32[1,46,16,128]{3,2,1,0:T(8,128)S(1)} %get-tuple-element.60), channel_id=1, source_target_pairs={{1,2},{2,1},{3,4},{4,3},{5,6},{6,5},{9,10},{10,9},{11,12},{12,11},... | collective-permute-start | bytes 1130504 | tf_op jit(solution)/shard_map/ppermute | solution.py:216
  32.9 0.0 collective-permute-done.5.yc
  33.0 0.0 collective-permute-done.6.yd
  33.0 2.6 %brick1.1 = (f32[1,16,32,128]{3,2,1,0:T(8,128)S(1)}, f32[1,15,32,128]{3,2,1,0:T(8,128)S(1)}, f32[1,15,32,128]{3,2,1,0:T(8,128)S(1)}, f32[1,46,16,128]{3,2,1,0:T(8,128)S(1)}, f32[1,46,16,128]{3,2,1,0:T(8,128)S(1)}) custom-call(f32[2,16,32,128]{3,2,1,0:T(8,128)S(1)} %copy-done, f32[1,15,32,128]{3,2,1,0:T(8,128)S(1)} %collective-permute-done.refs_2_.xa, ...), custom_call_target="tpu_custom_call" | custom-call | tf_op jit(solution)/shard_map/brick1/pallas_call | solution.py:192
  35.6 0.5 collective-permute-start.7
  36.1 3.2 %collective-permute-start.8 = (f32[1,46,16,128]{3,2,1,0:T(8,128)S(1)}, f32[1,46,16,128]{3,2,1,0:T(8,128)S(1)}, u32[]{:S(2)}, u32[]{:S(2)}) collective-permute-start(f32[1,46,16,128]{3,2,1,0:T(8,128)S(1)} %get-tuple-element.51), channel_id=1, source_target_pairs={{1,2},{2,1},{3,4},{4,3},{5,6},{6,5},{9,10},{10,9},{11,12},{12,11},... | collective-permute-start | bytes 1130504 | tf_op jit(solution)/shard_map/ppermute | solution.py:216
  39.3 0.0 collective-permute-done.15.refs_3_.rc
  39.3 0.7 %collective-permute-done.16.refs_4_.rd = f32[1,46,16,128]{3,2,1,0:T(8,128)S(1)} collective-permute-done((f32[1,46,16,128]{3,2,1,0:T(8,128)S(1)}, f32[1,46,16,128]{3,2,1,0:T(8,128)S(1)}, u32[]{:S(2)}, u32[]{:S(2)}) %collective-permute-start.16) | collective-permute-done | bytes 376864 | tf_op jit(solution)/shard_map/ppermute | solution.py:216
  40.0 0.6 add_rows0.1
  40.7 3.5 %collective-permute-start.17 = (f32[1,15,32,128]{3,2,1,0:T(8,128)S(1)}, f32[1,15,32,128]{3,2,1,0:T(8,128)S(1)}, u32[]{:S(2)}, u32[]{:S(2)}) collective-permute-start(f32[1,15,32,128]{3,2,1,0:T(8,128)S(1)} %get-tuple-element.63), channel_id=1, source_target_pairs={{0,8},{8,0},{16,24},{24,16},{1,9},{9,1},{17,25},{25,17},{2,10},{10... | collective-permute-start | bytes 737288 | tf_op jit(solution)/shard_map/ppermute | solution.py:216
  44.2 0.7 collective-permute-start.18
  44.8 0.0 collective-permute-done.7.refs_3_.rc
  44.9 0.2 collective-permute-done.8.refs_4_.rd
  45.0 0.6 add_rows1.1
  45.7 0.7 collective-permute-start.10
  46.3 6.6 %collective-permute-start.9 = (f32[1,15,32,128]{3,2,1,0:T(8,128)S(1)}, f32[1,15,32,128]{3,2,1,0:T(8,128)S(1)}, u32[]{:S(2)}, u32[]{:S(2)}) collective-permute-start(f32[1,15,32,128]{3,2,1,0:T(8,128)S(1)} %get-tuple-element.54), channel_id=1, source_target_pairs={{0,8},{8,0},{16,24},{24,16},{1,9},{9,1},{17,25},{25,17},{2,10},{10... | collective-permute-start | bytes 737288 | tf_op jit(solution)/shard_map/ppermute | solution.py:216
  53.0 0.0 collective-permute-done.17.qa
  53.0 0.0 collective-permute-done.18.qb
  53.0 1.4 %finish0.1.rest_0_ = f32[2,16,32,128]{3,2,1,0:T(8,128)} custom-call(s32[2]{0:T(128)S(1)} %pad_add_fusion.refs_0_.parity.place, f32[2,16,32,128]{3,2,1,0:T(8,128)S(1)} %copy-done, f32[1,16,32,128]{3,2,1,0:T(8,128)S(1)} %get-tuple-element.58.s_own, f32[1,46,16,128]{3,2,1,0:T(8,128)S(1)} %collective-permute-done.15.refs_3_.rc, ...), custom_call_target="tpu_custom_call" | custom-call | tf_op jit(solution)/shard_map/finish0/pallas_call | solution.py:363
  54.3 0.0 collective-permute-done.10.qb
  54.4 11.9 %collective-permute-done.9.qa = f32[1,15,32,128]{3,2,1,0:T(8,128)S(1)} collective-permute-done((f32[1,15,32,128]{3,2,1,0:T(8,128)S(1)}, f32[1,15,32,128]{3,2,1,0:T(8,128)S(1)}, u32[]{:S(2)}, u32[]{:S(2)}) %collective-permute-start.9) | collective-permute-done | bytes 245792 | tf_op jit(solution)/shard_map/ppermute | solution.py:216
  66.3 1.4 %finish1.1 = f32[2,16,32,128]{3,2,1,0:T(8,128)} custom-call(s32[2]{0:T(128)S(1)} %pad_add_fusion.refs_0_.parity.place, f32[2,16,32,128]{3,2,1,0:T(8,128)S(1)} %copy-done, f32[1,16,32,128]{3,2,1,0:T(8,128)S(1)} %get-tuple-element.49.s_own, f32[1,46,16,128]{3,2,1,0:T(8,128)S(1)} %collective-permute-done.7.refs_3_.rc, ...), custom_call_target="tpu_custom_call", output_to_operand_aliasing={{}: (7, {})} | custom-call | tf_op jit(solution)/shard_map/finish1/pallas_call | solution.py:363
  (2 shorter events, 0.1 us)
Async XLA Ops:
  0.0 2.6 %copy-start.2 = (f32[1,1,3,256,128]{4,3,2,1,0:T(8,128)S(1)}, f32[1,1,3,256,128]{4,3,2,1,0:T(8,128)}, u32[]{:S(2)}) copy-start(f32[1,1,3,256,128]{4,3,2,1,0:T(8,128)} %refs_2_.1) | copy-start | bytes 1179652
  0.0 2.6 %copy-start.4 = (s32[3,4]{1,0:T(4,128)S(1)}, s32[3,4]{1,0:T(4,128)}, u32[]{:S(2)}) copy-start(s32[3,4]{1,0:T(4,128)} %refs_1_.3) | copy-start | bytes 148
  1.1 9.1 %copy-start.3 = (f32[3,3,31]{2,1,0:T(4,128)S(1)}, f32[3,3,31]{2,1,0:T(4,128)}, u32[]{:S(2)}) copy-start(f32[3,3,31]{2,1,0:T(4,128)} %rest_1_.1) | copy-start | bytes 3352
  1.1 15.3 %copy-start = (f32[2,16,32,128]{3,2,1,0:T(8,128)S(1)}, f32[2,16,32,128]{3,2,1,0:T(8,128)}, u32[]{:S(2)}) copy-start(f32[2,16,32,128]{3,2,1,0:T(8,128)} %estimate.3) | copy-start | bytes 1572868
  1.2 15.2 %collective-permute-start.11 = (f32[1,15,32,128]{3,2,1,0:T(8,128)S(1)}, f32[1,15,32,128]{3,2,1,0:T(8,128)S(1)}, u32[]{:S(2)}, u32[]{:S(2)}) collective-permute-start(f32[1,15,32,128]{3,2,1,0:T(8,128)S(1)} %get-tuple-element.68.refs_3_), channel_id=1, source_target_pairs={{0,8},{8,0},{16,24},{24,16},{1,9},{9,1},{17,25},{25,17},{2,10},{10... | collective-permute-start | bytes 737288 | tf_op jit(solution)/shard_map/ppermute | solution.py:216
  3.2 6.1 %collective-permute-start.2 = (f32[3,4,32,128]{3,2,1,0:T(8,128)S(1)}, f32[3,4,32,128]{3,2,1,0:T(8,128)S(1)}, u32[]{:S(2)}, u32[]{:S(2)}) collective-permute-start(f32[3,4,32,128]{3,2,1,0:T(8,128)S(1)} %get-tuple-element.36), channel_id=1, source_target_pairs={{0,1},{1,0},{2,3},{3,2},{4,5},{5,4},{6,7},{7,6},{8,9},{9,8},{10,11... | collective-permute-start | bytes 589832 | tf_op jit(solution)/shard_map/ppermute | solution.py:379
  4.2 12.2 %collective-permute-start.12 = (f32[1,15,32,128]{3,2,1,0:T(8,128)S(1)}, f32[1,15,32,128]{3,2,1,0:T(8,128)S(1)}, u32[]{:S(2)}, u32[]{:S(2)}) collective-permute-start(f32[1,15,32,128]{3,2,1,0:T(8,128)S(1)} %get-tuple-element.67), channel_id=1, source_target_pairs={{8,16},{16,8},{9,17},{17,9},{10,18},{18,10},{11,19},{19,11},{12,20... | collective-permute-start | bytes 737288 | tf_op jit(solution)/shard_map/ppermute | solution.py:216
  4.9 23.4 %copy-start.1 = (f32[3,2,16,32,128]{4,3,2,1,0:T(8,128)S(1)}, f32[3,2,16,32,128]{4,3,2,1,0:T(8,128)}, u32[]{:S(2)}) copy-start(f32[3,2,16,32,128]{4,3,2,1,0:T(8,128)} %views.3) | copy-start | bytes 4718596
  5.0 16.1 %collective-permute-start = (f32[1,15,32,128]{3,2,1,0:T(8,128)S(1)}, f32[1,15,32,128]{3,2,1,0:T(8,128)S(1)}, u32[]{:S(2)}, u32[]{:S(2)}) collective-permute-start(f32[1,15,32,128]{3,2,1,0:T(8,128)S(1)} %get-tuple-element.70), channel_id=1, source_target_pairs={{0,8},{8,0},{16,24},{24,16},{1,9},{9,1},{17,25},{25,17},{2,10},{10... | collective-permute-start | bytes 737288 | tf_op jit(solution)/shard_map/ppermute | solution.py:216
  8.7 12.4 %collective-permute-start.1 = (f32[1,15,32,128]{3,2,1,0:T(8,128)S(1)}, f32[1,15,32,128]{3,2,1,0:T(8,128)S(1)}, u32[]{:S(2)}, u32[]{:S(2)}) collective-permute-start(f32[1,15,32,128]{3,2,1,0:T(8,128)S(1)} %get-tuple-element.69), channel_id=1, source_target_pairs={{8,16},{16,8},{9,17},{17,9},{10,18},{18,10},{11,19},{19,11},{12,20... | collective-permute-start | bytes 737288 | tf_op jit(solution)/shard_map/ppermute | solution.py:216
  9.9 3.5 %collective-permute-start.3 = (f32[3,2,32,128]{3,2,1,0:T(8,128)S(1)}, f32[3,2,32,128]{3,2,1,0:T(8,128)S(1)}, u32[]{:S(2)}, u32[]{:S(2)}) collective-permute-start(f32[3,2,32,128]{3,2,1,0:T(8,128)S(1)} %get-tuple-element.38._), channel_id=1, source_target_pairs={{0,2},{1,3},{2,0},{3,1},{4,6},{5,7},{6,4},{7,5},{8,10},{9,11},{10,... | collective-permute-start | bytes 294920 | tf_op jit(solution)/shard_map/ppermute | solution.py:379
  14.0 7.0 %collective-permute-start.4 = (f32[3,1,32,128]{3,2,0,1:T(8,128)S(1)}, f32[3,1,32,128]{3,2,0,1:T(8,128)S(1)}, u32[]{:S(2)}, u32[]{:S(2)}) collective-permute-start(f32[3,1,32,128]{3,2,0,1:T(8,128)S(1)} %bitcast.11), channel_id=1, source_target_pairs={{0,4},{1,5},{2,6},{3,7},{4,0},{5,1},{6,2},{7,3},{8,12},{9,13},{10,... | collective-permute-start | bytes 147464 | tf_op jit(solution)/shard_map/ppermute | solution.py:379
  17.0 8.4 %collective-permute-start.13 = (f32[1,46,16,128]{3,2,1,0:T(8,128)S(1)}, f32[1,46,16,128]{3,2,1,0:T(8,128)S(1)}, u32[]{:S(2)}, u32[]{:S(2)}) collective-permute-start(f32[1,46,16,128]{3,2,1,0:T(8,128)S(1)} %get-tuple-element.56), channel_id=1, source_target_pairs={{0,1},{1,0},{2,3},{3,2},{4,5},{5,4},{6,7},{7,6},{8,9},{9,8},{10,11... | collective-permute-start | bytes 1130504 | tf_op jit(solution)/shard_map/ppermute | solution.py:216
  19.1 9.2 %collective-permute-start.14 = (f32[1,46,16,128]{3,2,1,0:T(8,128)S(1)}, f32[1,46,16,128]{3,2,1,0:T(8,128)S(1)}, u32[]{:S(2)}, u32[]{:S(2)}) collective-permute-start(f32[1,46,16,128]{3,2,1,0:T(8,128)S(1)} %get-tuple-element.57), channel_id=1, source_target_pairs={{1,2},{2,1},{3,4},{4,3},{5,6},{6,5},{9,10},{10,9},{11,12},{12,11},... | collective-permute-start | bytes 1130504 | tf_op jit(solution)/shard_map/ppermute | solution.py:216
  21.7 11.3 %collective-permute-start.5 = (f32[1,46,16,128]{3,2,1,0:T(8,128)S(1)}, f32[1,46,16,128]{3,2,1,0:T(8,128)S(1)}, u32[]{:S(2)}, u32[]{:S(2)}) collective-permute-start(f32[1,46,16,128]{3,2,1,0:T(8,128)S(1)} %get-tuple-element.41), channel_id=1, source_target_pairs={{0,1},{1,0},{2,3},{3,2},{4,5},{5,4},{6,7},{7,6},{8,9},{9,8},{10,11... | collective-permute-start | bytes 1130504 | tf_op jit(solution)/shard_map/ppermute | solution.py:216
  22.3 10.6 %collective-permute-start.6 = (f32[1,46,16,128]{3,2,1,0:T(8,128)S(1)}, f32[1,46,16,128]{3,2,1,0:T(8,128)S(1)}, u32[]{:S(2)}, u32[]{:S(2)}) collective-permute-start(f32[1,46,16,128]{3,2,1,0:T(8,128)S(1)} %get-tuple-element.42), channel_id=1, source_target_pairs={{1,2},{2,1},{3,4},{4,3},{5,6},{6,5},{9,10},{10,9},{11,12},{12,11},... | collective-permute-start | bytes 1130504 | tf_op jit(solution)/shard_map/ppermute | solution.py:216
  30.9 8.4 %collective-permute-start.15 = (f32[1,46,16,128]{3,2,1,0:T(8,128)S(1)}, f32[1,46,16,128]{3,2,1,0:T(8,128)S(1)}, u32[]{:S(2)}, u32[]{:S(2)}) collective-permute-start(f32[1,46,16,128]{3,2,1,0:T(8,128)S(1)} %get-tuple-element.59), channel_id=1, source_target_pairs={{0,1},{1,0},{2,3},{3,2},{4,5},{5,4},{6,7},{7,6},{8,9},{9,8},{10,11... | collective-permute-start | bytes 1130504 | tf_op jit(solution)/shard_map/ppermute | solution.py:216
  31.0 9.0 %collective-permute-start.16 = (f32[1,46,16,128]{3,2,1,0:T(8,128)S(1)}, f32[1,46,16,128]{3,2,1,0:T(8,128)S(1)}, u32[]{:S(2)}, u32[]{:S(2)}) collective-permute-start(f32[1,46,16,128]{3,2,1,0:T(8,128)S(1)} %get-tuple-element.60), channel_id=1, source_target_pairs={{1,2},{2,1},{3,4},{4,3},{5,6},{6,5},{9,10},{10,9},{11,12},{12,11},... | collective-permute-start | bytes 1130504 | tf_op jit(solution)/shard_map/ppermute | solution.py:216
  35.6 9.3 %collective-permute-start.7 = (f32[1,46,16,128]{3,2,1,0:T(8,128)S(1)}, f32[1,46,16,128]{3,2,1,0:T(8,128)S(1)}, u32[]{:S(2)}, u32[]{:S(2)}) collective-permute-start(f32[1,46,16,128]{3,2,1,0:T(8,128)S(1)} %get-tuple-element.50), channel_id=1, source_target_pairs={{0,1},{1,0},{2,3},{3,2},{4,5},{5,4},{6,7},{7,6},{8,9},{9,8},{10,11... | collective-permute-start | bytes 1130504 | tf_op jit(solution)/shard_map/ppermute | solution.py:216
  36.1 8.9 %collective-permute-start.8 = (f32[1,46,16,128]{3,2,1,0:T(8,128)S(1)}, f32[1,46,16,128]{3,2,1,0:T(8,128)S(1)}, u32[]{:S(2)}, u32[]{:S(2)}) collective-permute-start(f32[1,46,16,128]{3,2,1,0:T(8,128)S(1)} %get-tuple-element.51), channel_id=1, source_target_pairs={{1,2},{2,1},{3,4},{4,3},{5,6},{6,5},{9,10},{10,9},{11,12},{12,11},... | collective-permute-start | bytes 1130504 | tf_op jit(solution)/shard_map/ppermute | solution.py:216
  40.7 12.3 %collective-permute-start.17 = (f32[1,15,32,128]{3,2,1,0:T(8,128)S(1)}, f32[1,15,32,128]{3,2,1,0:T(8,128)S(1)}, u32[]{:S(2)}, u32[]{:S(2)}) collective-permute-start(f32[1,15,32,128]{3,2,1,0:T(8,128)S(1)} %get-tuple-element.63), channel_id=1, source_target_pairs={{0,8},{8,0},{16,24},{24,16},{1,9},{9,1},{17,25},{25,17},{2,10},{10... | collective-permute-start | bytes 737288 | tf_op jit(solution)/shard_map/ppermute | solution.py:216
  44.2 8.8 %collective-permute-start.18 = (f32[1,15,32,128]{3,2,1,0:T(8,128)S(1)}, f32[1,15,32,128]{3,2,1,0:T(8,128)S(1)}, u32[]{:S(2)}, u32[]{:S(2)}) collective-permute-start(f32[1,15,32,128]{3,2,1,0:T(8,128)S(1)} %get-tuple-element.64), channel_id=1, source_target_pairs={{8,16},{16,8},{9,17},{17,9},{10,18},{18,10},{11,19},{19,11},{12,20... | collective-permute-start | bytes 737288 | tf_op jit(solution)/shard_map/ppermute | solution.py:216
  45.7 8.7 %collective-permute-start.10 = (f32[1,15,32,128]{3,2,1,0:T(8,128)S(1)}, f32[1,15,32,128]{3,2,1,0:T(8,128)S(1)}, u32[]{:S(2)}, u32[]{:S(2)}) collective-permute-start(f32[1,15,32,128]{3,2,1,0:T(8,128)S(1)} %get-tuple-element.55), channel_id=1, source_target_pairs={{8,16},{16,8},{9,17},{17,9},{10,18},{18,10},{11,19},{19,11},{12,20... | collective-permute-start | bytes 737288 | tf_op jit(solution)/shard_map/ppermute | solution.py:216
  46.3 19.9 %collective-permute-start.9 = (f32[1,15,32,128]{3,2,1,0:T(8,128)S(1)}, f32[1,15,32,128]{3,2,1,0:T(8,128)S(1)}, u32[]{:S(2)}, u32[]{:S(2)}) collective-permute-start(f32[1,15,32,128]{3,2,1,0:T(8,128)S(1)} %get-tuple-element.54), channel_id=1, source_target_pairs={{0,8},{8,0},{16,24},{24,16},{1,9},{9,1},{17,25},{25,17},{2,10},{10... | collective-permute-start | bytes 737288 | tf_op jit(solution)/shard_map/ppermute | solution.py:216

commit v4 on v3

--- a/solution.py
+++ b/solution.py
@@ -11,7 +11,7 @@
 BF16 = jnp.bfloat16
 SMALL = pltpu.CompilerParams(vmem_limit_bytes=8 * 1024 * 1024)
 FREE = pl.CostEstimate(flops=0, bytes_accessed=0, transcendentals=0)
-SKEW = 8
+SKEW = 4
 PAD = 16
 
 
@@ -349,6 +349,8 @@
         return pl.BlockSpec((1, planes) + array.shape[2:], lambda i: (0,) * 4)
 
     def body(place, estimate, s_own, rc, rd, qa, qb, *rest):
+        if channel == 1:
+            qa, qb = qb, qa
         out = rest[-1]
         out[...] = s_own[...]
         for got, rows in zip((rc, rd), row_starts(place, width)):
@@ -359,7 +361,8 @@
         out[...] = estimate[...] * out[...] / views
 
     more = [] if done is None else [done]
-    ins = [place, estimate, s_own, rc, rd, qa, qb] + more + list(deps)
+    ends = [qb, qa] if channel == 1 else [qa, qb]
+    ins = [place, estimate, s_own, rc, rd, *ends] + more + list(deps)
     return pl.pallas_call(
         body,
         grid=(1,),

time: 68 us -> 67.6 us (level)
  the two profiles are of different devices: /device:TPU:9 before, /device:TPU:13 now
where the time goes in v4:
time: 67.6 us; the launch traced here: 67.3 us
  starting transfers between devices  33.3 us (49%)
  waiting for transfers between devices  18.5 us (27%)
  Pallas kernels  13.9 us (21%)
  local copies, waits for them, and re-layouts  1.22 us (2%)
    ppermute x16, starting transfers between devices, trade(): return lax.ppermute(value, axis, pairs)  29.6 us
    ppermute x16, waiting for transfers between devices, trade(): return lax.ppermute(value, axis, pairs)  17.2 us
    pallas_call x2, Pallas kernels, brick(): pl.pallas_call(fused, grid=(1,), out_shape=[jax.ShapeDtypeStruct(s, F32)...  4.62 us
    pallas_call x7, Pallas kernels, call(): return out(*[array for _, array in ins], *deps)  4.23 us
    ppermute x3, starting transfers between devices, flip(): lax.ppermute(value, axis, [(i, i ^ step) for i in range(lax.axis_size(axi...  3.63 us
    pallas_call x2, Pallas kernels, finish(): pl.pallas_call(body, grid=(1,), out_shape=jax.ShapeDtypeStruct(estimate.s...  2.78 us
    pallas_call x1, Pallas kernels, bands(): pl.pallas_call(matrices, out_shape=[jax.ShapeDtypeStruct(s, BF16) for s i...  2.3 us
  transfers between devices with their start and end apart: 19, of which 6 were waited for; matrix products, arithmetic and copies ran while one was open for 0% of the time, Pallas kernels for 19%

profile of v4, /device:TPU:13, one launch (start us, length us, event | category | flops | bytes accessed | tf_op | source)
XLA Modules:
  0.0 67.3 jit_solution(2326493324483335975)
XLA Ops:
  0.0 0.0 copy-start.2
  0.0 0.0 copy-start.4
  0.0 1.1 %fusion = (f32[1,16,32,128]{3,2,1,0:T(8,128)S(1)}, f32[1,16,32,128]{3,2,1,0:T(8,128)S(1)}) fusion(f32[2,16,32,128]{3,2,1,0:T(8,128)} %estimate.3), kind=kLoop, calls=%fused_computation.5 | loop fusion | bytes 1048576 | tf_op jit(solution)/shard_map/slice | solution.py:394
  1.1 0.0 copy-start.3
  1.1 0.0 copy-start
  1.2 1.3 %collective-permute-start.11 = (f32[1,15,32,128]{3,2,1,0:T(8,128)S(1)}, f32[1,15,32,128]{3,2,1,0:T(8,128)S(1)}, u32[]{:S(2)}, u32[]{:S(2)}) collective-permute-start(f32[1,15,32,128]{3,2,1,0:T(8,128)S(1)} %get-tuple-element.68.refs_3_), channel_id=1, source_target_pairs={{0,8},{8,0},{16,24},{24,16},{1,9},{9,1},{17,25},{25,17},{2,10},{10... | collective-permute-start | bytes 737288 | tf_op jit(solution)/shard_map/ppermute | solution.py:216
  2.5 0.1 pad_add_fusion.refs_0_.parity.place
  2.6 0.0 copy-done.2
  2.6 0.0 copy-done.4
  2.6 0.6 mask_profiles.1
  3.2 1.0 %collective-permute-start.2 = (f32[3,4,32,128]{3,2,1,0:T(8,128)S(1)}, f32[3,4,32,128]{3,2,1,0:T(8,128)S(1)}, u32[]{:S(2)}, u32[]{:S(2)}) collective-permute-start(f32[3,4,32,128]{3,2,1,0:T(8,128)S(1)} %get-tuple-element.36), channel_id=1, source_target_pairs={{0,1},{1,0},{2,3},{3,2},{4,5},{5,4},{6,7},{7,6},{8,9},{9,8},{10,11... | collective-permute-start | bytes 589832 | tf_op jit(solution)/shard_map/ppermute | solution.py:382
  4.2 2.1 %collective-permute-start.12 = (f32[1,15,32,128]{3,2,1,0:T(8,128)S(1)}, f32[1,15,32,128]{3,2,1,0:T(8,128)S(1)}, u32[]{:S(2)}, u32[]{:S(2)}) collective-permute-start(f32[1,15,32,128]{3,2,1,0:T(8,128)S(1)} %get-tuple-element.67), channel_id=1, source_target_pairs={{8,16},{16,8},{9,17},{17,9},{10,18},{18,10},{11,19},{19,11},{12,20... | collective-permute-start | bytes 737288 | tf_op jit(solution)/shard_map/ppermute | solution.py:216
  6.4 0.0 copy-start.1
  6.4 0.1 collective-permute-start
  6.5 4.2 %collective-permute-start.1 = (f32[1,15,32,128]{3,2,1,0:T(8,128)S(1)}, f32[1,15,32,128]{3,2,1,0:T(8,128)S(1)}, u32[]{:S(2)}, u32[]{:S(2)}) collective-permute-start(f32[1,15,32,128]{3,2,1,0:T(8,128)S(1)} %get-tuple-element.69), channel_id=1, source_target_pairs={{8,16},{16,8},{9,17},{17,9},{10,18},{18,10},{11,19},{19,11},{12,20... | collective-permute-start | bytes 737288 | tf_op jit(solution)/shard_map/ppermute | solution.py:216
  10.7 0.0 collective-permute-done.2.refs_2_
  10.7 0.6 halve_profiles2.1
  11.3 0.2 collective-permute-start.3
  11.5 0.0 copy-done.3
  11.5 2.3 %matrices.1 = (bf16[48,144]{1,0:T(8,128)(2,1)S(1)}, bf16[48,144]{1,0:T(8,128)(2,1)S(1)}, bf16[3,32,192]{2,1,0:T(8,128)(2,1)S(1)}, bf16[3,64,96]{2,1,0:T(8,128)(2...) custom-call(f32[3,3,31]{2,1,0:T(4,128)S(1)} %copy-done.3, ...), custom_call_target="tpu_custom_call" | custom-call | tf_op jit(solution)/shard_map/matrices/pallas_call | solution.py:94
  13.8 1.3 %collective-permute-done.3.refs_2_ = f32[3,2,32,128]{3,2,1,0:T(8,128)S(1)} collective-permute-done((f32[3,2,32,128]{3,2,1,0:T(8,128)S(1)}, f32[3,2,32,128]{3,2,1,0:T(8,128)S(1)}, u32[]{:S(2)}, u32[]{:S(2)}) %collective-permute-start.3) | collective-permute-done | bytes 98336 | tf_op jit(solution)/shard_map/ppermute | solution.py:382
  15.1 0.6 halve_profiles4.1
  15.7 2.4 %collective-permute-start.4 = (f32[3,1,32,128]{3,2,0,1:T(8,128)S(1)}, f32[3,1,32,128]{3,2,0,1:T(8,128)S(1)}, u32[]{:S(2)}, u32[]{:S(2)}) collective-permute-start(f32[3,1,32,128]{3,2,0,1:T(8,128)S(1)} %bitcast.11), channel_id=1, source_target_pairs={{0,4},{1,5},{2,6},{3,7},{4,0},{5,1},{6,2},{7,3},{8,12},{9,13},{10,... | collective-permute-start | bytes 147464 | tf_op jit(solution)/shard_map/ppermute | solution.py:382
  18.0 0.0 collective-permute-done.11.refs_2_.xa
  18.1 0.0 collective-permute-done.12.refs_3_.xb
  18.1 0.0 copy-done
  18.1 0.6 pack_rows0.1
  18.7 1.8 %collective-permute-start.13 = (f32[1,46,16,128]{3,2,1,0:T(8,128)S(1)}, f32[1,46,16,128]{3,2,1,0:T(8,128)S(1)}, u32[]{:S(2)}, u32[]{:S(2)}) collective-permute-start(f32[1,46,16,128]{3,2,1,0:T(8,128)S(1)} %get-tuple-element.56), channel_id=1, source_target_pairs={{0,1},{1,0},{2,3},{3,2},{4,5},{5,4},{6,7},{7,6},{8,9},{9,8},{10,11... | collective-permute-start | bytes 1130504 | tf_op jit(solution)/shard_map/ppermute | solution.py:216
  20.5 1.9 %collective-permute-start.14 = (f32[1,46,16,128]{3,2,1,0:T(8,128)S(1)}, f32[1,46,16,128]{3,2,1,0:T(8,128)S(1)}, u32[]{:S(2)}, u32[]{:S(2)}) collective-permute-start(f32[1,46,16,128]{3,2,1,0:T(8,128)S(1)} %get-tuple-element.57), channel_id=1, source_target_pairs={{1,2},{2,1},{3,4},{4,3},{5,6},{6,5},{9,10},{10,9},{11,12},{12,11},... | collective-permute-start | bytes 1130504 | tf_op jit(solution)/shard_map/ppermute | solution.py:216
  22.4 0.0 collective-permute-done.refs_2_.xa
  22.4 2.7 %collective-permute-done.1.refs_3_.xb = f32[1,15,32,128]{3,2,1,0:T(8,128)S(1)} collective-permute-done((f32[1,15,32,128]{3,2,1,0:T(8,128)S(1)}, f32[1,15,32,128]{3,2,1,0:T(8,128)S(1)}, u32[]{:S(2)}, u32[]{:S(2)}) %collective-permute-start.1) | collective-permute-done | bytes 245792 | tf_op jit(solution)/shard_map/ppermute | solution.py:216
  25.1 0.0 collective-permute-done.4
  25.1 0.6 pack_rows1.1
  25.7 0.9 %collective-permute-start.5 = (f32[1,46,16,128]{3,2,1,0:T(8,128)S(1)}, f32[1,46,16,128]{3,2,1,0:T(8,128)S(1)}, u32[]{:S(2)}, u32[]{:S(2)}) collective-permute-start(f32[1,46,16,128]{3,2,1,0:T(8,128)S(1)} %get-tuple-element.41), channel_id=1, source_target_pairs={{0,1},{1,0},{2,3},{3,2},{4,5},{5,4},{6,7},{7,6},{8,9},{9,8},{10,11... | collective-permute-start | bytes 1130504 | tf_op jit(solution)/shard_map/ppermute | solution.py:216
  26.6 3.1 %collective-permute-start.6 = (f32[1,46,16,128]{3,2,1,0:T(8,128)S(1)}, f32[1,46,16,128]{3,2,1,0:T(8,128)S(1)}, u32[]{:S(2)}, u32[]{:S(2)}) collective-permute-start(f32[1,46,16,128]{3,2,1,0:T(8,128)S(1)} %get-tuple-element.42), channel_id=1, source_target_pairs={{1,2},{2,1},{3,4},{4,3},{5,6},{6,5},{9,10},{10,9},{11,12},{12,11},... | collective-permute-start | bytes 1130504 | tf_op jit(solution)/shard_map/ppermute | solution.py:216
  29.7 0.0 collective-permute-done.13.yc
  29.7 0.0 collective-permute-done.14.yd
  29.7 0.0 copy-done.1
  29.7 2.3 %brick0.1 = (f32[1,16,32,128]{3,2,1,0:T(8,128)S(1)}, f32[1,15,32,128]{3,2,1,0:T(8,128)S(1)}, f32[1,15,32,128]{3,2,1,0:T(8,128)S(1)}, f32[1,46,16,128]{3,2,1,0:T(8,128)S(1)}, f32[1,46,16,128]{3,2,1,0:T(8,128)S(1)}) custom-call(f32[2,16,32,128]{3,2,1,0:T(8,128)S(1)} %copy-done, f32[1,15,32,128]{3,2,1,0:T(8,128)S(1)} %collective-permute-done.11.refs_2_.xa, ...), custom_call_target="tpu_custom_call" | custom-call | tf_op jit(solution)/shard_map/brick0/pallas_call | solution.py:192
  32.0 0.1 collective-permute-start.15
  32.1 3.6 %collective-permute-start.16 = (f32[1,46,16,128]{3,2,1,0:T(8,128)S(1)}, f32[1,46,16,128]{3,2,1,0:T(8,128)S(1)}, u32[]{:S(2)}, u32[]{:S(2)}) collective-permute-start(f32[1,46,16,128]{3,2,1,0:T(8,128)S(1)} %get-tuple-element.60), channel_id=1, source_target_pairs={{1,2},{2,1},{3,4},{4,3},{5,6},{6,5},{9,10},{10,9},{11,12},{12,11},... | collective-permute-start | bytes 1130504 | tf_op jit(solution)/shard_map/ppermute | solution.py:216
  35.7 0.0 collective-permute-done.5.yc
  35.7 0.0 collective-permute-done.6.yd
  35.7 2.3 %brick1.1 = (f32[1,16,32,128]{3,2,1,0:T(8,128)S(1)}, f32[1,15,32,128]{3,2,1,0:T(8,128)S(1)}, f32[1,15,32,128]{3,2,1,0:T(8,128)S(1)}, f32[1,46,16,128]{3,2,1,0:T(8,128)S(1)}, f32[1,46,16,128]{3,2,1,0:T(8,128)S(1)}) custom-call(f32[2,16,32,128]{3,2,1,0:T(8,128)S(1)} %copy-done, f32[1,15,32,128]{3,2,1,0:T(8,128)S(1)} %collective-permute-done.refs_2_.xa, ...), custom_call_target="tpu_custom_call" | custom-call | tf_op jit(solution)/shard_map/brick1/pallas_call | solution.py:192
  38.0 0.1 collective-permute-start.7
  38.1 3.3 %collective-permute-start.8 = (f32[1,46,16,128]{3,2,1,0:T(8,128)S(1)}, f32[1,46,16,128]{3,2,1,0:T(8,128)S(1)}, u32[]{:S(2)}, u32[]{:S(2)}) collective-permute-start(f32[1,46,16,128]{3,2,1,0:T(8,128)S(1)} %get-tuple-element.51), channel_id=1, source_target_pairs={{1,2},{2,1},{3,4},{4,3},{5,6},{6,5},{9,10},{10,9},{11,12},{12,11},... | collective-permute-start | bytes 1130504 | tf_op jit(solution)/shard_map/ppermute | solution.py:216
  41.5 0.0 collective-permute-done.15.refs_3_.rc
  41.5 0.0 collective-permute-done.16.refs_4_.rd
  41.5 0.6 add_rows0.1
  42.1 0.1 collective-permute-start.17
  42.2 3.6 %collective-permute-start.18 = (f32[1,15,32,128]{3,2,1,0:T(8,128)S(1)}, f32[1,15,32,128]{3,2,1,0:T(8,128)S(1)}, u32[]{:S(2)}, u32[]{:S(2)}) collective-permute-start(f32[1,15,32,128]{3,2,1,0:T(8,128)S(1)} %get-tuple-element.64), channel_id=1, source_target_pairs={{8,16},{16,8},{9,17},{17,9},{10,18},{18,10},{11,19},{19,11},{12,20... | collective-permute-start | bytes 737288 | tf_op jit(solution)/shard_map/ppermute | solution.py:216
  45.8 0.0 collective-permute-done.7.refs_3_.rc
  45.8 1.6 %collective-permute-done.8.refs_4_.rd = f32[1,46,16,128]{3,2,1,0:T(8,128)S(1)} collective-permute-done((f32[1,46,16,128]{3,2,1,0:T(8,128)S(1)}, f32[1,46,16,128]{3,2,1,0:T(8,128)S(1)}, u32[]{:S(2)}, u32[]{:S(2)}) %collective-permute-start.8) | collective-permute-done | bytes 376864 | tf_op jit(solution)/shard_map/ppermute | solution.py:216
  47.3 0.6 add_rows1.1
  48.0 0.1 collective-permute-start.10
  48.0 3.6 %collective-permute-start.9 = (f32[1,15,32,128]{3,2,1,0:T(8,128)S(1)}, f32[1,15,32,128]{3,2,1,0:T(8,128)S(1)}, u32[]{:S(2)}, u32[]{:S(2)}) collective-permute-start(f32[1,15,32,128]{3,2,1,0:T(8,128)S(1)} %get-tuple-element.54), channel_id=1, source_target_pairs={{8,16},{16,8},{9,17},{17,9},{10,18},{18,10},{11,19},{19,11},{12,20... | collective-permute-start | bytes 737288 | tf_op jit(solution)/shard_map/ppermute | solution.py:216
  51.6 0.0 collective-permute-done.17.qa
  51.6 3.8 %collective-permute-done.18.qb = f32[1,15,32,128]{3,2,1,0:T(8,128)S(1)} collective-permute-done((f32[1,15,32,128]{3,2,1,0:T(8,128)S(1)}, f32[1,15,32,128]{3,2,1,0:T(8,128)S(1)}, u32[]{:S(2)}, u32[]{:S(2)}) %collective-permute-start.18) | collective-permute-done | bytes 245792 | tf_op jit(solution)/shard_map/ppermute | solution.py:216
  55.4 1.4 %finish0.1.rest_0_ = f32[2,16,32,128]{3,2,1,0:T(8,128)} custom-call(s32[2]{0:T(128)S(1)} %pad_add_fusion.refs_0_.parity.place, f32[2,16,32,128]{3,2,1,0:T(8,128)S(1)} %copy-done, f32[1,16,32,128]{3,2,1,0:T(8,128)S(1)} %get-tuple-element.58.s_own, f32[1,46,16,128]{3,2,1,0:T(8,128)S(1)} %collective-permute-done.15.refs_3_.rc, ...), custom_call_target="tpu_custom_call" | custom-call | tf_op jit(solution)/shard_map/finish0/pallas_call | solution.py:366
  56.8 1.5 %collective-permute-done.10.qb = f32[1,15,32,128]{3,2,1,0:T(8,128)S(1)} collective-permute-done((f32[1,15,32,128]{3,2,1,0:T(8,128)S(1)}, f32[1,15,32,128]{3,2,1,0:T(8,128)S(1)}, u32[]{:S(2)}, u32[]{:S(2)}) %collective-permute-start.10) | collective-permute-done | bytes 245792 | tf_op jit(solution)/shard_map/ppermute | solution.py:216
  58.3 7.6 %collective-permute-done.9.qa = f32[1,15,32,128]{3,2,1,0:T(8,128)S(1)} collective-permute-done((f32[1,15,32,128]{3,2,1,0:T(8,128)S(1)}, f32[1,15,32,128]{3,2,1,0:T(8,128)S(1)}, u32[]{:S(2)}, u32[]{:S(2)}) %collective-permute-start.9) | collective-permute-done | bytes 245792 | tf_op jit(solution)/shard_map/ppermute | solution.py:216
  65.9 1.4 %finish1.1 = f32[2,16,32,128]{3,2,1,0:T(8,128)} custom-call(s32[2]{0:T(128)S(1)} %pad_add_fusion.refs_0_.parity.place, f32[2,16,32,128]{3,2,1,0:T(8,128)S(1)} %copy-done, f32[1,16,32,128]{3,2,1,0:T(8,128)S(1)} %get-tuple-element.49.s_own, f32[1,46,16,128]{3,2,1,0:T(8,128)S(1)} %collective-permute-done.7.refs_3_.rc, ...), custom_call_target="tpu_custom_call", output_to_operand_aliasing={{}: (7, {})} | custom-call | tf_op jit(solution)/shard_map/finish1/pallas_call | solution.py:366
  (2 shorter events, 0.1 us)
Async XLA Ops:
  0.0 2.6 %copy-start.2 = (f32[1,1,3,256,128]{4,3,2,1,0:T(8,128)S(1)}, f32[1,1,3,256,128]{4,3,2,1,0:T(8,128)}, u32[]{:S(2)}) copy-start(f32[1,1,3,256,128]{4,3,2,1,0:T(8,128)} %refs_2_.1) | copy-start | bytes 1179652
  0.0 2.6 %copy-start.4 = (s32[3,4]{1,0:T(4,128)S(1)}, s32[3,4]{1,0:T(4,128)}, u32[]{:S(2)}) copy-start(s32[3,4]{1,0:T(4,128)} %refs_1_.3) | copy-start | bytes 148
  1.1 10.4 %copy-start.3 = (f32[3,3,31]{2,1,0:T(4,128)S(1)}, f32[3,3,31]{2,1,0:T(4,128)}, u32[]{:S(2)}) copy-start(f32[3,3,31]{2,1,0:T(4,128)} %rest_1_.1) | copy-start | bytes 3352
  1.1 16.9 %copy-start = (f32[2,16,32,128]{3,2,1,0:T(8,128)S(1)}, f32[2,16,32,128]{3,2,1,0:T(8,128)}, u32[]{:S(2)}) copy-start(f32[2,16,32,128]{3,2,1,0:T(8,128)} %estimate.3) | copy-start | bytes 1572868
  1.2 16.8 %collective-permute-start.11 = (f32[1,15,32,128]{3,2,1,0:T(8,128)S(1)}, f32[1,15,32,128]{3,2,1,0:T(8,128)S(1)}, u32[]{:S(2)}, u32[]{:S(2)}) collective-permute-start(f32[1,15,32,128]{3,2,1,0:T(8,128)S(1)} %get-tuple-element.68.refs_3_), channel_id=1, source_target_pairs={{0,8},{8,0},{16,24},{24,16},{1,9},{9,1},{17,25},{25,17},{2,10},{10... | collective-permute-start | bytes 737288 | tf_op jit(solution)/shard_map/ppermute | solution.py:216
  3.2 7.5 %collective-permute-start.2 = (f32[3,4,32,128]{3,2,1,0:T(8,128)S(1)}, f32[3,4,32,128]{3,2,1,0:T(8,128)S(1)}, u32[]{:S(2)}, u32[]{:S(2)}) collective-permute-start(f32[3,4,32,128]{3,2,1,0:T(8,128)S(1)} %get-tuple-element.36), channel_id=1, source_target_pairs={{0,1},{1,0},{2,3},{3,2},{4,5},{5,4},{6,7},{7,6},{8,9},{9,8},{10,11... | collective-permute-start | bytes 589832 | tf_op jit(solution)/shard_map/ppermute | solution.py:382
  4.2 13.8 %collective-permute-start.12 = (f32[1,15,32,128]{3,2,1,0:T(8,128)S(1)}, f32[1,15,32,128]{3,2,1,0:T(8,128)S(1)}, u32[]{:S(2)}, u32[]{:S(2)}) collective-permute-start(f32[1,15,32,128]{3,2,1,0:T(8,128)S(1)} %get-tuple-element.67), channel_id=1, source_target_pairs={{8,16},{16,8},{9,17},{17,9},{10,18},{18,10},{11,19},{19,11},{12,20... | collective-permute-start | bytes 737288 | tf_op jit(solution)/shard_map/ppermute | solution.py:216
  6.4 23.3 %copy-start.1 = (f32[3,2,16,32,128]{4,3,2,1,0:T(8,128)S(1)}, f32[3,2,16,32,128]{4,3,2,1,0:T(8,128)}, u32[]{:S(2)}) copy-start(f32[3,2,16,32,128]{4,3,2,1,0:T(8,128)} %views.3) | copy-start | bytes 4718596
  6.4 16.0 %collective-permute-start = (f32[1,15,32,128]{3,2,1,0:T(8,128)S(1)}, f32[1,15,32,128]{3,2,1,0:T(8,128)S(1)}, u32[]{:S(2)}, u32[]{:S(2)}) collective-permute-start(f32[1,15,32,128]{3,2,1,0:T(8,128)S(1)} %get-tuple-element.70), channel_id=1, source_target_pairs={{0,8},{8,0},{16,24},{24,16},{1,9},{9,1},{17,25},{25,17},{2,10},{10... | collective-permute-start | bytes 737288 | tf_op jit(solution)/shard_map/ppermute | solution.py:216
  6.5 18.6 %collective-permute-start.1 = (f32[1,15,32,128]{3,2,1,0:T(8,128)S(1)}, f32[1,15,32,128]{3,2,1,0:T(8,128)S(1)}, u32[]{:S(2)}, u32[]{:S(2)}) collective-permute-start(f32[1,15,32,128]{3,2,1,0:T(8,128)S(1)} %get-tuple-element.69), channel_id=1, source_target_pairs={{8,16},{16,8},{9,17},{17,9},{10,18},{18,10},{11,19},{19,11},{12,20... | collective-permute-start | bytes 737288 | tf_op jit(solution)/shard_map/ppermute | solution.py:216
  11.3 3.8 %collective-permute-start.3 = (f32[3,2,32,128]{3,2,1,0:T(8,128)S(1)}, f32[3,2,32,128]{3,2,1,0:T(8,128)S(1)}, u32[]{:S(2)}, u32[]{:S(2)}) collective-permute-start(f32[3,2,32,128]{3,2,1,0:T(8,128)S(1)} %get-tuple-element.38._), channel_id=1, source_target_pairs={{0,2},{1,3},{2,0},{3,1},{4,6},{5,7},{6,4},{7,5},{8,10},{9,11},{10,... | collective-permute-start | bytes 294920 | tf_op jit(solution)/shard_map/ppermute | solution.py:382
  15.7 9.4 %collective-permute-start.4 = (f32[3,1,32,128]{3,2,0,1:T(8,128)S(1)}, f32[3,1,32,128]{3,2,0,1:T(8,128)S(1)}, u32[]{:S(2)}, u32[]{:S(2)}) collective-permute-start(f32[3,1,32,128]{3,2,0,1:T(8,128)S(1)} %bitcast.11), channel_id=1, source_target_pairs={{0,4},{1,5},{2,6},{3,7},{4,0},{5,1},{6,2},{7,3},{8,12},{9,13},{10,... | collective-permute-start | bytes 147464 | tf_op jit(solution)/shard_map/ppermute | solution.py:382
  18.7 11.0 %collective-permute-start.13 = (f32[1,46,16,128]{3,2,1,0:T(8,128)S(1)}, f32[1,46,16,128]{3,2,1,0:T(8,128)S(1)}, u32[]{:S(2)}, u32[]{:S(2)}) collective-permute-start(f32[1,46,16,128]{3,2,1,0:T(8,128)S(1)} %get-tuple-element.56), channel_id=1, source_target_pairs={{0,1},{1,0},{2,3},{3,2},{4,5},{5,4},{6,7},{7,6},{8,9},{9,8},{10,11... | collective-permute-start | bytes 1130504 | tf_op jit(solution)/shard_map/ppermute | solution.py:216
  20.5 9.2 %collective-permute-start.14 = (f32[1,46,16,128]{3,2,1,0:T(8,128)S(1)}, f32[1,46,16,128]{3,2,1,0:T(8,128)S(1)}, u32[]{:S(2)}, u32[]{:S(2)}) collective-permute-start(f32[1,46,16,128]{3,2,1,0:T(8,128)S(1)} %get-tuple-element.57), channel_id=1, source_target_pairs={{1,2},{2,1},{3,4},{4,3},{5,6},{6,5},{9,10},{10,9},{11,12},{12,11},... | collective-permute-start | bytes 1130504 | tf_op jit(solution)/shard_map/ppermute | solution.py:216
  25.7 10.0 %collective-permute-start.5 = (f32[1,46,16,128]{3,2,1,0:T(8,128)S(1)}, f32[1,46,16,128]{3,2,1,0:T(8,128)S(1)}, u32[]{:S(2)}, u32[]{:S(2)}) collective-permute-start(f32[1,46,16,128]{3,2,1,0:T(8,128)S(1)} %get-tuple-element.41), channel_id=1, source_target_pairs={{0,1},{1,0},{2,3},{3,2},{4,5},{5,4},{6,7},{7,6},{8,9},{9,8},{10,11... | collective-permute-start | bytes 1130504 | tf_op jit(solution)/shard_map/ppermute | solution.py:216
  26.6 9.1 %collective-permute-start.6 = (f32[1,46,16,128]{3,2,1,0:T(8,128)S(1)}, f32[1,46,16,128]{3,2,1,0:T(8,128)S(1)}, u32[]{:S(2)}, u32[]{:S(2)}) collective-permute-start(f32[1,46,16,128]{3,2,1,0:T(8,128)S(1)} %get-tuple-element.42), channel_id=1, source_target_pairs={{1,2},{2,1},{3,4},{4,3},{5,6},{6,5},{9,10},{10,9},{11,12},{12,11},... | collective-permute-start | bytes 1130504 | tf_op jit(solution)/shard_map/ppermute | solution.py:216
  32.0 9.4 %collective-permute-start.15 = (f32[1,46,16,128]{3,2,1,0:T(8,128)S(1)}, f32[1,46,16,128]{3,2,1,0:T(8,128)S(1)}, u32[]{:S(2)}, u32[]{:S(2)}) collective-permute-start(f32[1,46,16,128]{3,2,1,0:T(8,128)S(1)} %get-tuple-element.59), channel_id=1, source_target_pairs={{0,1},{1,0},{2,3},{3,2},{4,5},{5,4},{6,7},{7,6},{8,9},{9,8},{10,11... | collective-permute-start | bytes 1130504 | tf_op jit(solution)/shard_map/ppermute | solution.py:216
  32.1 9.4 %collective-permute-start.16 = (f32[1,46,16,128]{3,2,1,0:T(8,128)S(1)}, f32[1,46,16,128]{3,2,1,0:T(8,128)S(1)}, u32[]{:S(2)}, u32[]{:S(2)}) collective-permute-start(f32[1,46,16,128]{3,2,1,0:T(8,128)S(1)} %get-tuple-element.60), channel_id=1, source_target_pairs={{1,2},{2,1},{3,4},{4,3},{5,6},{6,5},{9,10},{10,9},{11,12},{12,11},... | collective-permute-start | bytes 1130504 | tf_op jit(solution)/shard_map/ppermute | solution.py:216
  38.0 7.7 %collective-permute-start.7 = (f32[1,46,16,128]{3,2,1,0:T(8,128)S(1)}, f32[1,46,16,128]{3,2,1,0:T(8,128)S(1)}, u32[]{:S(2)}, u32[]{:S(2)}) collective-permute-start(f32[1,46,16,128]{3,2,1,0:T(8,128)S(1)} %get-tuple-element.50), channel_id=1, source_target_pairs={{0,1},{1,0},{2,3},{3,2},{4,5},{5,4},{6,7},{7,6},{8,9},{9,8},{10,11... | collective-permute-start | bytes 1130504 | tf_op jit(solution)/shard_map/ppermute | solution.py:216
  38.1 9.2 %collective-permute-start.8 = (f32[1,46,16,128]{3,2,1,0:T(8,128)S(1)}, f32[1,46,16,128]{3,2,1,0:T(8,128)S(1)}, u32[]{:S(2)}, u32[]{:S(2)}) collective-permute-start(f32[1,46,16,128]{3,2,1,0:T(8,128)S(1)} %get-tuple-element.51), channel_id=1, source_target_pairs={{1,2},{2,1},{3,4},{4,3},{5,6},{6,5},{9,10},{10,9},{11,12},{12,11},... | collective-permute-start | bytes 1130504 | tf_op jit(solution)/shard_map/ppermute | solution.py:216
  42.1 9.5 %collective-permute-start.17 = (f32[1,15,32,128]{3,2,1,0:T(8,128)S(1)}, f32[1,15,32,128]{3,2,1,0:T(8,128)S(1)}, u32[]{:S(2)}, u32[]{:S(2)}) collective-permute-start(f32[1,15,32,128]{3,2,1,0:T(8,128)S(1)} %get-tuple-element.63), channel_id=1, source_target_pairs={{0,8},{8,0},{16,24},{24,16},{1,9},{9,1},{17,25},{25,17},{2,10},{10... | collective-permute-start | bytes 737288 | tf_op jit(solution)/shard_map/ppermute | solution.py:216
  42.2 13.2 %collective-permute-start.18 = (f32[1,15,32,128]{3,2,1,0:T(8,128)S(1)}, f32[1,15,32,128]{3,2,1,0:T(8,128)S(1)}, u32[]{:S(2)}, u32[]{:S(2)}) collective-permute-start(f32[1,15,32,128]{3,2,1,0:T(8,128)S(1)} %get-tuple-element.64), channel_id=1, source_target_pairs={{8,16},{16,8},{9,17},{17,9},{10,18},{18,10},{11,19},{19,11},{12,20... | collective-permute-start | bytes 737288 | tf_op jit(solution)/shard_map/ppermute | solution.py:216
  48.0 10.3 %collective-permute-start.10 = (f32[1,15,32,128]{3,2,1,0:T(8,128)S(1)}, f32[1,15,32,128]{3,2,1,0:T(8,128)S(1)}, u32[]{:S(2)}, u32[]{:S(2)}) collective-permute-start(f32[1,15,32,128]{3,2,1,0:T(8,128)S(1)} %get-tuple-element.55), channel_id=1, source_target_pairs={{0,8},{8,0},{16,24},{24,16},{1,9},{9,1},{17,25},{25,17},{2,10},{10... | collective-permute-start | bytes 737288 | tf_op jit(solution)/shard_map/ppermute | solution.py:216
  48.0 17.9 %collective-permute-start.9 = (f32[1,15,32,128]{3,2,1,0:T(8,128)S(1)}, f32[1,15,32,128]{3,2,1,0:T(8,128)S(1)}, u32[]{:S(2)}, u32[]{:S(2)}) collective-permute-start(f32[1,15,32,128]{3,2,1,0:T(8,128)S(1)} %get-tuple-element.54), channel_id=1, source_target_pairs={{8,16},{16,8},{9,17},{17,9},{10,18},{18,10},{11,19},{19,11},{12,20... | collective-permute-start | bytes 737288 | tf_op jit(solution)/shard_map/ppermute | solution.py:216

commit v5 on v4

--- a/solution.py
+++ b/solution.py
@@ -352,13 +352,19 @@
         if channel == 1:
             qa, qb = qb, qa
         out = rest[-1]
-        out[...] = s_own[...]
-        for got, rows in zip((rc, rd), row_starts(place, width)):
-            out[0, :, rows, :] += got[0]
-        odd = place[0] % 2
-        out[0, pl.ds((planes - reach) * (1 - odd), reach)] += qa[0]
-        out[0, pl.ds((planes - reach) * odd, reach)] += qb[0]
-        out[...] = estimate[...] * out[...] / views
+        odd, cross = place[0] % 2, place[1] % 2 == 1
+        gap = planes - reach
+        for i in range(planes):
+            total = s_own[0, i]
+            low = jnp.where(cross, rc[0, i], rd[0, i])
+            high = jnp.where(cross, rd[0, i], rc[0, i])
+            total = total + jnp.concatenate([low, high], axis=0)
+            for got, start in ((qa, gap * (1 - odd)), (qb, gap * odd)):
+                at = i - start
+                inside = jnp.logical_and(at >= 0, at < reach)
+                value = got[0, jnp.clip(at, 0, reach - 1)]
+                total = total + jnp.where(inside, value, 0.0)
+            out[0, i] = estimate[0, i] * total / views
 
     more = [] if done is None else [done]
     ends = [qb, qa] if channel == 1 else [qa, qb]

time: 67.6 us -> 67.6 us (level)
  no operation moved by 1% of the time
where the time goes in v5:
time: 67.6 us; the launch traced here: 67.3 us
  starting transfers between devices  33.3 us (49%)
  waiting for transfers between devices  18.5 us (27%)
  Pallas kernels  13.8 us (20%)
  local copies, waits for them, and re-layouts  1.22 us (2%)
    ppermute x16, starting transfers between devices, trade(): return lax.ppermute(value, axis, pairs)  29.6 us
    ppermute x16, waiting for transfers between devices, trade(): return lax.ppermute(value, axis, pairs)  17.3 us
    pallas_call x2, Pallas kernels, brick(): pl.pallas_call(fused, grid=(1,), out_shape=[jax.ShapeDtypeStruct(s, F32)...  4.62 us
    pallas_call x7, Pallas kernels, call(): return out(*[array for _, array in ins], *deps)  4.23 us
    ppermute x3, starting transfers between devices, flip(): lax.ppermute(value, axis, [(i, i ^ step) for i in range(lax.axis_size(axi...  3.63 us
    pallas_call x2, Pallas kernels, finish(): pl.pallas_call(body, grid=(1,), out_shape=jax.ShapeDtypeStruct(estimate.s...  2.67 us
    pallas_call x1, Pallas kernels, bands(): pl.pallas_call(matrices, out_shape=[jax.ShapeDtypeStruct(s, BF16) for s i...  2.3 us
  transfers between devices with their start and end apart: 19, of which 6 were waited for; matrix products, arithmetic and copies ran while one was open for 0% of the time, Pallas kernels for 19%

profile of v5, /device:TPU:13, one launch (start us, length us, event | category | flops | bytes accessed | tf_op | source)
XLA Modules:
  0.0 67.3 jit_solution(15425258136798890755)
XLA Ops:
  0.0 0.0 copy-start.2
  0.0 0.0 copy-start.4
  0.0 1.1 %fusion = (f32[1,16,32,128]{3,2,1,0:T(8,128)S(1)}, f32[1,16,32,128]{3,2,1,0:T(8,128)S(1)}) fusion(f32[2,16,32,128]{3,2,1,0:T(8,128)} %estimate.3), kind=kLoop, calls=%fused_computation.5 | loop fusion | bytes 1048576 | tf_op jit(solution)/shard_map/slice | solution.py:400
  1.1 0.0 copy-start.3
  1.1 0.0 copy-start
  1.2 1.3 %collective-permute-start.11 = (f32[1,15,32,128]{3,2,1,0:T(8,128)S(1)}, f32[1,15,32,128]{3,2,1,0:T(8,128)S(1)}, u32[]{:S(2)}, u32[]{:S(2)}) collective-permute-start(f32[1,15,32,128]{3,2,1,0:T(8,128)S(1)} %get-tuple-element.68.refs_3_), channel_id=1, source_target_pairs={{0,8},{8,0},{16,24},{24,16},{1,9},{9,1},{17,25},{25,17},{2,10},{10... | collective-permute-start | bytes 737288 | tf_op jit(solution)/shard_map/ppermute | solution.py:216
  2.5 0.1 pad_add_fusion.refs_0_.parity.place
  2.6 0.0 copy-done.2
  2.6 0.0 copy-done.4
  2.6 0.6 mask_profiles.1
  3.2 1.0 %collective-permute-start.2 = (f32[3,4,32,128]{3,2,1,0:T(8,128)S(1)}, f32[3,4,32,128]{3,2,1,0:T(8,128)S(1)}, u32[]{:S(2)}, u32[]{:S(2)}) collective-permute-start(f32[3,4,32,128]{3,2,1,0:T(8,128)S(1)} %get-tuple-element.36), channel_id=1, source_target_pairs={{0,1},{1,0},{2,3},{3,2},{4,5},{5,4},{6,7},{7,6},{8,9},{9,8},{10,11... | collective-permute-start | bytes 589832 | tf_op jit(solution)/shard_map/ppermute | solution.py:388
  4.2 2.1 %collective-permute-start.12 = (f32[1,15,32,128]{3,2,1,0:T(8,128)S(1)}, f32[1,15,32,128]{3,2,1,0:T(8,128)S(1)}, u32[]{:S(2)}, u32[]{:S(2)}) collective-permute-start(f32[1,15,32,128]{3,2,1,0:T(8,128)S(1)} %get-tuple-element.67), channel_id=1, source_target_pairs={{8,16},{16,8},{9,17},{17,9},{10,18},{18,10},{11,19},{19,11},{12,20... | collective-permute-start | bytes 737288 | tf_op jit(solution)/shard_map/ppermute | solution.py:216
  6.4 0.0 copy-start.1
  6.4 0.1 collective-permute-start
  6.5 4.2 %collective-permute-start.1 = (f32[1,15,32,128]{3,2,1,0:T(8,128)S(1)}, f32[1,15,32,128]{3,2,1,0:T(8,128)S(1)}, u32[]{:S(2)}, u32[]{:S(2)}) collective-permute-start(f32[1,15,32,128]{3,2,1,0:T(8,128)S(1)} %get-tuple-element.69), channel_id=1, source_target_pairs={{8,16},{16,8},{9,17},{17,9},{10,18},{18,10},{11,19},{19,11},{12,20... | collective-permute-start | bytes 737288 | tf_op jit(solution)/shard_map/ppermute | solution.py:216
  10.7 0.0 collective-permute-done.2.refs_2_
  10.7 0.6 halve_profiles2.1
  11.3 0.2 collective-permute-start.3
  11.5 0.0 copy-done.3
  11.5 2.3 %matrices.1 = (bf16[48,144]{1,0:T(8,128)(2,1)S(1)}, bf16[48,144]{1,0:T(8,128)(2,1)S(1)}, bf16[3,32,192]{2,1,0:T(8,128)(2,1)S(1)}, bf16[3,64,96]{2,1,0:T(8,128)(2...) custom-call(f32[3,3,31]{2,1,0:T(4,128)S(1)} %copy-done.3, ...), custom_call_target="tpu_custom_call" | custom-call | tf_op jit(solution)/shard_map/matrices/pallas_call | solution.py:94
  13.8 1.3 %collective-permute-done.3.refs_2_ = f32[3,2,32,128]{3,2,1,0:T(8,128)S(1)} collective-permute-done((f32[3,2,32,128]{3,2,1,0:T(8,128)S(1)}, f32[3,2,32,128]{3,2,1,0:T(8,128)S(1)}, u32[]{:S(2)}, u32[]{:S(2)}) %collective-permute-start.3) | collective-permute-done | bytes 98336 | tf_op jit(solution)/shard_map/ppermute | solution.py:388
  15.1 0.6 halve_profiles4.1
  15.7 2.4 %collective-permute-start.4 = (f32[3,1,32,128]{3,2,0,1:T(8,128)S(1)}, f32[3,1,32,128]{3,2,0,1:T(8,128)S(1)}, u32[]{:S(2)}, u32[]{:S(2)}) collective-permute-start(f32[3,1,32,128]{3,2,0,1:T(8,128)S(1)} %bitcast.11), channel_id=1, source_target_pairs={{0,4},{1,5},{2,6},{3,7},{4,0},{5,1},{6,2},{7,3},{8,12},{9,13},{10,... | collective-permute-start | bytes 147464 | tf_op jit(solution)/shard_map/ppermute | solution.py:388
  18.0 0.0 collective-permute-done.11.refs_2_.xa
  18.1 0.0 collective-permute-done.12.refs_3_.xb
  18.1 0.0 copy-done
  18.1 0.6 pack_rows0.1
  18.7 1.8 %collective-permute-start.13 = (f32[1,46,16,128]{3,2,1,0:T(8,128)S(1)}, f32[1,46,16,128]{3,2,1,0:T(8,128)S(1)}, u32[]{:S(2)}, u32[]{:S(2)}) collective-permute-start(f32[1,46,16,128]{3,2,1,0:T(8,128)S(1)} %get-tuple-element.56), channel_id=1, source_target_pairs={{0,1},{1,0},{2,3},{3,2},{4,5},{5,4},{6,7},{7,6},{8,9},{9,8},{10,11... | collective-permute-start | bytes 1130504 | tf_op jit(solution)/shard_map/ppermute | solution.py:216
  20.5 1.9 %collective-permute-start.14 = (f32[1,46,16,128]{3,2,1,0:T(8,128)S(1)}, f32[1,46,16,128]{3,2,1,0:T(8,128)S(1)}, u32[]{:S(2)}, u32[]{:S(2)}) collective-permute-start(f32[1,46,16,128]{3,2,1,0:T(8,128)S(1)} %get-tuple-element.57), channel_id=1, source_target_pairs={{1,2},{2,1},{3,4},{4,3},{5,6},{6,5},{9,10},{10,9},{11,12},{12,11},... | collective-permute-start | bytes 1130504 | tf_op jit(solution)/shard_map/ppermute | solution.py:216
  22.4 0.0 collective-permute-done.refs_2_.xa
  22.4 2.7 %collective-permute-done.1.refs_3_.xb = f32[1,15,32,128]{3,2,1,0:T(8,128)S(1)} collective-permute-done((f32[1,15,32,128]{3,2,1,0:T(8,128)S(1)}, f32[1,15,32,128]{3,2,1,0:T(8,128)S(1)}, u32[]{:S(2)}, u32[]{:S(2)}) %collective-permute-start.1) | collective-permute-done | bytes 245792 | tf_op jit(solution)/shard_map/ppermute | solution.py:216
  25.1 0.0 collective-permute-done.4
  25.1 0.6 pack_rows1.1
  25.7 0.9 %collective-permute-start.5 = (f32[1,46,16,128]{3,2,1,0:T(8,128)S(1)}, f32[1,46,16,128]{3,2,1,0:T(8,128)S(1)}, u32[]{:S(2)}, u32[]{:S(2)}) collective-permute-start(f32[1,46,16,128]{3,2,1,0:T(8,128)S(1)} %get-tuple-element.41), channel_id=1, source_target_pairs={{0,1},{1,0},{2,3},{3,2},{4,5},{5,4},{6,7},{7,6},{8,9},{9,8},{10,11... | collective-permute-start | bytes 1130504 | tf_op jit(solution)/shard_map/ppermute | solution.py:216
  26.6 3.1 %collective-permute-start.6 = (f32[1,46,16,128]{3,2,1,0:T(8,128)S(1)}, f32[1,46,16,128]{3,2,1,0:T(8,128)S(1)}, u32[]{:S(2)}, u32[]{:S(2)}) collective-permute-start(f32[1,46,16,128]{3,2,1,0:T(8,128)S(1)} %get-tuple-element.42), channel_id=1, source_target_pairs={{1,2},{2,1},{3,4},{4,3},{5,6},{6,5},{9,10},{10,9},{11,12},{12,11},... | collective-permute-start | bytes 1130504 | tf_op jit(solution)/shard_map/ppermute | solution.py:216
  29.7 0.0 collective-permute-done.13.yc
  29.7 0.0 collective-permute-done.14.yd
  29.7 0.0 copy-done.1
  29.7 2.3 %brick0.1 = (f32[1,16,32,128]{3,2,1,0:T(8,128)S(1)}, f32[1,15,32,128]{3,2,1,0:T(8,128)S(1)}, f32[1,15,32,128]{3,2,1,0:T(8,128)S(1)}, f32[1,46,16,128]{3,2,1,0:T(8,128)S(1)}, f32[1,46,16,128]{3,2,1,0:T(8,128)S(1)}) custom-call(f32[2,16,32,128]{3,2,1,0:T(8,128)S(1)} %copy-done, f32[1,15,32,128]{3,2,1,0:T(8,128)S(1)} %collective-permute-done.11.refs_2_.xa, ...), custom_call_target="tpu_custom_call" | custom-call | tf_op jit(solution)/shard_map/brick0/pallas_call | solution.py:192
  32.0 0.1 collective-permute-start.15
  32.1 3.6 %collective-permute-start.16 = (f32[1,46,16,128]{3,2,1,0:T(8,128)S(1)}, f32[1,46,16,128]{3,2,1,0:T(8,128)S(1)}, u32[]{:S(2)}, u32[]{:S(2)}) collective-permute-start(f32[1,46,16,128]{3,2,1,0:T(8,128)S(1)} %get-tuple-element.60), channel_id=1, source_target_pairs={{1,2},{2,1},{3,4},{4,3},{5,6},{6,5},{9,10},{10,9},{11,12},{12,11},... | collective-permute-start | bytes 1130504 | tf_op jit(solution)/shard_map/ppermute | solution.py:216
  35.7 0.0 collective-permute-done.5.yc
  35.7 0.0 collective-permute-done.6.yd
  35.7 2.3 %brick1.1 = (f32[1,16,32,128]{3,2,1,0:T(8,128)S(1)}, f32[1,15,32,128]{3,2,1,0:T(8,128)S(1)}, f32[1,15,32,128]{3,2,1,0:T(8,128)S(1)}, f32[1,46,16,128]{3,2,1,0:T(8,128)S(1)}, f32[1,46,16,128]{3,2,1,0:T(8,128)S(1)}) custom-call(f32[2,16,32,128]{3,2,1,0:T(8,128)S(1)} %copy-done, f32[1,15,32,128]{3,2,1,0:T(8,128)S(1)} %collective-permute-done.refs_2_.xa, ...), custom_call_target="tpu_custom_call" | custom-call | tf_op jit(solution)/shard_map/brick1/pallas_call | solution.py:192
  38.0 0.1 collective-permute-start.7
  38.1 3.3 %collective-permute-start.8 = (f32[1,46,16,128]{3,2,1,0:T(8,128)S(1)}, f32[1,46,16,128]{3,2,1,0:T(8,128)S(1)}, u32[]{:S(2)}, u32[]{:S(2)}) collective-permute-start(f32[1,46,16,128]{3,2,1,0:T(8,128)S(1)} %get-tuple-element.51), channel_id=1, source_target_pairs={{1,2},{2,1},{3,4},{4,3},{5,6},{6,5},{9,10},{10,9},{11,12},{12,11},... | collective-permute-start | bytes 1130504 | tf_op jit(solution)/shard_map/ppermute | solution.py:216
  41.5 0.0 collective-permute-done.15.refs_3_.rc
  41.5 0.0 collective-permute-done.16.refs_4_.rd
  41.5 0.6 add_rows0.1
  42.1 0.1 collective-permute-start.17
  42.2 3.6 %collective-permute-start.18 = (f32[1,15,32,128]{3,2,1,0:T(8,128)S(1)}, f32[1,15,32,128]{3,2,1,0:T(8,128)S(1)}, u32[]{:S(2)}, u32[]{:S(2)}) collective-permute-start(f32[1,15,32,128]{3,2,1,0:T(8,128)S(1)} %get-tuple-element.64), channel_id=1, source_target_pairs={{8,16},{16,8},{9,17},{17,9},{10,18},{18,10},{11,19},{19,11},{12,20... | collective-permute-start | bytes 737288 | tf_op jit(solution)/shard_map/ppermute | solution.py:216
  45.8 0.0 collective-permute-done.7.refs_3_.rc
  45.8 1.6 %collective-permute-done.8.refs_4_.rd = f32[1,46,16,128]{3,2,1,0:T(8,128)S(1)} collective-permute-done((f32[1,46,16,128]{3,2,1,0:T(8,128)S(1)}, f32[1,46,16,128]{3,2,1,0:T(8,128)S(1)}, u32[]{:S(2)}, u32[]{:S(2)}) %collective-permute-start.8) | collective-permute-done | bytes 376864 | tf_op jit(solution)/shard_map/ppermute | solution.py:216
  47.3 0.6 add_rows1.1
  48.0 0.1 collective-permute-start.10
  48.0 3.6 %collective-permute-start.9 = (f32[1,15,32,128]{3,2,1,0:T(8,128)S(1)}, f32[1,15,32,128]{3,2,1,0:T(8,128)S(1)}, u32[]{:S(2)}, u32[]{:S(2)}) collective-permute-start(f32[1,15,32,128]{3,2,1,0:T(8,128)S(1)} %get-tuple-element.54), channel_id=1, source_target_pairs={{8,16},{16,8},{9,17},{17,9},{10,18},{18,10},{11,19},{19,11},{12,20... | collective-permute-start | bytes 737288 | tf_op jit(solution)/shard_map/ppermute | solution.py:216
  51.6 0.0 collective-permute-done.17.qa
  51.6 3.8 %collective-permute-done.18.qb = f32[1,15,32,128]{3,2,1,0:T(8,128)S(1)} collective-permute-done((f32[1,15,32,128]{3,2,1,0:T(8,128)S(1)}, f32[1,15,32,128]{3,2,1,0:T(8,128)S(1)}, u32[]{:S(2)}, u32[]{:S(2)}) %collective-permute-start.18) | collective-permute-done | bytes 245792 | tf_op jit(solution)/shard_map/ppermute | solution.py:216
  55.4 1.3 %finish0.1.rest_0_ = f32[2,16,32,128]{3,2,1,0:T(8,128)} custom-call(s32[2]{0:T(128)S(1)} %pad_add_fusion.refs_0_.parity.place, f32[2,16,32,128]{3,2,1,0:T(8,128)S(1)} %copy-done, f32[1,16,32,128]{3,2,1,0:T(8,128)S(1)} %get-tuple-element.58.s_own, f32[1,46,16,128]{3,2,1,0:T(8,128)S(1)} %collective-permute-done.15.refs_3_.rc, ...), custom_call_target="tpu_custom_call" | custom-call | tf_op jit(solution)/shard_map/finish0/pallas_call | solution.py:372
  56.7 1.6 %collective-permute-done.10.qb = f32[1,15,32,128]{3,2,1,0:T(8,128)S(1)} collective-permute-done((f32[1,15,32,128]{3,2,1,0:T(8,128)S(1)}, f32[1,15,32,128]{3,2,1,0:T(8,128)S(1)}, u32[]{:S(2)}, u32[]{:S(2)}) %collective-permute-start.10) | collective-permute-done | bytes 245792 | tf_op jit(solution)/shard_map/ppermute | solution.py:216
  58.3 7.6 %collective-permute-done.9.qa = f32[1,15,32,128]{3,2,1,0:T(8,128)S(1)} collective-permute-done((f32[1,15,32,128]{3,2,1,0:T(8,128)S(1)}, f32[1,15,32,128]{3,2,1,0:T(8,128)S(1)}, u32[]{:S(2)}, u32[]{:S(2)}) %collective-permute-start.9) | collective-permute-done | bytes 245792 | tf_op jit(solution)/shard_map/ppermute | solution.py:216
  65.9 1.3 %finish1.1 = f32[2,16,32,128]{3,2,1,0:T(8,128)} custom-call(s32[2]{0:T(128)S(1)} %pad_add_fusion.refs_0_.parity.place, f32[2,16,32,128]{3,2,1,0:T(8,128)S(1)} %copy-done, f32[1,16,32,128]{3,2,1,0:T(8,128)S(1)} %get-tuple-element.49.s_own, f32[1,46,16,128]{3,2,1,0:T(8,128)S(1)} %collective-permute-done.7.refs_3_.rc, ...), custom_call_target="tpu_custom_call", output_to_operand_aliasing={{}: (7, {})} | custom-call | tf_op jit(solution)/shard_map/finish1/pallas_call | solution.py:372
  (2 shorter events, 0.1 us)
Async XLA Ops:
  0.0 2.6 %copy-start.2 = (f32[1,1,3,256,128]{4,3,2,1,0:T(8,128)S(1)}, f32[1,1,3,256,128]{4,3,2,1,0:T(8,128)}, u32[]{:S(2)}) copy-start(f32[1,1,3,256,128]{4,3,2,1,0:T(8,128)} %refs_2_.1) | copy-start | bytes 1179652
  0.0 2.6 %copy-start.4 = (s32[3,4]{1,0:T(4,128)S(1)}, s32[3,4]{1,0:T(4,128)}, u32[]{:S(2)}) copy-start(s32[3,4]{1,0:T(4,128)} %refs_1_.3) | copy-start | bytes 148
  1.1 10.4 %copy-start.3 = (f32[3,3,31]{2,1,0:T(4,128)S(1)}, f32[3,3,31]{2,1,0:T(4,128)}, u32[]{:S(2)}) copy-start(f32[3,3,31]{2,1,0:T(4,128)} %rest_1_.1) | copy-start | bytes 3352
  1.1 16.9 %copy-start = (f32[2,16,32,128]{3,2,1,0:T(8,128)S(1)}, f32[2,16,32,128]{3,2,1,0:T(8,128)}, u32[]{:S(2)}) copy-start(f32[2,16,32,128]{3,2,1,0:T(8,128)} %estimate.3) | copy-start | bytes 1572868
  1.2 16.8 %collective-permute-start.11 = (f32[1,15,32,128]{3,2,1,0:T(8,128)S(1)}, f32[1,15,32,128]{3,2,1,0:T(8,128)S(1)}, u32[]{:S(2)}, u32[]{:S(2)}) collective-permute-start(f32[1,15,32,128]{3,2,1,0:T(8,128)S(1)} %get-tuple-element.68.refs_3_), channel_id=1, source_target_pairs={{0,8},{8,0},{16,24},{24,16},{1,9},{9,1},{17,25},{25,17},{2,10},{10... | collective-permute-start | bytes 737288 | tf_op jit(solution)/shard_map/ppermute | solution.py:216
  3.2 7.5 %collective-permute-start.2 = (f32[3,4,32,128]{3,2,1,0:T(8,128)S(1)}, f32[3,4,32,128]{3,2,1,0:T(8,128)S(1)}, u32[]{:S(2)}, u32[]{:S(2)}) collective-permute-start(f32[3,4,32,128]{3,2,1,0:T(8,128)S(1)} %get-tuple-element.36), channel_id=1, source_target_pairs={{0,1},{1,0},{2,3},{3,2},{4,5},{5,4},{6,7},{7,6},{8,9},{9,8},{10,11... | collective-permute-start | bytes 589832 | tf_op jit(solution)/shard_map/ppermute | solution.py:388
  4.2 13.8 %collective-permute-start.12 = (f32[1,15,32,128]{3,2,1,0:T(8,128)S(1)}, f32[1,15,32,128]{3,2,1,0:T(8,128)S(1)}, u32[]{:S(2)}, u32[]{:S(2)}) collective-permute-start(f32[1,15,32,128]{3,2,1,0:T(8,128)S(1)} %get-tuple-element.67), channel_id=1, source_target_pairs={{8,16},{16,8},{9,17},{17,9},{10,18},{18,10},{11,19},{19,11},{12,20... | collective-permute-start | bytes 737288 | tf_op jit(solution)/shard_map/ppermute | solution.py:216
  6.4 23.3 %copy-start.1 = (f32[3,2,16,32,128]{4,3,2,1,0:T(8,128)S(1)}, f32[3,2,16,32,128]{4,3,2,1,0:T(8,128)}, u32[]{:S(2)}) copy-start(f32[3,2,16,32,128]{4,3,2,1,0:T(8,128)} %views.3) | copy-start | bytes 4718596
  6.4 16.0 %collective-permute-start = (f32[1,15,32,128]{3,2,1,0:T(8,128)S(1)}, f32[1,15,32,128]{3,2,1,0:T(8,128)S(1)}, u32[]{:S(2)}, u32[]{:S(2)}) collective-permute-start(f32[1,15,32,128]{3,2,1,0:T(8,128)S(1)} %get-tuple-element.70), channel_id=1, source_target_pairs={{0,8},{8,0},{16,24},{24,16},{1,9},{9,1},{17,25},{25,17},{2,10},{10... | collective-permute-start | bytes 737288 | tf_op jit(solution)/shard_map/ppermute | solution.py:216
  6.5 18.6 %collective-permute-start.1 = (f32[1,15,32,128]{3,2,1,0:T(8,128)S(1)}, f32[1,15,32,128]{3,2,1,0:T(8,128)S(1)}, u32[]{:S(2)}, u32[]{:S(2)}) collective-permute-start(f32[1,15,32,128]{3,2,1,0:T(8,128)S(1)} %get-tuple-element.69), channel_id=1, source_target_pairs={{8,16},{16,8},{9,17},{17,9},{10,18},{18,10},{11,19},{19,11},{12,20... | collective-permute-start | bytes 737288 | tf_op jit(solution)/shard_map/ppermute | solution.py:216
  11.3 3.8 %collective-permute-start.3 = (f32[3,2,32,128]{3,2,1,0:T(8,128)S(1)}, f32[3,2,32,128]{3,2,1,0:T(8,128)S(1)}, u32[]{:S(2)}, u32[]{:S(2)}) collective-permute-start(f32[3,2,32,128]{3,2,1,0:T(8,128)S(1)} %get-tuple-element.38._), channel_id=1, source_target_pairs={{0,2},{1,3},{2,0},{3,1},{4,6},{5,7},{6,4},{7,5},{8,10},{9,11},{10,... | collective-permute-start | bytes 294920 | tf_op jit(solution)/shard_map/ppermute | solution.py:388
  15.7 9.4 %collective-permute-start.4 = (f32[3,1,32,128]{3,2,0,1:T(8,128)S(1)}, f32[3,1,32,128]{3,2,0,1:T(8,128)S(1)}, u32[]{:S(2)}, u32[]{:S(2)}) collective-permute-start(f32[3,1,32,128]{3,2,0,1:T(8,128)S(1)} %bitcast.11), channel_id=1, source_target_pairs={{0,4},{1,5},{2,6},{3,7},{4,0},{5,1},{6,2},{7,3},{8,12},{9,13},{10,... | collective-permute-start | bytes 147464 | tf_op jit(solution)/shard_map/ppermute | solution.py:388
  18.7 11.0 %collective-permute-start.13 = (f32[1,46,16,128]{3,2,1,0:T(8,128)S(1)}, f32[1,46,16,128]{3,2,1,0:T(8,128)S(1)}, u32[]{:S(2)}, u32[]{:S(2)}) collective-permute-start(f32[1,46,16,128]{3,2,1,0:T(8,128)S(1)} %get-tuple-element.56), channel_id=1, source_target_pairs={{0,1},{1,0},{2,3},{3,2},{4,5},{5,4},{6,7},{7,6},{8,9},{9,8},{10,11... | collective-permute-start | bytes 1130504 | tf_op jit(solution)/shard_map/ppermute | solution.py:216
  20.5 9.2 %collective-permute-start.14 = (f32[1,46,16,128]{3,2,1,0:T(8,128)S(1)}, f32[1,46,16,128]{3,2,1,0:T(8,128)S(1)}, u32[]{:S(2)}, u32[]{:S(2)}) collective-permute-start(f32[1,46,16,128]{3,2,1,0:T(8,128)S(1)} %get-tuple-element.57), channel_id=1, source_target_pairs={{1,2},{2,1},{3,4},{4,3},{5,6},{6,5},{9,10},{10,9},{11,12},{12,11},... | collective-permute-start | bytes 1130504 | tf_op jit(solution)/shard_map/ppermute | solution.py:216
  25.7 10.0 %collective-permute-start.5 = (f32[1,46,16,128]{3,2,1,0:T(8,128)S(1)}, f32[1,46,16,128]{3,2,1,0:T(8,128)S(1)}, u32[]{:S(2)}, u32[]{:S(2)}) collective-permute-start(f32[1,46,16,128]{3,2,1,0:T(8,128)S(1)} %get-tuple-element.41), channel_id=1, source_target_pairs={{0,1},{1,0},{2,3},{3,2},{4,5},{5,4},{6,7},{7,6},{8,9},{9,8},{10,11... | collective-permute-start | bytes 1130504 | tf_op jit(solution)/shard_map/ppermute | solution.py:216
  26.6 9.1 %collective-permute-start.6 = (f32[1,46,16,128]{3,2,1,0:T(8,128)S(1)}, f32[1,46,16,128]{3,2,1,0:T(8,128)S(1)}, u32[]{:S(2)}, u32[]{:S(2)}) collective-permute-start(f32[1,46,16,128]{3,2,1,0:T(8,128)S(1)} %get-tuple-element.42), channel_id=1, source_target_pairs={{1,2},{2,1},{3,4},{4,3},{5,6},{6,5},{9,10},{10,9},{11,12},{12,11},... | collective-permute-start | bytes 1130504 | tf_op jit(solution)/shard_map/ppermute | solution.py:216
  32.0 9.4 %collective-permute-start.15 = (f32[1,46,16,128]{3,2,1,0:T(8,128)S(1)}, f32[1,46,16,128]{3,2,1,0:T(8,128)S(1)}, u32[]{:S(2)}, u32[]{:S(2)}) collective-permute-start(f32[1,46,16,128]{3,2,1,0:T(8,128)S(1)} %get-tuple-element.59), channel_id=1, source_target_pairs={{0,1},{1,0},{2,3},{3,2},{4,5},{5,4},{6,7},{7,6},{8,9},{9,8},{10,11... | collective-permute-start | bytes 1130504 | tf_op jit(solution)/shard_map/ppermute | solution.py:216
  32.1 9.4 %collective-permute-start.16 = (f32[1,46,16,128]{3,2,1,0:T(8,128)S(1)}, f32[1,46,16,128]{3,2,1,0:T(8,128)S(1)}, u32[]{:S(2)}, u32[]{:S(2)}) collective-permute-start(f32[1,46,16,128]{3,2,1,0:T(8,128)S(1)} %get-tuple-element.60), channel_id=1, source_target_pairs={{1,2},{2,1},{3,4},{4,3},{5,6},{6,5},{9,10},{10,9},{11,12},{12,11},... | collective-permute-start | bytes 1130504 | tf_op jit(solution)/shard_map/ppermute | solution.py:216
  38.0 7.7 %collective-permute-start.7 = (f32[1,46,16,128]{3,2,1,0:T(8,128)S(1)}, f32[1,46,16,128]{3,2,1,0:T(8,128)S(1)}, u32[]{:S(2)}, u32[]{:S(2)}) collective-permute-start(f32[1,46,16,128]{3,2,1,0:T(8,128)S(1)} %get-tuple-element.50), channel_id=1, source_target_pairs={{0,1},{1,0},{2,3},{3,2},{4,5},{5,4},{6,7},{7,6},{8,9},{9,8},{10,11... | collective-permute-start | bytes 1130504 | tf_op jit(solution)/shard_map/ppermute | solution.py:216
  38.1 9.2 %collective-permute-start.8 = (f32[1,46,16,128]{3,2,1,0:T(8,128)S(1)}, f32[1,46,16,128]{3,2,1,0:T(8,128)S(1)}, u32[]{:S(2)}, u32[]{:S(2)}) collective-permute-start(f32[1,46,16,128]{3,2,1,0:T(8,128)S(1)} %get-tuple-element.51), channel_id=1, source_target_pairs={{1,2},{2,1},{3,4},{4,3},{5,6},{6,5},{9,10},{10,9},{11,12},{12,11},... | collective-permute-start | bytes 1130504 | tf_op jit(solution)/shard_map/ppermute | solution.py:216
  42.1 9.5 %collective-permute-start.17 = (f32[1,15,32,128]{3,2,1,0:T(8,128)S(1)}, f32[1,15,32,128]{3,2,1,0:T(8,128)S(1)}, u32[]{:S(2)}, u32[]{:S(2)}) collective-permute-start(f32[1,15,32,128]{3,2,1,0:T(8,128)S(1)} %get-tuple-element.63), channel_id=1, source_target_pairs={{0,8},{8,0},{16,24},{24,16},{1,9},{9,1},{17,25},{25,17},{2,10},{10... | collective-permute-start | bytes 737288 | tf_op jit(solution)/shard_map/ppermute | solution.py:216
  42.2 13.2 %collective-permute-start.18 = (f32[1,15,32,128]{3,2,1,0:T(8,128)S(1)}, f32[1,15,32,128]{3,2,1,0:T(8,128)S(1)}, u32[]{:S(2)}, u32[]{:S(2)}) collective-permute-start(f32[1,15,32,128]{3,2,1,0:T(8,128)S(1)} %get-tuple-element.64), channel_id=1, source_target_pairs={{8,16},{16,8},{9,17},{17,9},{10,18},{18,10},{11,19},{19,11},{12,20... | collective-permute-start | bytes 737288 | tf_op jit(solution)/shard_map/ppermute | solution.py:216
  48.0 10.3 %collective-permute-start.10 = (f32[1,15,32,128]{3,2,1,0:T(8,128)S(1)}, f32[1,15,32,128]{3,2,1,0:T(8,128)S(1)}, u32[]{:S(2)}, u32[]{:S(2)}) collective-permute-start(f32[1,15,32,128]{3,2,1,0:T(8,128)S(1)} %get-tuple-element.55), channel_id=1, source_target_pairs={{0,8},{8,0},{16,24},{24,16},{1,9},{9,1},{17,25},{25,17},{2,10},{10... | collective-permute-start | bytes 737288 | tf_op jit(solution)/shard_map/ppermute | solution.py:216
  48.0 17.9 %collective-permute-start.9 = (f32[1,15,32,128]{3,2,1,0:T(8,128)S(1)}, f32[1,15,32,128]{3,2,1,0:T(8,128)S(1)}, u32[]{:S(2)}, u32[]{:S(2)}) collective-permute-start(f32[1,15,32,128]{3,2,1,0:T(8,128)S(1)} %get-tuple-element.54), channel_id=1, source_target_pairs={{8,16},{16,8},{9,17},{17,9},{10,18},{18,10},{11,19},{19,11},{12,20... | collective-permute-start | bytes 737288 | tf_op jit(solution)/shard_map/ppermute | solution.py:216

commit v6 on v5

--- a/solution.py
+++ b/solution.py
@@ -329,11 +329,9 @@
     base = rc.shape[1] - 2 * reach
 
     def body(place, s_xa, s_xb, rc, rd, first, second):
-        first[...] = s_xa[...]
-        second[...] = s_xb[...]
         for got, rows in zip((rc, rd), row_starts(place, width)):
-            first[0, :, rows, :] += got[0, base : base + reach]
-            second[0, :, rows, :] += got[0, base + reach :]
+            first[0, :, rows, :] = s_xa[0, :, rows, :] + got[0, base : base + reach]
+            second[0, :, rows, :] = s_xb[0, :, rows, :] + got[0, base + reach :]
 
     return call(
         body, "add_rows%d" % channel,

time: 67.6 us -> 67.5 us (level)
  no operation moved by 1% of the time
where the time goes in v6:
time: 67.5 us; the launch traced here: 67.2 us
  starting transfers between devices  33.3 us (49%)
  waiting for transfers between devices  18.6 us (28%)
  Pallas kernels  13.8 us (20%)
  local copies, waits for them, and re-layouts  1.22 us (2%)
    ppermute x16, starting transfers between devices, trade(): return lax.ppermute(value, axis, pairs)  29.6 us
    ppermute x16, waiting for transfers between devices, trade(): return lax.ppermute(value, axis, pairs)  17.3 us
    pallas_call x2, Pallas kernels, brick(): pl.pallas_call(fused, grid=(1,), out_shape=[jax.ShapeDtypeStruct(s, F32)...  4.62 us
    pallas_call x7, Pallas kernels, call(): return out(*[array for _, array in ins], *deps)  4.18 us
    ppermute x3, starting transfers between devices, flip(): lax.ppermute(value, axis, [(i, i ^ step) for i in range(lax.axis_size(axi...  3.63 us
    pallas_call x2, Pallas kernels, finish(): pl.pallas_call(body, grid=(1,), out_shape=jax.ShapeDtypeStruct(estimate.s...  2.67 us
    pallas_call x1, Pallas kernels, bands(): pl.pallas_call(matrices, out_shape=[jax.ShapeDtypeStruct(s, BF16) for s i...  2.3 us
  transfers between devices with their start and end apart: 19, of which 6 were waited for; matrix products, arithmetic and copies ran while one was open for 0% of the time, Pallas kernels for 19%

profile of v6, /device:TPU:13, one launch (start us, length us, event | category | flops | bytes accessed | tf_op | source)
XLA Modules:
  0.0 67.2 jit_solution(8772264475028159079)
XLA Ops:
  0.0 0.0 copy-start.2
  0.0 0.0 copy-start.4
  0.0 1.1 %fusion = (f32[1,16,32,128]{3,2,1,0:T(8,128)S(1)}, f32[1,16,32,128]{3,2,1,0:T(8,128)S(1)}) fusion(f32[2,16,32,128]{3,2,1,0:T(8,128)} %estimate.3), kind=kLoop, calls=%fused_computation.5 | loop fusion | bytes 1048576 | tf_op jit(solution)/shard_map/slice | solution.py:398
  1.1 0.0 copy-start.3
  1.1 0.0 copy-start
  1.2 1.3 %collective-permute-start.11 = (f32[1,15,32,128]{3,2,1,0:T(8,128)S(1)}, f32[1,15,32,128]{3,2,1,0:T(8,128)S(1)}, u32[]{:S(2)}, u32[]{:S(2)}) collective-permute-start(f32[1,15,32,128]{3,2,1,0:T(8,128)S(1)} %get-tuple-element.68.refs_3_), channel_id=1, source_target_pairs={{0,8},{8,0},{16,24},{24,16},{1,9},{9,1},{17,25},{25,17},{2,10},{10... | collective-permute-start | bytes 737288 | tf_op jit(solution)/shard_map/ppermute | solution.py:216
  2.5 0.1 pad_add_fusion.refs_0_.parity.place
  2.6 0.0 copy-done.2
  2.6 0.0 copy-done.4
  2.6 0.6 mask_profiles.1
  3.2 1.0 %collective-permute-start.2 = (f32[3,4,32,128]{3,2,1,0:T(8,128)S(1)}, f32[3,4,32,128]{3,2,1,0:T(8,128)S(1)}, u32[]{:S(2)}, u32[]{:S(2)}) collective-permute-start(f32[3,4,32,128]{3,2,1,0:T(8,128)S(1)} %get-tuple-element.36), channel_id=1, source_target_pairs={{0,1},{1,0},{2,3},{3,2},{4,5},{5,4},{6,7},{7,6},{8,9},{9,8},{10,11... | collective-permute-start | bytes 589832 | tf_op jit(solution)/shard_map/ppermute | solution.py:386
  4.2 2.1 %collective-permute-start.12 = (f32[1,15,32,128]{3,2,1,0:T(8,128)S(1)}, f32[1,15,32,128]{3,2,1,0:T(8,128)S(1)}, u32[]{:S(2)}, u32[]{:S(2)}) collective-permute-start(f32[1,15,32,128]{3,2,1,0:T(8,128)S(1)} %get-tuple-element.67), channel_id=1, source_target_pairs={{8,16},{16,8},{9,17},{17,9},{10,18},{18,10},{11,19},{19,11},{12,20... | collective-permute-start | bytes 737288 | tf_op jit(solution)/shard_map/ppermute | solution.py:216
  6.4 0.0 copy-start.1
  6.4 0.1 collective-permute-start
  6.5 4.2 %collective-permute-start.1 = (f32[1,15,32,128]{3,2,1,0:T(8,128)S(1)}, f32[1,15,32,128]{3,2,1,0:T(8,128)S(1)}, u32[]{:S(2)}, u32[]{:S(2)}) collective-permute-start(f32[1,15,32,128]{3,2,1,0:T(8,128)S(1)} %get-tuple-element.69), channel_id=1, source_target_pairs={{8,16},{16,8},{9,17},{17,9},{10,18},{18,10},{11,19},{19,11},{12,20... | collective-permute-start | bytes 737288 | tf_op jit(solution)/shard_map/ppermute | solution.py:216
  10.7 0.0 collective-permute-done.2.refs_2_
  10.7 0.6 halve_profiles2.1
  11.3 0.2 collective-permute-start.3
  11.5 0.0 copy-done.3
  11.5 2.3 %matrices.1 = (bf16[48,144]{1,0:T(8,128)(2,1)S(1)}, bf16[48,144]{1,0:T(8,128)(2,1)S(1)}, bf16[3,32,192]{2,1,0:T(8,128)(2,1)S(1)}, bf16[3,64,96]{2,1,0:T(8,128)(2...) custom-call(f32[3,3,31]{2,1,0:T(4,128)S(1)} %copy-done.3, ...), custom_call_target="tpu_custom_call" | custom-call | tf_op jit(solution)/shard_map/matrices/pallas_call | solution.py:94
  13.8 1.3 %collective-permute-done.3.refs_2_ = f32[3,2,32,128]{3,2,1,0:T(8,128)S(1)} collective-permute-done((f32[3,2,32,128]{3,2,1,0:T(8,128)S(1)}, f32[3,2,32,128]{3,2,1,0:T(8,128)S(1)}, u32[]{:S(2)}, u32[]{:S(2)}) %collective-permute-start.3) | collective-permute-done | bytes 98336 | tf_op jit(solution)/shard_map/ppermute | solution.py:386
  15.1 0.6 halve_profiles4.1
  15.7 2.4 %collective-permute-start.4 = (f32[3,1,32,128]{3,2,0,1:T(8,128)S(1)}, f32[3,1,32,128]{3,2,0,1:T(8,128)S(1)}, u32[]{:S(2)}, u32[]{:S(2)}) collective-permute-start(f32[3,1,32,128]{3,2,0,1:T(8,128)S(1)} %bitcast.11), channel_id=1, source_target_pairs={{0,4},{1,5},{2,6},{3,7},{4,0},{5,1},{6,2},{7,3},{8,12},{9,13},{10,... | collective-permute-start | bytes 147464 | tf_op jit(solution)/shard_map/ppermute | solution.py:386
  18.0 0.0 collective-permute-done.11.refs_2_.xa
  18.1 0.0 collective-permute-done.12.refs_3_.xb
  18.1 0.0 copy-done
  18.1 0.6 pack_rows0.1
  18.7 1.8 %collective-permute-start.13 = (f32[1,46,16,128]{3,2,1,0:T(8,128)S(1)}, f32[1,46,16,128]{3,2,1,0:T(8,128)S(1)}, u32[]{:S(2)}, u32[]{:S(2)}) collective-permute-start(f32[1,46,16,128]{3,2,1,0:T(8,128)S(1)} %get-tuple-element.56), channel_id=1, source_target_pairs={{0,1},{1,0},{2,3},{3,2},{4,5},{5,4},{6,7},{7,6},{8,9},{9,8},{10,11... | collective-permute-start | bytes 1130504 | tf_op jit(solution)/shard_map/ppermute | solution.py:216
  20.5 1.9 %collective-permute-start.14 = (f32[1,46,16,128]{3,2,1,0:T(8,128)S(1)}, f32[1,46,16,128]{3,2,1,0:T(8,128)S(1)}, u32[]{:S(2)}, u32[]{:S(2)}) collective-permute-start(f32[1,46,16,128]{3,2,1,0:T(8,128)S(1)} %get-tuple-element.57), channel_id=1, source_target_pairs={{1,2},{2,1},{3,4},{4,3},{5,6},{6,5},{9,10},{10,9},{11,12},{12,11},... | collective-permute-start | bytes 1130504 | tf_op jit(solution)/shard_map/ppermute | solution.py:216
  22.4 0.0 collective-permute-done.refs_2_.xa
  22.4 2.7 %collective-permute-done.1.refs_3_.xb = f32[1,15,32,128]{3,2,1,0:T(8,128)S(1)} collective-permute-done((f32[1,15,32,128]{3,2,1,0:T(8,128)S(1)}, f32[1,15,32,128]{3,2,1,0:T(8,128)S(1)}, u32[]{:S(2)}, u32[]{:S(2)}) %collective-permute-start.1) | collective-permute-done | bytes 245792 | tf_op jit(solution)/shard_map/ppermute | solution.py:216
  25.1 0.0 collective-permute-done.4
  25.1 0.6 pack_rows1.1
  25.7 0.9 %collective-permute-start.5 = (f32[1,46,16,128]{3,2,1,0:T(8,128)S(1)}, f32[1,46,16,128]{3,2,1,0:T(8,128)S(1)}, u32[]{:S(2)}, u32[]{:S(2)}) collective-permute-start(f32[1,46,16,128]{3,2,1,0:T(8,128)S(1)} %get-tuple-element.41), channel_id=1, source_target_pairs={{0,1},{1,0},{2,3},{3,2},{4,5},{5,4},{6,7},{7,6},{8,9},{9,8},{10,11... | collective-permute-start | bytes 1130504 | tf_op jit(solution)/shard_map/ppermute | solution.py:216
  26.6 3.1 %collective-permute-start.6 = (f32[1,46,16,128]{3,2,1,0:T(8,128)S(1)}, f32[1,46,16,128]{3,2,1,0:T(8,128)S(1)}, u32[]{:S(2)}, u32[]{:S(2)}) collective-permute-start(f32[1,46,16,128]{3,2,1,0:T(8,128)S(1)} %get-tuple-element.42), channel_id=1, source_target_pairs={{1,2},{2,1},{3,4},{4,3},{5,6},{6,5},{9,10},{10,9},{11,12},{12,11},... | collective-permute-start | bytes 1130504 | tf_op jit(solution)/shard_map/ppermute | solution.py:216
  29.7 0.0 collective-permute-done.13.yc
  29.7 0.0 collective-permute-done.14.yd
  29.7 0.0 copy-done.1
  29.7 2.3 %brick0.1 = (f32[1,16,32,128]{3,2,1,0:T(8,128)S(1)}, f32[1,15,32,128]{3,2,1,0:T(8,128)S(1)}, f32[1,15,32,128]{3,2,1,0:T(8,128)S(1)}, f32[1,46,16,128]{3,2,1,0:T(8,128)S(1)}, f32[1,46,16,128]{3,2,1,0:T(8,128)S(1)}) custom-call(f32[2,16,32,128]{3,2,1,0:T(8,128)S(1)} %copy-done, f32[1,15,32,128]{3,2,1,0:T(8,128)S(1)} %collective-permute-done.11.refs_2_.xa, ...), custom_call_target="tpu_custom_call" | custom-call | tf_op jit(solution)/shard_map/brick0/pallas_call | solution.py:192
  32.0 0.1 collective-permute-start.15
  32.1 3.6 %collective-permute-start.16 = (f32[1,46,16,128]{3,2,1,0:T(8,128)S(1)}, f32[1,46,16,128]{3,2,1,0:T(8,128)S(1)}, u32[]{:S(2)}, u32[]{:S(2)}) collective-permute-start(f32[1,46,16,128]{3,2,1,0:T(8,128)S(1)} %get-tuple-element.60), channel_id=1, source_target_pairs={{1,2},{2,1},{3,4},{4,3},{5,6},{6,5},{9,10},{10,9},{11,12},{12,11},... | collective-permute-start | bytes 1130504 | tf_op jit(solution)/shard_map/ppermute | solution.py:216
  35.7 0.0 collective-permute-done.5.yc
  35.7 0.0 collective-permute-done.6.yd
  35.7 2.3 %brick1.1 = (f32[1,16,32,128]{3,2,1,0:T(8,128)S(1)}, f32[1,15,32,128]{3,2,1,0:T(8,128)S(1)}, f32[1,15,32,128]{3,2,1,0:T(8,128)S(1)}, f32[1,46,16,128]{3,2,1,0:T(8,128)S(1)}, f32[1,46,16,128]{3,2,1,0:T(8,128)S(1)}) custom-call(f32[2,16,32,128]{3,2,1,0:T(8,128)S(1)} %copy-done, f32[1,15,32,128]{3,2,1,0:T(8,128)S(1)} %collective-permute-done.refs_2_.xa, ...), custom_call_target="tpu_custom_call" | custom-call | tf_op jit(solution)/shard_map/brick1/pallas_call | solution.py:192
  38.0 0.1 collective-permute-start.7
  38.1 3.3 %collective-permute-start.8 = (f32[1,46,16,128]{3,2,1,0:T(8,128)S(1)}, f32[1,46,16,128]{3,2,1,0:T(8,128)S(1)}, u32[]{:S(2)}, u32[]{:S(2)}) collective-permute-start(f32[1,46,16,128]{3,2,1,0:T(8,128)S(1)} %get-tuple-element.51), channel_id=1, source_target_pairs={{1,2},{2,1},{3,4},{4,3},{5,6},{6,5},{9,10},{10,9},{11,12},{12,11},... | collective-permute-start | bytes 1130504 | tf_op jit(solution)/shard_map/ppermute | solution.py:216
  41.5 0.0 collective-permute-done.15.refs_3_.rc
  41.5 0.0 collective-permute-done.16.refs_4_.rd
  41.5 0.6 add_rows0.1
  42.1 0.1 collective-permute-start.17
  42.2 3.6 %collective-permute-start.18 = (f32[1,15,32,128]{3,2,1,0:T(8,128)S(1)}, f32[1,15,32,128]{3,2,1,0:T(8,128)S(1)}, u32[]{:S(2)}, u32[]{:S(2)}) collective-permute-start(f32[1,15,32,128]{3,2,1,0:T(8,128)S(1)} %get-tuple-element.64), channel_id=1, source_target_pairs={{8,16},{16,8},{9,17},{17,9},{10,18},{18,10},{11,19},{19,11},{12,20... | collective-permute-start | bytes 737288 | tf_op jit(solution)/shard_map/ppermute | solution.py:216
  45.7 0.0 collective-permute-done.7.refs_3_.rc
  45.7 1.6 %collective-permute-done.8.refs_4_.rd = f32[1,46,16,128]{3,2,1,0:T(8,128)S(1)} collective-permute-done((f32[1,46,16,128]{3,2,1,0:T(8,128)S(1)}, f32[1,46,16,128]{3,2,1,0:T(8,128)S(1)}, u32[]{:S(2)}, u32[]{:S(2)}) %collective-permute-start.8) | collective-permute-done | bytes 376864 | tf_op jit(solution)/shard_map/ppermute | solution.py:216
  47.3 0.6 add_rows1.1
  47.9 0.1 collective-permute-start.10
  48.0 3.6 %collective-permute-start.9 = (f32[1,15,32,128]{3,2,1,0:T(8,128)S(1)}, f32[1,15,32,128]{3,2,1,0:T(8,128)S(1)}, u32[]{:S(2)}, u32[]{:S(2)}) collective-permute-start(f32[1,15,32,128]{3,2,1,0:T(8,128)S(1)} %get-tuple-element.54), channel_id=1, source_target_pairs={{8,16},{16,8},{9,17},{17,9},{10,18},{18,10},{11,19},{19,11},{12,20... | collective-permute-start | bytes 737288 | tf_op jit(solution)/shard_map/ppermute | solution.py:216
  51.6 0.0 collective-permute-done.17.qa
  51.6 3.8 %collective-permute-done.18.qb = f32[1,15,32,128]{3,2,1,0:T(8,128)S(1)} collective-permute-done((f32[1,15,32,128]{3,2,1,0:T(8,128)S(1)}, f32[1,15,32,128]{3,2,1,0:T(8,128)S(1)}, u32[]{:S(2)}, u32[]{:S(2)}) %collective-permute-start.18) | collective-permute-done | bytes 245792 | tf_op jit(solution)/shard_map/ppermute | solution.py:216
  55.4 1.3 %finish0.1.rest_0_ = f32[2,16,32,128]{3,2,1,0:T(8,128)} custom-call(s32[2]{0:T(128)S(1)} %pad_add_fusion.refs_0_.parity.place, f32[2,16,32,128]{3,2,1,0:T(8,128)S(1)} %copy-done, f32[1,16,32,128]{3,2,1,0:T(8,128)S(1)} %get-tuple-element.58.s_own, f32[1,46,16,128]{3,2,1,0:T(8,128)S(1)} %collective-permute-done.15.refs_3_.rc, ...), custom_call_target="tpu_custom_call" | custom-call | tf_op jit(solution)/shard_map/finish0/pallas_call | solution.py:370
  56.7 1.6 %collective-permute-done.10.qb = f32[1,15,32,128]{3,2,1,0:T(8,128)S(1)} collective-permute-done((f32[1,15,32,128]{3,2,1,0:T(8,128)S(1)}, f32[1,15,32,128]{3,2,1,0:T(8,128)S(1)}, u32[]{:S(2)}, u32[]{:S(2)}) %collective-permute-start.10) | collective-permute-done | bytes 245792 | tf_op jit(solution)/shard_map/ppermute | solution.py:216
  58.3 7.6 %collective-permute-done.9.qa = f32[1,15,32,128]{3,2,1,0:T(8,128)S(1)} collective-permute-done((f32[1,15,32,128]{3,2,1,0:T(8,128)S(1)}, f32[1,15,32,128]{3,2,1,0:T(8,128)S(1)}, u32[]{:S(2)}, u32[]{:S(2)}) %collective-permute-start.9) | collective-permute-done | bytes 245792 | tf_op jit(solution)/shard_map/ppermute | solution.py:216
  65.9 1.3 %finish1.1 = f32[2,16,32,128]{3,2,1,0:T(8,128)} custom-call(s32[2]{0:T(128)S(1)} %pad_add_fusion.refs_0_.parity.place, f32[2,16,32,128]{3,2,1,0:T(8,128)S(1)} %copy-done, f32[1,16,32,128]{3,2,1,0:T(8,128)S(1)} %get-tuple-element.49.s_own, f32[1,46,16,128]{3,2,1,0:T(8,128)S(1)} %collective-permute-done.7.refs_3_.rc, ...), custom_call_target="tpu_custom_call", output_to_operand_aliasing={{}: (7, {})} | custom-call | tf_op jit(solution)/shard_map/finish1/pallas_call | solution.py:370
  (2 shorter events, 0.1 us)
Async XLA Ops:
  0.0 2.6 %copy-start.2 = (f32[1,1,3,256,128]{4,3,2,1,0:T(8,128)S(1)}, f32[1,1,3,256,128]{4,3,2,1,0:T(8,128)}, u32[]{:S(2)}) copy-start(f32[1,1,3,256,128]{4,3,2,1,0:T(8,128)} %refs_2_.1) | copy-start | bytes 1179652
  0.0 2.6 %copy-start.4 = (s32[3,4]{1,0:T(4,128)S(1)}, s32[3,4]{1,0:T(4,128)}, u32[]{:S(2)}) copy-start(s32[3,4]{1,0:T(4,128)} %refs_1_.3) | copy-start | bytes 148
  1.1 10.4 %copy-start.3 = (f32[3,3,31]{2,1,0:T(4,128)S(1)}, f32[3,3,31]{2,1,0:T(4,128)}, u32[]{:S(2)}) copy-start(f32[3,3,31]{2,1,0:T(4,128)} %rest_1_.1) | copy-start | bytes 3352
  1.1 16.9 %copy-start = (f32[2,16,32,128]{3,2,1,0:T(8,128)S(1)}, f32[2,16,32,128]{3,2,1,0:T(8,128)}, u32[]{:S(2)}) copy-start(f32[2,16,32,128]{3,2,1,0:T(8,128)} %estimate.3) | copy-start | bytes 1572868
  1.2 16.8 %collective-permute-start.11 = (f32[1,15,32,128]{3,2,1,0:T(8,128)S(1)}, f32[1,15,32,128]{3,2,1,0:T(8,128)S(1)}, u32[]{:S(2)}, u32[]{:S(2)}) collective-permute-start(f32[1,15,32,128]{3,2,1,0:T(8,128)S(1)} %get-tuple-element.68.refs_3_), channel_id=1, source_target_pairs={{0,8},{8,0},{16,24},{24,16},{1,9},{9,1},{17,25},{25,17},{2,10},{10... | collective-permute-start | bytes 737288 | tf_op jit(solution)/shard_map/ppermute | solution.py:216
  3.2 7.5 %collective-permute-start.2 = (f32[3,4,32,128]{3,2,1,0:T(8,128)S(1)}, f32[3,4,32,128]{3,2,1,0:T(8,128)S(1)}, u32[]{:S(2)}, u32[]{:S(2)}) collective-permute-start(f32[3,4,32,128]{3,2,1,0:T(8,128)S(1)} %get-tuple-element.36), channel_id=1, source_target_pairs={{0,1},{1,0},{2,3},{3,2},{4,5},{5,4},{6,7},{7,6},{8,9},{9,8},{10,11... | collective-permute-start | bytes 589832 | tf_op jit(solution)/shard_map/ppermute | solution.py:386
  4.2 13.8 %collective-permute-start.12 = (f32[1,15,32,128]{3,2,1,0:T(8,128)S(1)}, f32[1,15,32,128]{3,2,1,0:T(8,128)S(1)}, u32[]{:S(2)}, u32[]{:S(2)}) collective-permute-start(f32[1,15,32,128]{3,2,1,0:T(8,128)S(1)} %get-tuple-element.67), channel_id=1, source_target_pairs={{8,16},{16,8},{9,17},{17,9},{10,18},{18,10},{11,19},{19,11},{12,20... | collective-permute-start | bytes 737288 | tf_op jit(solution)/shard_map/ppermute | solution.py:216
  6.4 23.3 %copy-start.1 = (f32[3,2,16,32,128]{4,3,2,1,0:T(8,128)S(1)}, f32[3,2,16,32,128]{4,3,2,1,0:T(8,128)}, u32[]{:S(2)}) copy-start(f32[3,2,16,32,128]{4,3,2,1,0:T(8,128)} %views.3) | copy-start | bytes 4718596
  6.4 16.0 %collective-permute-start = (f32[1,15,32,128]{3,2,1,0:T(8,128)S(1)}, f32[1,15,32,128]{3,2,1,0:T(8,128)S(1)}, u32[]{:S(2)}, u32[]{:S(2)}) collective-permute-start(f32[1,15,32,128]{3,2,1,0:T(8,128)S(1)} %get-tuple-element.70), channel_id=1, source_target_pairs={{0,8},{8,0},{16,24},{24,16},{1,9},{9,1},{17,25},{25,17},{2,10},{10... | collective-permute-start | bytes 737288 | tf_op jit(solution)/shard_map/ppermute | solution.py:216
  6.5 18.6 %collective-permute-start.1 = (f32[1,15,32,128]{3,2,1,0:T(8,128)S(1)}, f32[1,15,32,128]{3,2,1,0:T(8,128)S(1)}, u32[]{:S(2)}, u32[]{:S(2)}) collective-permute-start(f32[1,15,32,128]{3,2,1,0:T(8,128)S(1)} %get-tuple-element.69), channel_id=1, source_target_pairs={{8,16},{16,8},{9,17},{17,9},{10,18},{18,10},{11,19},{19,11},{12,20... | collective-permute-start | bytes 737288 | tf_op jit(solution)/shard_map/ppermute | solution.py:216
  11.3 3.8 %collective-permute-start.3 = (f32[3,2,32,128]{3,2,1,0:T(8,128)S(1)}, f32[3,2,32,128]{3,2,1,0:T(8,128)S(1)}, u32[]{:S(2)}, u32[]{:S(2)}) collective-permute-start(f32[3,2,32,128]{3,2,1,0:T(8,128)S(1)} %get-tuple-element.38._), channel_id=1, source_target_pairs={{0,2},{1,3},{2,0},{3,1},{4,6},{5,7},{6,4},{7,5},{8,10},{9,11},{10,... | collective-permute-start | bytes 294920 | tf_op jit(solution)/shard_map/ppermute | solution.py:386
  15.7 9.4 %collective-permute-start.4 = (f32[3,1,32,128]{3,2,0,1:T(8,128)S(1)}, f32[3,1,32,128]{3,2,0,1:T(8,128)S(1)}, u32[]{:S(2)}, u32[]{:S(2)}) collective-permute-start(f32[3,1,32,128]{3,2,0,1:T(8,128)S(1)} %bitcast.11), channel_id=1, source_target_pairs={{0,4},{1,5},{2,6},{3,7},{4,0},{5,1},{6,2},{7,3},{8,12},{9,13},{10,... | collective-permute-start | bytes 147464 | tf_op jit(solution)/shard_map/ppermute | solution.py:386
  18.7 11.0 %collective-permute-start.13 = (f32[1,46,16,128]{3,2,1,0:T(8,128)S(1)}, f32[1,46,16,128]{3,2,1,0:T(8,128)S(1)}, u32[]{:S(2)}, u32[]{:S(2)}) collective-permute-start(f32[1,46,16,128]{3,2,1,0:T(8,128)S(1)} %get-tuple-element.56), channel_id=1, source_target_pairs={{0,1},{1,0},{2,3},{3,2},{4,5},{5,4},{6,7},{7,6},{8,9},{9,8},{10,11... | collective-permute-start | bytes 1130504 | tf_op jit(solution)/shard_map/ppermute | solution.py:216
  20.5 9.2 %collective-permute-start.14 = (f32[1,46,16,128]{3,2,1,0:T(8,128)S(1)}, f32[1,46,16,128]{3,2,1,0:T(8,128)S(1)}, u32[]{:S(2)}, u32[]{:S(2)}) collective-permute-start(f32[1,46,16,128]{3,2,1,0:T(8,128)S(1)} %get-tuple-element.57), channel_id=1, source_target_pairs={{1,2},{2,1},{3,4},{4,3},{5,6},{6,5},{9,10},{10,9},{11,12},{12,11},... | collective-permute-start | bytes 1130504 | tf_op jit(solution)/shard_map/ppermute | solution.py:216
  25.7 10.0 %collective-permute-start.5 = (f32[1,46,16,128]{3,2,1,0:T(8,128)S(1)}, f32[1,46,16,128]{3,2,1,0:T(8,128)S(1)}, u32[]{:S(2)}, u32[]{:S(2)}) collective-permute-start(f32[1,46,16,128]{3,2,1,0:T(8,128)S(1)} %get-tuple-element.41), channel_id=1, source_target_pairs={{0,1},{1,0},{2,3},{3,2},{4,5},{5,4},{6,7},{7,6},{8,9},{9,8},{10,11... | collective-permute-start | bytes 1130504 | tf_op jit(solution)/shard_map/ppermute | solution.py:216
  26.6 9.1 %collective-permute-start.6 = (f32[1,46,16,128]{3,2,1,0:T(8,128)S(1)}, f32[1,46,16,128]{3,2,1,0:T(8,128)S(1)}, u32[]{:S(2)}, u32[]{:S(2)}) collective-permute-start(f32[1,46,16,128]{3,2,1,0:T(8,128)S(1)} %get-tuple-element.42), channel_id=1, source_target_pairs={{1,2},{2,1},{3,4},{4,3},{5,6},{6,5},{9,10},{10,9},{11,12},{12,11},... | collective-permute-start | bytes 1130504 | tf_op jit(solution)/shard_map/ppermute | solution.py:216
  32.0 9.4 %collective-permute-start.15 = (f32[1,46,16,128]{3,2,1,0:T(8,128)S(1)}, f32[1,46,16,128]{3,2,1,0:T(8,128)S(1)}, u32[]{:S(2)}, u32[]{:S(2)}) collective-permute-start(f32[1,46,16,128]{3,2,1,0:T(8,128)S(1)} %get-tuple-element.59), channel_id=1, source_target_pairs={{0,1},{1,0},{2,3},{3,2},{4,5},{5,4},{6,7},{7,6},{8,9},{9,8},{10,11... | collective-permute-start | bytes 1130504 | tf_op jit(solution)/shard_map/ppermute | solution.py:216
  32.1 9.4 %collective-permute-start.16 = (f32[1,46,16,128]{3,2,1,0:T(8,128)S(1)}, f32[1,46,16,128]{3,2,1,0:T(8,128)S(1)}, u32[]{:S(2)}, u32[]{:S(2)}) collective-permute-start(f32[1,46,16,128]{3,2,1,0:T(8,128)S(1)} %get-tuple-element.60), channel_id=1, source_target_pairs={{1,2},{2,1},{3,4},{4,3},{5,6},{6,5},{9,10},{10,9},{11,12},{12,11},... | collective-permute-start | bytes 1130504 | tf_op jit(solution)/shard_map/ppermute | solution.py:216
  38.0 7.7 %collective-permute-start.7 = (f32[1,46,16,128]{3,2,1,0:T(8,128)S(1)}, f32[1,46,16,128]{3,2,1,0:T(8,128)S(1)}, u32[]{:S(2)}, u32[]{:S(2)}) collective-permute-start(f32[1,46,16,128]{3,2,1,0:T(8,128)S(1)} %get-tuple-element.50), channel_id=1, source_target_pairs={{0,1},{1,0},{2,3},{3,2},{4,5},{5,4},{6,7},{7,6},{8,9},{9,8},{10,11... | collective-permute-start | bytes 1130504 | tf_op jit(solution)/shard_map/ppermute | solution.py:216
  38.1 9.2 %collective-permute-start.8 = (f32[1,46,16,128]{3,2,1,0:T(8,128)S(1)}, f32[1,46,16,128]{3,2,1,0:T(8,128)S(1)}, u32[]{:S(2)}, u32[]{:S(2)}) collective-permute-start(f32[1,46,16,128]{3,2,1,0:T(8,128)S(1)} %get-tuple-element.51), channel_id=1, source_target_pairs={{1,2},{2,1},{3,4},{4,3},{5,6},{6,5},{9,10},{10,9},{11,12},{12,11},... | collective-permute-start | bytes 1130504 | tf_op jit(solution)/shard_map/ppermute | solution.py:216
  42.1 9.5 %collective-permute-start.17 = (f32[1,15,32,128]{3,2,1,0:T(8,128)S(1)}, f32[1,15,32,128]{3,2,1,0:T(8,128)S(1)}, u32[]{:S(2)}, u32[]{:S(2)}) collective-permute-start(f32[1,15,32,128]{3,2,1,0:T(8,128)S(1)} %get-tuple-element.63), channel_id=1, source_target_pairs={{0,8},{8,0},{16,24},{24,16},{1,9},{9,1},{17,25},{25,17},{2,10},{10... | collective-permute-start | bytes 737288 | tf_op jit(solution)/shard_map/ppermute | solution.py:216
  42.2 13.2 %collective-permute-start.18 = (f32[1,15,32,128]{3,2,1,0:T(8,128)S(1)}, f32[1,15,32,128]{3,2,1,0:T(8,128)S(1)}, u32[]{:S(2)}, u32[]{:S(2)}) collective-permute-start(f32[1,15,32,128]{3,2,1,0:T(8,128)S(1)} %get-tuple-element.64), channel_id=1, source_target_pairs={{8,16},{16,8},{9,17},{17,9},{10,18},{18,10},{11,19},{19,11},{12,20... | collective-permute-start | bytes 737288 | tf_op jit(solution)/shard_map/ppermute | solution.py:216
  47.9 10.3 %collective-permute-start.10 = (f32[1,15,32,128]{3,2,1,0:T(8,128)S(1)}, f32[1,15,32,128]{3,2,1,0:T(8,128)S(1)}, u32[]{:S(2)}, u32[]{:S(2)}) collective-permute-start(f32[1,15,32,128]{3,2,1,0:T(8,128)S(1)} %get-tuple-element.55), channel_id=1, source_target_pairs={{0,8},{8,0},{16,24},{24,16},{1,9},{9,1},{17,25},{25,17},{2,10},{10... | collective-permute-start | bytes 737288 | tf_op jit(solution)/shard_map/ppermute | solution.py:216
  48.0 17.9 %collective-permute-start.9 = (f32[1,15,32,128]{3,2,1,0:T(8,128)S(1)}, f32[1,15,32,128]{3,2,1,0:T(8,128)S(1)}, u32[]{:S(2)}, u32[]{:S(2)}) collective-permute-start(f32[1,15,32,128]{3,2,1,0:T(8,128)S(1)} %get-tuple-element.54), channel_id=1, source_target_pairs={{8,16},{16,8},{9,17},{17,9},{10,18},{18,10},{11,19},{19,11},{12,20... | collective-permute-start | bytes 737288 | tf_op jit(solution)/shard_map/ppermute | solution.py:216
